TPU v7x, 32 devices: a whole 2x2x4 slice. The times are simulated.
32 devices in a mesh: vox: 4 (over y, core), fas: 8 (over z, x).
Axes of the slice: x: 2, y: 2, z: 4, core: 2. Of those that a mesh axis runs over, the one named last changes fastest.
Arguments:
- signal: float32 [64, 6144], P('vox', 'fas'), may hold values from -6 to 6
- initial_weights: float32 [262144], P('fas'), may hold values from 0.1 to 2
- coefficients: bfloat16 [8192, 4096], P(('vox', 'fas')), may hold values from 0 to 0.032958984
- block_rows: int32 [8192], P(('vox', 'fas')), may hold values from 0 to 63, as said below
- block_cols: int32 [8192], P(('vox', 'fas')), may hold values from 0 to 4095, as said below
- block_atoms: int32 [8192, 64], P(('vox', 'fas')), may hold values from 0 to 359
- block_count: int32 [32], P(('vox', 'fas')), may hold values from 64 to 256, as said below
- dictionary: bfloat16 [360, 96], replicated, may hold values from -6 to 6
Outputs:
- weights: float32 [262144], P('fas')
- residual: float32 [64, 6144], P('vox', 'fas')
Inputs may be any that keep to these rules, and one draw needn't show every extreme that they name: Block slots are stored device by device: the device with vox index i and fas index f holds slots (i * 8 + f) * 256 to (i * 8 + f + 1) * 256 - 1, and every block_rows value there lies in i * 16 to (i + 1) * 16 - 1. For the slots of the device with fas index f, every block_cols value lies in f * 512 to (f + 1) * 512 - 1. `block_count`: entry i * 8 + f is the number of live slots of the device with vox index i and fas index f, its first slots; some device has all 256 live.
All inputs are finite; a program needn't handle non-finite values.
Results may differ from a plain program's by a relative error of at most 0.0003.
Values sent between devices are 32-bit elements; how exact they have to be, the bound alone decides.
No kernel may reach another device: no remote copies, remote signals or barrier semaphores. Data moves between devices by JAX's collectives and lax.ppermute only.
A program may use at most 128 MiB of HBM per device.

v0:
```python
import functools

import jax
import jax.numpy as jnp
from jax import lax
from jax.experimental import pallas as pl
from jax.experimental.pallas import tpu as pltpu
from jax.sharding import PartitionSpec as P

BV = 64
BF = 64
DIRS = 96
ITERS = 5
LANES = 128
GROUP = 4
BUILD = 19
UNROLL = 38
PACK = BV * DIRS // LANES
HALF = BV // 2
QUART = BV // 4
VMEM_LIMIT = 16 * 1024 * 1024


def group_cap(slots, rows):
    groups = (slots + (GROUP - 1) * rows) // GROUP
    return -(-groups // UNROLL) * UNROLL


def plan_spots(cap):
    places = -(-cap * GROUP // LANES) * LANES
    return places, 2 * places, 2 * places + -(-cap // LANES) * LANES


def lane_ids(rows):
    return lax.broadcasted_iota(jnp.int32, (rows, LANES), 1)


def plan_slots(vox_rows, fas_rows, cap, row_ref, side_ref, count_ref, plan_ref):
    f32, i32 = jnp.float32, jnp.int32
    slots = row_ref.shape[1]
    places = cap * GROUP
    count = count_ref[...]
    down = lax.broadcasted_iota(i32, (slots, 1), 0)
    along = lax.broadcasted_iota(i32, (1, slots), 1)
    rows_down = jnp.where(down < count, lax.rem(side_ref[:, 0:1], vox_rows), vox_rows)
    cols_down = lax.rem(side_ref[:, 1:2], fas_rows)
    rows_along = jnp.where(along < count, lax.rem(row_ref[...], vox_rows), vox_rows)
    lane = lane_ids(1)
    member = (rows_down == lane) & (lane < vox_rows)
    counts = jnp.sum(member.astype(i32), axis=0, keepdims=True)
    groups = (counts + GROUP - 1) // GROUP
    earlier = lax.broadcasted_iota(i32, (LANES, LANES), 0) < lane_ids(LANES)
    start = jnp.dot(
        jnp.broadcast_to(groups, (8, LANES)).astype(f32).astype(jnp.bfloat16),
        earlier.astype(f32).astype(jnp.bfloat16),
        preferred_element_type=f32,
    )[0:1].astype(i32)
    rank = jnp.sum(
        ((rows_along == rows_down) & (along < down)).astype(i32), axis=1, keepdims=True
    )
    first = jnp.sum(jnp.where(member, start, 0), axis=1, keepdims=True)
    place = jnp.where(rows_down < vox_rows, first * GROUP + rank, -1)
    spots = lax.broadcasted_iota(i32, (1, places), 1)
    chosen = place == spots
    slot_at, row_at, turns_at = plan_spots(cap)
    plan_ref[:, 0:places] = jnp.sum(jnp.where(chosen, cols_down, 0), axis=0, keepdims=True)
    slot = jnp.sum(jnp.where(chosen, down + 1, 0), axis=0, keepdims=True) - 1
    plan_ref[:, slot_at : slot_at + places] = slot
    heads = lax.broadcasted_iota(i32, (1, cap), 1) * GROUP
    row = jnp.sum(jnp.where(place == heads, rows_down, 0), axis=0, keepdims=True)
    plan_ref[:, row_at : row_at + cap] = row
    total = jnp.sum(groups, axis=1, keepdims=True)
    turns = (total + UNROLL - 1) // UNROLL
    plan_ref[:, turns_at:] = jnp.broadcast_to(turns, (1, LANES))


def setup_kernel(
    vox_rows,
    fas_rows,
    cap,
    row_ref,
    side_ref,
    count_ref,
    coef_ref,
    atom_ref,
    dict_ref,
    cp_ref,
    at_ref,
    a_ref,
    meta_ref,
    plan_ref,
    sem,
):
    plan_slots(vox_rows, fas_rows, cap, row_ref, side_ref, count_ref, plan_ref)
    plan = pltpu.make_async_copy(plan_ref, meta_ref, sem)
    plan.start()
    plan.wait()
    slot_at, _, turns_at = plan_spots(cap)
    atoms_pad = dict_ref.shape[1]
    left32 = lane_ids(HALF) < BF
    left1 = lane_ids(1) < BF
    atom_ids = lax.broadcasted_iota(jnp.int16, (atoms_pad, LANES), 0)

    def build(q):
        tops, bottoms, marks = [], [], []
        for pair in range(GROUP // 2):
            s0 = meta_ref[0, slot_at + q * GROUP + 2 * pair]
            s1 = meta_ref[0, slot_at + q * GROUP + 2 * pair + 1]
            k0 = jnp.maximum(s0, 0)
            k1 = jnp.maximum(s1, 0)
            m0 = (s0 >= 0).astype(jnp.float32)
            m1 = (s1 >= 0).astype(jnp.float32)
            c0 = coef_ref[k0].astype(jnp.float32) * m0
            c1 = coef_ref[k1].astype(jnp.float32) * m1
            tops.append(jnp.where(left32, c0, pltpu.roll(c1, BF, 1)))
            bottoms.append(jnp.where(left32, pltpu.roll(c0, BF, 1), c1))
            ids = jnp.where(left1, atom_ref[pl.ds(k0, 1), :], atom_ref[pl.ds(k1, 1), :])
            ids = jnp.broadcast_to(ids, (atoms_pad, LANES)).astype(jnp.int16)
            marks.append(jnp.where(atom_ids == ids, jnp.bfloat16(1), jnp.bfloat16(0)))
        top = jnp.concatenate(tops, axis=1)
        bottom = jnp.concatenate(bottoms, axis=1)
        cp_ref[q] = jnp.concatenate([top, bottom], axis=0).astype(jnp.bfloat16)
        marked = jnp.concatenate(marks, axis=1)
        table = jnp.dot(dict_ref[...], marked, preferred_element_type=jnp.float32)
        at_ref[q] = table.astype(jnp.bfloat16)
        a_ref[q] = table.T.astype(jnp.bfloat16)

    def turn(t, carry):
        for n in range(BUILD):
            build(t * BUILD + n)
        return carry

    lax.fori_loop(0, meta_ref[0, turns_at] * (UNROLL // BUILD), turn, 0)


def spread_table(values, table_ref):
    rows = values.shape[0]
    left = lane_ids(rows) < BF
    turned = pltpu.roll(values, BF, 1)
    table_ref[pl.ds(0, rows, stride=2), :] = jnp.where(left, values, turned)
    table_ref[pl.ds(1, rows, stride=2), :] = jnp.where(left, turned, values)


def run_forward(cap, meta_ref, cp_ref, a_ref, table_ref, acc_ref):
    left = lane_ids(1) < BF
    _, row_at, turns_at = plan_spots(cap)

    def turn(t, carry):
        outs = []
        for n in range(UNROLL):
            q = t * UNROLL + n
            u = []
            for pair in range(GROUP // 2):
                p = q * GROUP + 2 * pair
                u0 = table_ref[pl.ds(meta_ref[0, p], 1), :]
                u1 = table_ref[pl.ds(meta_ref[0, p + 1], 1), :]
                u.append(jnp.where(left, u0, u1))
            scaled = cp_ref[q].astype(jnp.float32) * jnp.concatenate(u, axis=1)
            high = scaled.astype(jnp.bfloat16)
            low = (scaled - high.astype(jnp.float32)).astype(jnp.bfloat16)
            both = jnp.concatenate([high, low], axis=0)
            out = jnp.dot(both, a_ref[q], preferred_element_type=jnp.float32)
            outs.append(out[:BV] + out[BV:])
        for n in range(UNROLL):
            r = meta_ref[0, row_at + t * UNROLL + n]
            acc_ref[r] = acc_ref[r] + outs[n]
        return carry

    lax.fori_loop(0, meta_ref[0, turns_at], turn, 0)


def packed_row(acc_ref, r):
    lane = lane_ids(QUART)
    last = acc_ref[r, 3 * QUART :, :]
    return [
        jnp.where(
            lane < DIRS,
            acc_ref[r, i * QUART : (i + 1) * QUART, :],
            pltpu.roll(last, DIRS - 32 * i, 1),
        )
        for i in range(3)
    ]


def pack_rows(acc_ref, out_refs):
    parts = len(out_refs)
    rows = acc_ref.shape[0] // parts
    place = lax.rem(lax.axis_index("fas"), parts) if parts > 1 else 0
    for s in range(parts):
        for n in range(rows):
            r = (place ^ s) * rows + n if parts > 1 else n
            for i, piece in enumerate(packed_row(acc_ref, r)):
                out_refs[s][pl.ds(n * PACK + i * QUART, QUART), :] = piece


def first_kernel(cap, meta_ref, w_ref, sig_ref, cp_ref, a_ref, *refs):
    *out_refs, table_ref, acc_ref = refs
    spread_table(w_ref[...], table_ref)
    acc_ref[...] = sig_ref[...]
    run_forward(cap, meta_ref, cp_ref, a_ref, table_ref, acc_ref)
    pack_rows(acc_ref, out_refs)


def image_kernel(cap, meta_ref, g_ref, w_ref, cp_ref, a_ref, out_ref, p_ref, sq_ref, table_ref, acc_ref):
    gradient = g_ref[...]
    projected = jnp.where((w_ref[...] > 0) | (gradient < 0), gradient, 0.0)
    p_ref[...] = projected
    sq_ref[...] = jnp.sum((projected * projected).reshape(-1, 8, LANES), axis=0)
    spread_table(projected, table_ref)
    acc_ref[...] = jnp.zeros_like(acc_ref)
    run_forward(cap, meta_ref, cp_ref, a_ref, table_ref, acc_ref)
    pack_rows(acc_ref, [out_ref])


def update_kernel(
    cap,
    vox_total,
    last,
    meta_ref,
    sums_ref,
    p_ref,
    w_ref,
    sig_ref,
    cp_ref,
    a_ref,
    new_ref,
    *refs,
):
    *out_refs, table_ref, acc_ref = refs
    sums = jnp.sum(sums_ref[...], axis=0)
    left = lane_ids(1) < BF
    image_sq = jnp.sum(jnp.where(left, sums, 0.0), keepdims=True)
    grad_sq = jnp.sum(jnp.where(left, 0.0, sums), keepdims=True) * (1.0 / vox_total)
    step = grad_sq / (image_sq + 1e-6)
    updated = jnp.maximum(w_ref[...] - step * p_ref[...], 0.0)
    new_ref[...] = updated
    spread_table(updated, table_ref)
    acc_ref[...] = sig_ref[...]
    run_forward(cap, meta_ref, cp_ref, a_ref, table_ref, acc_ref)
    if last:
        out_refs[0][...] = acc_ref[...]
    else:
        pack_rows(acc_ref, out_refs)


def backward_kernel(cap, vox_rows, meta_ref, cp_ref, at_ref, *refs):
    *res_refs, out_ref, split_ref, table_ref = refs
    lane = lane_ids(QUART)
    parts = len(res_refs)
    rows = vox_rows // parts
    place = lax.rem(lax.axis_index("fas"), parts) if parts > 1 else 0
    for s, n in [(s, n) for s in range(parts) for n in range(rows)]:
        r = (place ^ s) * rows + n if parts > 1 else n
        packed = [res_refs[s][pl.ds(n * PACK + i * QUART, QUART), :] for i in range(3)]
        turned = [pltpu.roll(packed[i], 32 * (i + 1), 1) for i in range(3)]
        last = jnp.where(lane < 32, turned[0], jnp.where(lane < 64, turned[1], turned[2]))
        whole = jnp.concatenate(packed + [last], axis=0)
        whole = jnp.where(lane_ids(BV) < DIRS, whole, 0.0)
        high = whole.astype(jnp.bfloat16)
        low = (whole - high.astype(jnp.float32)).astype(jnp.bfloat16)
        split_ref[r] = jnp.concatenate([high, low], axis=0)
    table_ref[...] = jnp.zeros_like(table_ref)
    left = lane_ids(1) < BF
    _, row_at, turns_at = plan_spots(cap)

    def turn(t, carry):
        sums = []
        for n in range(UNROLL):
            q = t * UNROLL + n
            r = meta_ref[0, row_at + q]
            part = jnp.dot(split_ref[r], at_ref[q], preferred_element_type=jnp.float32)
            part = (part[:BV] + part[BV:]) * cp_ref[q].astype(jnp.float32)
            sums.append(jnp.sum(part, axis=0, keepdims=True))
        for n in range(UNROLL):
            for pair in range(GROUP // 2):
                p = (t * UNROLL + n) * GROUP + 2 * pair
                row = sums[n][:, pair * LANES : (pair + 1) * LANES]
                c0 = pl.ds(meta_ref[0, p], 1)
                table_ref[c0, :] = table_ref[c0, :] + jnp.where(left, row, 0.0)
                c1 = pl.ds(meta_ref[0, p + 1], 1)
                table_ref[c1, :] = table_ref[c1, :] + jnp.where(left, 0.0, row)
        return carry

    lax.fori_loop(0, meta_ref[0, turns_at], turn, 0)
    rows = out_ref.shape[0]
    even = table_ref[pl.ds(0, rows, stride=2), :]
    odd = table_ref[pl.ds(1, rows, stride=2), :]
    even = even + pltpu.roll(even, BF, 1)
    odd = odd + pltpu.roll(odd, BF, 1)
    out_ref[...] = jnp.where(lane_ids(rows) < BF, even, odd)


def share_kernel(shares_ref, out_ref):
    out_ref[...] = jnp.sum(shares_ref[...], axis=0)


def sum_kernel(*refs):
    *in_refs, out_ref = refs
    total = in_refs[0][...]
    for ref in in_refs[1:]:
        total = total + ref[...]
    out_ref[...] = total


def spread_kernel(mine_ref, other_ref, out_ref):
    total = mine_ref[...] + other_ref[...]
    for i in range(out_ref.shape[0]):
        out_ref[i] = total


def norm_kernel(shares_ref, sq_ref, out_ref):
    image = jnp.sum(shares_ref[...], axis=0)
    image_sq = jnp.sum(image * image, axis=0, keepdims=True)
    proj_sq = jnp.sum(sq_ref[...], axis=0, keepdims=True)
    image_sq = image_sq + pltpu.roll(image_sq, BF, 1)
    proj_sq = proj_sq + pltpu.roll(proj_sq, BF, 1)
    sums = jnp.where(lane_ids(1) < BF, image_sq, proj_sq)
    out_ref[...] = jnp.broadcast_to(sums[None], out_ref.shape)


def call(kernel, outs, ins, scratch=()):
    spaces = {"v": pltpu.VMEM, "s": pltpu.SMEM, "m": pltpu.SMEM, "n": pltpu.VMEM}
    run = pl.pallas_call(
        kernel,
        out_shape=tuple(
            spaces[kind](shape, dtype) for shape, dtype, kind in outs
        ),
        in_specs=[pl.BlockSpec(memory_space=spaces[kind]) for kind in ins],
        out_specs=tuple(pl.BlockSpec(memory_space=spaces[kind]) for _, _, kind in outs),
        scratch_shapes=list(scratch),
        compiler_params=pltpu.CompilerParams(vmem_limit_bytes=VMEM_LIMIT),
    )

    def placed(*args):
        return run(
            *(
                pltpu.with_memory_space_constraint(x, spaces[kind]) if kind in "vm" else x
                for x, kind in zip(args, ins)
            )
        )

    return placed


def local(
    n_vox,
    n_fas,
    signal,
    initial_weights,
    coefficients,
    block_rows,
    block_cols,
    block_atoms,
    block_count,
    dictionary,
):
    f32, bf16, i32 = jnp.float32, jnp.bfloat16, jnp.int32
    vox_rows = signal.shape[0]
    fas_rows = initial_weights.shape[0] // BF
    slots = coefficients.shape[0]
    cap = group_cap(slots, vox_rows)
    atoms = dictionary.shape[0]
    atoms_pad = -(-atoms // LANES) * LANES
    wide = GROUP * BF
    half_rows = fas_rows // 2

    coef_view = coefficients.reshape(slots, HALF, LANES)
    atom_view = jnp.concatenate([block_atoms, block_atoms], axis=1)
    dict_t = jnp.pad(dictionary.T, ((0, LANES - DIRS), (0, atoms_pad - atoms)))
    fas_place = lax.axis_index("fas")
    side = jnp.stack([block_rows, block_cols], axis=1)
    side = jnp.pad(side, ((0, 0), (0, LANES - 2)))
    plan_size = plan_spots(cap)[2] + LANES
    cp, at, a, meta = call(
        functools.partial(setup_kernel, vox_rows, fas_rows, cap),
        [
            ((cap, BV, wide), bf16, "v"),
            ((cap, LANES, wide), bf16, "v"),
            ((cap, wide, LANES), bf16, "v"),
            ((1, plan_size), i32, "m"),
        ],
        "nvnvvv",
        [pltpu.VMEM((1, plan_size), i32), pltpu.SemaphoreType.DMA],
    )(block_rows[None], side, block_count[None], coef_view, atom_view, dict_t)

    own = signal.shape[1] // DIRS // 2
    negative = -signal.reshape(vox_rows, own, 2, DIRS).transpose(0, 2, 1, 3)
    negative = jnp.pad(negative, ((0, 0), (0, 0), (0, 0), (0, LANES - DIRS)))
    sig = lax.dynamic_update_slice(
        jnp.zeros((vox_rows, 2, HALF, LANES), f32), negative, (0, 0, fas_place * own, 0)
    ).reshape(vox_rows, BV, LANES)

    image_rows = vox_rows * PACK
    table = pltpu.VMEM((fas_rows, LANES), f32)
    acc = pltpu.VMEM((vox_rows, BV, LANES), f32)
    image_out = ((image_rows, LANES), f32, "v")
    flat_out = ((half_rows, LANES), f32, "v")

    def swap(x, axis, groups=None):
        return lax.all_to_all(x, axis, 0, 0, axis_index_groups=groups)

    half = n_fas // 2
    halves = [list(range(half)), list(range(half, n_fas))]
    across = [(i, (i + half) % n_fas) for i in range(n_fas)]
    share_rows = image_rows // n_fas
    half_share = image_rows // half

    parts = half if half <= 4 else 1
    share_out = ((half_share, LANES), f32, "v")
    image_outs = [share_out] * parts if parts > 1 else [image_out]

    def to_place(x, s):
        return lax.ppermute(x, "fas", [(i, i ^ s) for i in range(n_fas)])

    def sum_all(partial):
        if parts > 1:
            shares = [partial[0]] + [to_place(partial[s], s) for s in range(1, parts)]
            (mine,) = call(sum_kernel, [share_out], "v" * parts)(*shares)
            other = lax.ppermute(mine, "fas", across)
            (total,) = call(sum_kernel, [share_out], "vv")(mine, other)
            return [total] + [to_place(total, s) for s in range(1, parts)]
        shares = swap(partial[0].reshape(half, half_share, LANES), "fas", halves)
        (mine,) = call(share_kernel, [share_out], "v")(shares)
        other = lax.ppermute(mine, "fas", across)
        (total,) = call(spread_kernel, [((half, half_share, LANES), f32, "v")], "vv")(mine, other)
        return [swap(total, "fas", halves).reshape(image_rows, LANES)]

    weights = initial_weights.reshape(half_rows, LANES)
    partial = call(
        functools.partial(first_kernel, cap), image_outs, "mvvvv", [table, acc]
    )(meta, weights, sig, cp, a)
    for sweep in range(ITERS):
        last = sweep == ITERS - 1
        whole = sum_all(partial)
        (gradient,) = call(
            functools.partial(backward_kernel, cap, vox_rows),
            [flat_out],
            "mvv" + "v" * parts,
            [pltpu.VMEM((vox_rows, 2 * BV, LANES), bf16), table],
        )(meta, cp, at, *whole)
        bit = 1
        while bit < n_vox:
            gradient = gradient + lax.ppermute(
                gradient, "vox", [(i, i ^ bit) for i in range(n_vox)]
            )
            bit *= 2
        image, projected, proj_sq = call(
            functools.partial(image_kernel, cap),
            [image_out, flat_out, ((8, LANES), f32, "v")],
            "mvvvv",
            [table, acc],
        )(meta, gradient, weights, cp, a)
        shares = swap(image.reshape(n_fas, share_rows, LANES), "fas")
        (sums,) = call(norm_kernel, [((n_vox * n_fas, 1, LANES), f32, "v")], "vv")(shares, proj_sq)
        sums = swap(sums, ("vox", "fas"))
        outs = [((vox_rows, BV, LANES), f32, "v")] if last else image_outs
        weights, *partial = call(
            functools.partial(update_kernel, cap, n_vox, last),
            [flat_out, *outs],
            "mvvvvvv",
            [table, acc],
        )(meta, sums, projected, weights, sig, cp, a)
    final = partial[0].reshape(vox_rows, 2, n_fas, own, LANES)[..., :DIRS].transpose(2, 0, 3, 1, 4)
    final = swap(final.reshape(n_fas, vox_rows, own * 2 * DIRS), "fas")
    return (weights.reshape(-1), jnp.sum(final, axis=0))


def solution(mesh):
    placed = (
        P("vox", "fas"),
        P("fas"),
        P(("vox", "fas"), None),
        P(("vox", "fas")),
        P(("vox", "fas")),
        P(("vox", "fas"), None),
        P(("vox", "fas")),
        P(),
    )
    return jax.shard_map(
        functools.partial(local, mesh.shape["vox"], mesh.shape["fas"]),
        mesh=mesh,
        in_specs=placed,
        out_specs=(P("fas"), P("vox", "fas")),
        check_vma=False,
    )
```

profile of v0, /device:TPU:0, one launch (start us, length us, event | category | flops | bytes accessed | tf_op | source)
XLA Modules:
  0.0 330.6 jit_solution(1043015497648106718)
XLA Ops:
  0.7 2.1 copy.25
  4.2 5.1 %shard_map.95 = (bf16[76,64,256]{2,1,0:T(8,128)(2,1)S(1)}, bf16[76,128,256]{2,1,0:T(8,128)(2,1)S(1)}, bf16[76,256,128]{2,1,0:T(8,128)(2,1)S(1)}, s32[1,1024]{1,0:T(1,128)S(4)}) custom-call(s32[1,256]{1,0:T(1,128)S(1)} %bitcast.42, s32[256,128]{1,0:T(8,128)S(1)} %pad.12.side_ref, s32[1,1]{1,0:T(1,128)} %bitcast.23.count_ref, ...), custom_call_target="tpu_custom_call" | custom-call | tf_op jit(solution)/shard_map/pallas_call | solution.py:335
  16.1 4.0 %collective-permute-done.2.refs_3_ = f32[192,128]{1,0:T(8,128)S(1)} collective-permute-done((f32[192,128]{1,0:T(8,128)S(1)}, f32[192,128]{1,0:T(8,128)S(1)}, u32[]{:S(2)}, u32[]{:S(2)}) %collective-permute-start.2) | collective-permute-done | bytes 98336 | tf_op jit(solution)/shard_map/ppermute | solution.py:413
  20.1 4.0 %collective-permute-start.3 = (f32[192,128]{1,0:T(8,128)S(1)}, f32[192,128]{1,0:T(8,128)S(1)}, u32[]{:S(2)}, u32[]{:S(2)}) collective-permute-start(f32[192,128]{1,0:T(8,128)S(1)} %shard_map.97.refs_0_), channel_id=1, source_target_pairs={{0,4},{1,5},{2,6},{3,7},{4,0},{5,1},{6,2},{7,3},{8,12},{9,13},{10,... | collective-permute-start | bytes 294920 | tf_op jit(solution)/shard_map/ppermute | solution.py:419
  24.1 4.0 %collective-permute-done.3.refs_1_ = f32[192,128]{1,0:T(8,128)S(1)} collective-permute-done((f32[192,128]{1,0:T(8,128)S(1)}, f32[192,128]{1,0:T(8,128)S(1)}, u32[]{:S(2)}, u32[]{:S(2)}) %collective-permute-start.3) | collective-permute-done | bytes 98336 | tf_op jit(solution)/shard_map/ppermute | solution.py:419
  31.6 2.2 collective-permute-done.4.refs_1_
  35.5 2.6 shard_map.99
  40.7 4.4 %collective-permute-done.8 = f32[256,128]{1,0:T(8,128)S(1)} collective-permute-done((f32[256,128]{1,0:T(8,128)S(1)}, f32[256,128]{1,0:T(8,128)S(1)}, u32[]{:S(2)}, u32[]{:S(2)}) %collective-permute-start.8) | collective-permute-done | bytes 131104 | tf_op jit(solution)/shard_map/ppermute | solution.py:443
  47.1 16.1 %all_to_all.55.shares_ref = f32[8,96,128]{2,1,0:T(8,128)S(1)} all-to-all(f32[8,96,128]{2,1,0:T(8,128)S(1)} %bitcast.36), channel_id=1, replica_groups=mesh['vox'=4,'fas'=8] {'fas'}, dimensions={0} | all-to-all | bytes 786432 | tf_op jit(solution)/shard_map/all_to_all | solution.py:400
  63.4 10.2 %all_to_all.56.sums_ref = f32[32,1,128]{2,1,0:T(1,128)S(1)} all-to-all(f32[32,1,128]{2,1,0:T(1,128)S(1)} %shard_map.101), channel_id=1, replica_groups=mesh['vox'=4,'fas'=8] {'vox','fas'}, dimensions={0} | all-to-all | bytes 32768 | tf_op jit(solution)/shard_map/all_to_all | solution.py:400
  73.6 2.1 shard_map.102
  77.0 2.3 collective-permute-start.9
  84.2 6.0 %collective-permute-done.12.refs_1_ = f32[192,128]{1,0:T(8,128)S(1)} collective-permute-done((f32[192,128]{1,0:T(8,128)S(1)}, f32[192,128]{1,0:T(8,128)S(1)}, u32[]{:S(2)}, u32[]{:S(2)}) %collective-permute-start.12) | collective-permute-done | bytes 98336 | tf_op jit(solution)/shard_map/ppermute | solution.py:419
  91.6 2.1 collective-permute-start.15
  97.4 2.6 shard_map.105
  102.0 5.0 %collective-permute-done.17 = f32[256,128]{1,0:T(8,128)S(1)} collective-permute-done((f32[256,128]{1,0:T(8,128)S(1)}, f32[256,128]{1,0:T(8,128)S(1)}, u32[]{:S(2)}, u32[]{:S(2)}) %collective-permute-start.17) | collective-permute-done | bytes 131104 | tf_op jit(solution)/shard_map/ppermute | solution.py:443
  109.0 14.9 %all_to_all.57.shares_ref = f32[8,96,128]{2,1,0:T(8,128)S(1)} all-to-all(f32[8,96,128]{2,1,0:T(8,128)S(1)} %bitcast.37), channel_id=1, replica_groups=mesh['vox'=4,'fas'=8] {'fas'}, dimensions={0} | all-to-all | bytes 786432 | tf_op jit(solution)/shard_map/all_to_all | solution.py:400
  124.0 9.5 %all_to_all.58.sums_ref = f32[32,1,128]{2,1,0:T(1,128)S(1)} all-to-all(f32[32,1,128]{2,1,0:T(1,128)S(1)} %shard_map.107), channel_id=1, replica_groups=mesh['vox'=4,'fas'=8] {'vox','fas'}, dimensions={0} | all-to-all | bytes 32768 | tf_op jit(solution)/shard_map/all_to_all | solution.py:400
  133.5 2.3 shard_map.108
  136.2 3.2 collective-permute-start.20
  139.4 2.2 collective-permute-done.18.refs_1_
  143.6 6.1 %collective-permute-done.21.refs_1_ = f32[192,128]{1,0:T(8,128)S(1)} collective-permute-done((f32[192,128]{1,0:T(8,128)S(1)}, f32[192,128]{1,0:T(8,128)S(1)}, u32[]{:S(2)}, u32[]{:S(2)}) %collective-permute-start.21) | collective-permute-done | bytes 98336 | tf_op jit(solution)/shard_map/ppermute | solution.py:419
  151.3 2.0 collective-permute-start.24
  156.9 2.6 shard_map.111
  162.1 4.5 %collective-permute-done.26 = f32[256,128]{1,0:T(8,128)S(1)} collective-permute-done((f32[256,128]{1,0:T(8,128)S(1)}, f32[256,128]{1,0:T(8,128)S(1)}, u32[]{:S(2)}, u32[]{:S(2)}) %collective-permute-start.26) | collective-permute-done | bytes 131104 | tf_op jit(solution)/shard_map/ppermute | solution.py:443
  168.6 14.2 %all_to_all.59.shares_ref = f32[8,96,128]{2,1,0:T(8,128)S(1)} all-to-all(f32[8,96,128]{2,1,0:T(8,128)S(1)} %bitcast.38), channel_id=1, replica_groups=mesh['vox'=4,'fas'=8] {'fas'}, dimensions={0} | all-to-all | bytes 786432 | tf_op jit(solution)/shard_map/all_to_all | solution.py:400
  182.9 10.1 %all_to_all.60.sums_ref = f32[32,1,128]{2,1,0:T(1,128)S(1)} all-to-all(f32[32,1,128]{2,1,0:T(1,128)S(1)} %shard_map.113), channel_id=1, replica_groups=mesh['vox'=4,'fas'=8] {'vox','fas'}, dimensions={0} | all-to-all | bytes 32768 | tf_op jit(solution)/shard_map/all_to_all | solution.py:400
  193.0 2.1 shard_map.114
  195.5 3.2 collective-permute-start.29
  198.7 2.2 collective-permute-done.27.refs_1_
  202.9 6.1 %collective-permute-done.30.refs_1_ = f32[192,128]{1,0:T(8,128)S(1)} collective-permute-done((f32[192,128]{1,0:T(8,128)S(1)}, f32[192,128]{1,0:T(8,128)S(1)}, u32[]{:S(2)}, u32[]{:S(2)}) %collective-permute-start.30) | collective-permute-done | bytes 98336 | tf_op jit(solution)/shard_map/ppermute | solution.py:419
  210.6 2.0 collective-permute-start.33
  216.3 2.6 shard_map.117
  221.4 4.5 %collective-permute-done.35 = f32[256,128]{1,0:T(8,128)S(1)} collective-permute-done((f32[256,128]{1,0:T(8,128)S(1)}, f32[256,128]{1,0:T(8,128)S(1)}, u32[]{:S(2)}, u32[]{:S(2)}) %collective-permute-start.35) | collective-permute-done | bytes 131104 | tf_op jit(solution)/shard_map/ppermute | solution.py:443
  227.9 14.2 %all_to_all.61.shares_ref = f32[8,96,128]{2,1,0:T(8,128)S(1)} all-to-all(f32[8,96,128]{2,1,0:T(8,128)S(1)} %bitcast.39), channel_id=1, replica_groups=mesh['vox'=4,'fas'=8] {'fas'}, dimensions={0} | all-to-all | bytes 786432 | tf_op jit(solution)/shard_map/all_to_all | solution.py:400
  242.2 10.1 %all_to_all.62.sums_ref = f32[32,1,128]{2,1,0:T(1,128)S(1)} all-to-all(f32[32,1,128]{2,1,0:T(1,128)S(1)} %shard_map.119), channel_id=1, replica_groups=mesh['vox'=4,'fas'=8] {'vox','fas'}, dimensions={0} | all-to-all | bytes 32768 | tf_op jit(solution)/shard_map/all_to_all | solution.py:400
  252.3 2.1 shard_map.120
  254.9 3.2 collective-permute-start.38
  258.0 2.2 collective-permute-done.36.refs_1_
  262.2 6.1 %collective-permute-done.39.refs_1_ = f32[192,128]{1,0:T(8,128)S(1)} collective-permute-done((f32[192,128]{1,0:T(8,128)S(1)}, f32[192,128]{1,0:T(8,128)S(1)}, u32[]{:S(2)}, u32[]{:S(2)}) %collective-permute-start.39) | collective-permute-done | bytes 98336 | tf_op jit(solution)/shard_map/ppermute | solution.py:419
  269.9 2.1 collective-permute-start.42
  275.6 2.6 shard_map.123
  280.7 4.5 %collective-permute-done.44 = f32[256,128]{1,0:T(8,128)S(1)} collective-permute-done((f32[256,128]{1,0:T(8,128)S(1)}, f32[256,128]{1,0:T(8,128)S(1)}, u32[]{:S(2)}, u32[]{:S(2)}) %collective-permute-start.44) | collective-permute-done | bytes 131104 | tf_op jit(solution)/shard_map/ppermute | solution.py:443
  287.2 14.2 %all_to_all.63.shares_ref = f32[8,96,128]{2,1,0:T(8,128)S(1)} all-to-all(f32[8,96,128]{2,1,0:T(8,128)S(1)} %bitcast.40), channel_id=1, replica_groups=mesh['vox'=4,'fas'=8] {'fas'}, dimensions={0} | all-to-all | bytes 786432 | tf_op jit(solution)/shard_map/all_to_all | solution.py:400
  301.6 10.1 %all_to_all.64.sums_ref = f32[32,1,128]{2,1,0:T(1,128)S(1)} all-to-all(f32[32,1,128]{2,1,0:T(1,128)S(1)} %shard_map.125), channel_id=1, replica_groups=mesh['vox'=4,'fas'=8] {'vox','fas'}, dimensions={0} | all-to-all | bytes 32768 | tf_op jit(solution)/shard_map/all_to_all | solution.py:400
  311.6 2.0 shard_map.126
  315.4 3.5 %all-to-all-start.10 = ((f32[8,16,768]{2,1,0:T(8,128)}), f32[8,16,768]{2,1,0:T(8,128)S(1)}, u32[]{:S(2)}, u32[]{:S(2)}) async-start(f32[8,16,768]{2,1,0:T(8,128)} %reshape.49), calls=%async_computation.10 | async-start | bytes 786432 | tf_op jit(solution)/shard_map/all_to_all | solution.py:400
  319.6 10.4 %all-to-all-done.10 = f32[8,16,768]{2,1,0:T(8,128)S(1)} async-done(((f32[8,16,768]{2,1,0:T(8,128)}), f32[8,16,768]{2,1,0:T(8,128)S(1)}, u32[]{:S(2)}, u32[]{:S(2)}) %all-to-all-start.10) | async-done | bytes 393248 | tf_op jit(solution)/shard_map/all_to_all | solution.py:400
  (124 shorter events, 72.6 us)
Async XLA Ops:
  0.7 3.4 %copy-start.2 = (bf16[360,96]{0,1:T(8,128)(2,1)S(1)}, bf16[360,96]{0,1:T(8,128)(2,1)}, u32[]{:S(2)}) copy-start(bf16[360,96]{0,1:T(8,128)(2,1)} %param.15) | copy-start | bytes 207364
  2.8 6.5 %copy-start = (f32[32768]{0:T(1024)S(1)}, f32[32768]{0:T(1024)}, u32[]{:S(2)}) copy-start(f32[32768]{0:T(1024)} %param.9) | copy-start | bytes 393220
  11.3 4.7 %collective-permute-start = (f32[192,128]{1,0:T(8,128)S(1)}, f32[192,128]{1,0:T(8,128)S(1)}, u32[]{:S(2)}, u32[]{:S(2)}) collective-permute-start(f32[192,128]{1,0:T(8,128)S(1)} %get-tuple-element.52), channel_id=1, source_target_pairs={{0,1},{1,0},{2,3},{3,2},{4,5},{5,4},{6,7},{7,6},{8,9},{9,8},{10,11... | collective-permute-start | bytes 294920 | tf_op jit(solution)/shard_map/ppermute | solution.py:413
  11.5 4.6 %collective-permute-start.1 = (f32[192,128]{1,0:T(8,128)S(1)}, f32[192,128]{1,0:T(8,128)S(1)}, u32[]{:S(2)}, u32[]{:S(2)}) collective-permute-start(f32[192,128]{1,0:T(8,128)S(1)} %get-tuple-element.53), channel_id=1, source_target_pairs={{0,2},{1,3},{2,0},{3,1},{4,6},{5,7},{6,4},{7,5},{8,10},{9,11},{10,... | collective-permute-start | bytes 294920 | tf_op jit(solution)/shard_map/ppermute | solution.py:413
  13.1 7.0 %collective-permute-start.2 = (f32[192,128]{1,0:T(8,128)S(1)}, f32[192,128]{1,0:T(8,128)S(1)}, u32[]{:S(2)}, u32[]{:S(2)}) collective-permute-start(f32[192,128]{1,0:T(8,128)S(1)} %get-tuple-element.54), channel_id=1, source_target_pairs={{0,3},{1,2},{2,1},{3,0},{4,7},{5,6},{6,5},{7,4},{8,11},{9,10},{10,... | collective-permute-start | bytes 294920 | tf_op jit(solution)/shard_map/ppermute | solution.py:413
  20.1 8.0 %collective-permute-start.3 = (f32[192,128]{1,0:T(8,128)S(1)}, f32[192,128]{1,0:T(8,128)S(1)}, u32[]{:S(2)}, u32[]{:S(2)}) collective-permute-start(f32[192,128]{1,0:T(8,128)S(1)} %shard_map.97.refs_0_), channel_id=1, source_target_pairs={{0,4},{1,5},{2,6},{3,7},{4,0},{5,1},{6,2},{7,3},{8,12},{9,13},{10,... | collective-permute-start | bytes 294920 | tf_op jit(solution)/shard_map/ppermute | solution.py:419
  28.1 5.7 %collective-permute-start.4 = (f32[192,128]{1,0:T(8,128)S(1)}, f32[192,128]{1,0:T(8,128)S(1)}, u32[]{:S(2)}, u32[]{:S(2)}) collective-permute-start(f32[192,128]{1,0:T(8,128)S(1)} %shard_map.98.refs_0_), channel_id=1, source_target_pairs={{0,1},{1,0},{2,3},{3,2},{4,5},{5,4},{6,7},{7,6},{8,9},{9,8},{10,11... | collective-permute-start | bytes 294920 | tf_op jit(solution)/shard_map/ppermute | solution.py:413
  28.8 5.1 %collective-permute-start.5 = (f32[192,128]{1,0:T(8,128)S(1)}, f32[192,128]{1,0:T(8,128)S(1)}, u32[]{:S(2)}, u32[]{:S(2)}) collective-permute-start(f32[192,128]{1,0:T(8,128)S(1)} %shard_map.98.refs_0_), channel_id=1, source_target_pairs={{0,2},{1,3},{2,0},{3,1},{4,6},{5,7},{6,4},{7,5},{8,10},{9,11},{10,... | collective-permute-start | bytes 294920 | tf_op jit(solution)/shard_map/ppermute | solution.py:413
  29.7 5.8 %collective-permute-start.6 = (f32[192,128]{1,0:T(8,128)S(1)}, f32[192,128]{1,0:T(8,128)S(1)}, u32[]{:S(2)}, u32[]{:S(2)}) collective-permute-start(f32[192,128]{1,0:T(8,128)S(1)} %shard_map.98.refs_0_), channel_id=1, source_target_pairs={{0,3},{1,2},{2,1},{3,0},{4,7},{5,6},{6,5},{7,4},{8,11},{9,10},{10,... | collective-permute-start | bytes 294920 | tf_op jit(solution)/shard_map/ppermute | solution.py:413
  38.1 1.4 collective-permute-start.7
  39.5 5.6 %collective-permute-start.8 = (f32[256,128]{1,0:T(8,128)S(1)}, f32[256,128]{1,0:T(8,128)S(1)}, u32[]{:S(2)}, u32[]{:S(2)}) collective-permute-start(f32[256,128]{1,0:T(8,128)S(1)} %add.40), channel_id=1, source_target_pairs={{0,16},{8,24},{16,0},{24,8},{1,17},{9,25},{17,1},{25,9},{2,18},{10... | collective-permute-start | bytes 393224 | tf_op jit(solution)/shard_map/ppermute | solution.py:443
  75.7 5.0 %collective-permute-start.10 = (f32[192,128]{1,0:T(8,128)S(1)}, f32[192,128]{1,0:T(8,128)S(1)}, u32[]{:S(2)}, u32[]{:S(2)}) collective-permute-start(f32[192,128]{1,0:T(8,128)S(1)} %get-tuple-element.60), channel_id=1, source_target_pairs={{0,2},{1,3},{2,0},{3,1},{4,6},{5,7},{6,4},{7,5},{8,10},{9,11},{10,... | collective-permute-start | bytes 294920 | tf_op jit(solution)/shard_map/ppermute | solution.py:413
  75.8 6.0 %collective-permute-start.11 = (f32[192,128]{1,0:T(8,128)S(1)}, f32[192,128]{1,0:T(8,128)S(1)}, u32[]{:S(2)}, u32[]{:S(2)}) collective-permute-start(f32[192,128]{1,0:T(8,128)S(1)} %get-tuple-element.61), channel_id=1, source_target_pairs={{0,3},{1,2},{2,1},{3,0},{4,7},{5,6},{6,5},{7,4},{8,11},{9,10},{10,... | collective-permute-start | bytes 294920 | tf_op jit(solution)/shard_map/ppermute | solution.py:413
  77.0 6.1 %collective-permute-start.9 = (f32[192,128]{1,0:T(8,128)S(1)}, f32[192,128]{1,0:T(8,128)S(1)}, u32[]{:S(2)}, u32[]{:S(2)}) collective-permute-start(f32[192,128]{1,0:T(8,128)S(1)} %get-tuple-element.59), channel_id=1, source_target_pairs={{0,1},{1,0},{2,3},{3,2},{4,5},{5,4},{6,7},{7,6},{8,9},{9,8},{10,11... | collective-permute-start | bytes 294920 | tf_op jit(solution)/shard_map/ppermute | solution.py:413
  83.1 7.0 %collective-permute-start.12 = (f32[192,128]{1,0:T(8,128)S(1)}, f32[192,128]{1,0:T(8,128)S(1)}, u32[]{:S(2)}, u32[]{:S(2)}) collective-permute-start(f32[192,128]{1,0:T(8,128)S(1)} %shard_map.103.refs_0_), channel_id=1, source_target_pairs={{0,4},{1,5},{2,6},{3,7},{4,0},{5,1},{6,2},{7,3},{8,12},{9,13},{10,... | collective-permute-start | bytes 294920 | tf_op jit(solution)/shard_map/ppermute | solution.py:419
  90.2 4.7 %collective-permute-start.13 = (f32[192,128]{1,0:T(8,128)S(1)}, f32[192,128]{1,0:T(8,128)S(1)}, u32[]{:S(2)}, u32[]{:S(2)}) collective-permute-start(f32[192,128]{1,0:T(8,128)S(1)} %shard_map.104.refs_0_), channel_id=1, source_target_pairs={{0,1},{1,0},{2,3},{3,2},{4,5},{5,4},{6,7},{7,6},{8,9},{9,8},{10,11... | collective-permute-start | bytes 294920 | tf_op jit(solution)/shard_map/ppermute | solution.py:413
  91.5 4.6 %collective-permute-start.14 = (f32[192,128]{1,0:T(8,128)S(1)}, f32[192,128]{1,0:T(8,128)S(1)}, u32[]{:S(2)}, u32[]{:S(2)}) collective-permute-start(f32[192,128]{1,0:T(8,128)S(1)} %shard_map.104.refs_0_), channel_id=1, source_target_pairs={{0,2},{1,3},{2,0},{3,1},{4,6},{5,7},{6,4},{7,5},{8,10},{9,11},{10,... | collective-permute-start | bytes 294920 | tf_op jit(solution)/shard_map/ppermute | solution.py:413
  91.6 5.7 %collective-permute-start.15 = (f32[192,128]{1,0:T(8,128)S(1)}, f32[192,128]{1,0:T(8,128)S(1)}, u32[]{:S(2)}, u32[]{:S(2)}) collective-permute-start(f32[192,128]{1,0:T(8,128)S(1)} %shard_map.104.refs_0_), channel_id=1, source_target_pairs={{0,3},{1,2},{2,1},{3,0},{4,7},{5,6},{6,5},{7,4},{8,11},{9,10},{10,... | collective-permute-start | bytes 294920 | tf_op jit(solution)/shard_map/ppermute | solution.py:413
  99.9 1.4 collective-permute-start.16
  101.4 5.6 %collective-permute-start.17 = (f32[256,128]{1,0:T(8,128)S(1)}, f32[256,128]{1,0:T(8,128)S(1)}, u32[]{:S(2)}, u32[]{:S(2)}) collective-permute-start(f32[256,128]{1,0:T(8,128)S(1)} %add.42), channel_id=1, source_target_pairs={{0,16},{8,24},{16,0},{24,8},{1,17},{9,25},{17,1},{25,9},{2,18},{10... | collective-permute-start | bytes 393224 | tf_op jit(solution)/shard_map/ppermute | solution.py:443
  135.8 5.7 %collective-permute-start.18 = (f32[192,128]{1,0:T(8,128)S(1)}, f32[192,128]{1,0:T(8,128)S(1)}, u32[]{:S(2)}, u32[]{:S(2)}) collective-permute-start(f32[192,128]{1,0:T(8,128)S(1)} %get-tuple-element.67), channel_id=1, source_target_pairs={{0,1},{1,0},{2,3},{3,2},{4,5},{5,4},{6,7},{7,6},{8,9},{9,8},{10,11... | collective-permute-start | bytes 294920 | tf_op jit(solution)/shard_map/ppermute | solution.py:413
  135.9 5.7 %collective-permute-start.19 = (f32[192,128]{1,0:T(8,128)S(1)}, f32[192,128]{1,0:T(8,128)S(1)}, u32[]{:S(2)}, u32[]{:S(2)}) collective-permute-start(f32[192,128]{1,0:T(8,128)S(1)} %get-tuple-element.68), channel_id=1, source_target_pairs={{0,2},{1,3},{2,0},{3,1},{4,6},{5,7},{6,4},{7,5},{8,10},{9,11},{10,... | collective-permute-start | bytes 294920 | tf_op jit(solution)/shard_map/ppermute | solution.py:413
  136.2 6.8 %collective-permute-start.20 = (f32[192,128]{1,0:T(8,128)S(1)}, f32[192,128]{1,0:T(8,128)S(1)}, u32[]{:S(2)}, u32[]{:S(2)}) collective-permute-start(f32[192,128]{1,0:T(8,128)S(1)} %get-tuple-element.69), channel_id=1, source_target_pairs={{0,3},{1,2},{2,1},{3,0},{4,7},{5,6},{6,5},{7,4},{8,11},{9,10},{10,... | collective-permute-start | bytes 294920 | tf_op jit(solution)/shard_map/ppermute | solution.py:413
  143.1 6.6 %collective-permute-start.21 = (f32[192,128]{1,0:T(8,128)S(1)}, f32[192,128]{1,0:T(8,128)S(1)}, u32[]{:S(2)}, u32[]{:S(2)}) collective-permute-start(f32[192,128]{1,0:T(8,128)S(1)} %shard_map.109.refs_0_), channel_id=1, source_target_pairs={{0,4},{1,5},{2,6},{3,7},{4,0},{5,1},{6,2},{7,3},{8,12},{9,13},{10,... | collective-permute-start | bytes 294920 | tf_op jit(solution)/shard_map/ppermute | solution.py:419
  149.7 4.7 %collective-permute-start.22 = (f32[192,128]{1,0:T(8,128)S(1)}, f32[192,128]{1,0:T(8,128)S(1)}, u32[]{:S(2)}, u32[]{:S(2)}) collective-permute-start(f32[192,128]{1,0:T(8,128)S(1)} %shard_map.110.refs_0_), channel_id=1, source_target_pairs={{0,1},{1,0},{2,3},{3,2},{4,5},{5,4},{6,7},{7,6},{8,9},{9,8},{10,11... | collective-permute-start | bytes 294920 | tf_op jit(solution)/shard_map/ppermute | solution.py:413
  151.0 4.6 %collective-permute-start.23 = (f32[192,128]{1,0:T(8,128)S(1)}, f32[192,128]{1,0:T(8,128)S(1)}, u32[]{:S(2)}, u32[]{:S(2)}) collective-permute-start(f32[192,128]{1,0:T(8,128)S(1)} %shard_map.110.refs_0_), channel_id=1, source_target_pairs={{0,2},{1,3},{2,0},{3,1},{4,6},{5,7},{6,4},{7,5},{8,10},{9,11},{10,... | collective-permute-start | bytes 294920 | tf_op jit(solution)/shard_map/ppermute | solution.py:413
  151.3 5.7 %collective-permute-start.24 = (f32[192,128]{1,0:T(8,128)S(1)}, f32[192,128]{1,0:T(8,128)S(1)}, u32[]{:S(2)}, u32[]{:S(2)}) collective-permute-start(f32[192,128]{1,0:T(8,128)S(1)} %shard_map.110.refs_0_), channel_id=1, source_target_pairs={{0,3},{1,2},{2,1},{3,0},{4,7},{5,6},{6,5},{7,4},{8,11},{9,10},{10,... | collective-permute-start | bytes 294920 | tf_op jit(solution)/shard_map/ppermute | solution.py:413
  159.5 1.4 collective-permute-start.25
  161.0 5.6 %collective-permute-start.26 = (f32[256,128]{1,0:T(8,128)S(1)}, f32[256,128]{1,0:T(8,128)S(1)}, u32[]{:S(2)}, u32[]{:S(2)}) collective-permute-start(f32[256,128]{1,0:T(8,128)S(1)} %add.44), channel_id=1, source_target_pairs={{0,16},{8,24},{16,0},{24,8},{1,17},{9,25},{17,1},{25,9},{2,18},{10... | collective-permute-start | bytes 393224 | tf_op jit(solution)/shard_map/ppermute | solution.py:443
  195.2 5.7 %collective-permute-start.27 = (f32[192,128]{1,0:T(8,128)S(1)}, f32[192,128]{1,0:T(8,128)S(1)}, u32[]{:S(2)}, u32[]{:S(2)}) collective-permute-start(f32[192,128]{1,0:T(8,128)S(1)} %get-tuple-element.75), channel_id=1, source_target_pairs={{0,1},{1,0},{2,3},{3,2},{4,5},{5,4},{6,7},{7,6},{8,9},{9,8},{10,11... | collective-permute-start | bytes 294920 | tf_op jit(solution)/shard_map/ppermute | solution.py:413
  195.2 5.7 %collective-permute-start.28 = (f32[192,128]{1,0:T(8,128)S(1)}, f32[192,128]{1,0:T(8,128)S(1)}, u32[]{:S(2)}, u32[]{:S(2)}) collective-permute-start(f32[192,128]{1,0:T(8,128)S(1)} %get-tuple-element.76), channel_id=1, source_target_pairs={{0,2},{1,3},{2,0},{3,1},{4,6},{5,7},{6,4},{7,5},{8,10},{9,11},{10,... | collective-permute-start | bytes 294920 | tf_op jit(solution)/shard_map/ppermute | solution.py:413
  195.5 6.8 %collective-permute-start.29 = (f32[192,128]{1,0:T(8,128)S(1)}, f32[192,128]{1,0:T(8,128)S(1)}, u32[]{:S(2)}, u32[]{:S(2)}) collective-permute-start(f32[192,128]{1,0:T(8,128)S(1)} %get-tuple-element.77), channel_id=1, source_target_pairs={{0,3},{1,2},{2,1},{3,0},{4,7},{5,6},{6,5},{7,4},{8,11},{9,10},{10,... | collective-permute-start | bytes 294920 | tf_op jit(solution)/shard_map/ppermute | solution.py:413
  202.4 6.6 %collective-permute-start.30 = (f32[192,128]{1,0:T(8,128)S(1)}, f32[192,128]{1,0:T(8,128)S(1)}, u32[]{:S(2)}, u32[]{:S(2)}) collective-permute-start(f32[192,128]{1,0:T(8,128)S(1)} %shard_map.115.refs_0_), channel_id=1, source_target_pairs={{0,4},{1,5},{2,6},{3,7},{4,0},{5,1},{6,2},{7,3},{8,12},{9,13},{10,... | collective-permute-start | bytes 294920 | tf_op jit(solution)/shard_map/ppermute | solution.py:419
  209.1 4.7 %collective-permute-start.31 = (f32[192,128]{1,0:T(8,128)S(1)}, f32[192,128]{1,0:T(8,128)S(1)}, u32[]{:S(2)}, u32[]{:S(2)}) collective-permute-start(f32[192,128]{1,0:T(8,128)S(1)} %shard_map.116.refs_0_), channel_id=1, source_target_pairs={{0,1},{1,0},{2,3},{3,2},{4,5},{5,4},{6,7},{7,6},{8,9},{9,8},{10,11... | collective-permute-start | bytes 294920 | tf_op jit(solution)/shard_map/ppermute | solution.py:413
  210.3 4.6 %collective-permute-start.32 = (f32[192,128]{1,0:T(8,128)S(1)}, f32[192,128]{1,0:T(8,128)S(1)}, u32[]{:S(2)}, u32[]{:S(2)}) collective-permute-start(f32[192,128]{1,0:T(8,128)S(1)} %shard_map.116.refs_0_), channel_id=1, source_target_pairs={{0,2},{1,3},{2,0},{3,1},{4,6},{5,7},{6,4},{7,5},{8,10},{9,11},{10,... | collective-permute-start | bytes 294920 | tf_op jit(solution)/shard_map/ppermute | solution.py:413
  210.6 5.7 %collective-permute-start.33 = (f32[192,128]{1,0:T(8,128)S(1)}, f32[192,128]{1,0:T(8,128)S(1)}, u32[]{:S(2)}, u32[]{:S(2)}) collective-permute-start(f32[192,128]{1,0:T(8,128)S(1)} %shard_map.116.refs_0_), channel_id=1, source_target_pairs={{0,3},{1,2},{2,1},{3,0},{4,7},{5,6},{6,5},{7,4},{8,11},{9,10},{10,... | collective-permute-start | bytes 294920 | tf_op jit(solution)/shard_map/ppermute | solution.py:413
  218.8 1.4 collective-permute-start.34
  220.3 5.6 %collective-permute-start.35 = (f32[256,128]{1,0:T(8,128)S(1)}, f32[256,128]{1,0:T(8,128)S(1)}, u32[]{:S(2)}, u32[]{:S(2)}) collective-permute-start(f32[256,128]{1,0:T(8,128)S(1)} %add.46), channel_id=1, source_target_pairs={{0,16},{8,24},{16,0},{24,8},{1,17},{9,25},{17,1},{25,9},{2,18},{10... | collective-permute-start | bytes 393224 | tf_op jit(solution)/shard_map/ppermute | solution.py:443
  254.5 5.7 %collective-permute-start.36 = (f32[192,128]{1,0:T(8,128)S(1)}, f32[192,128]{1,0:T(8,128)S(1)}, u32[]{:S(2)}, u32[]{:S(2)}) collective-permute-start(f32[192,128]{1,0:T(8,128)S(1)} %get-tuple-element.83), channel_id=1, source_target_pairs={{0,1},{1,0},{2,3},{3,2},{4,5},{5,4},{6,7},{7,6},{8,9},{9,8},{10,11... | collective-permute-start | bytes 294920 | tf_op jit(solution)/shard_map/ppermute | solution.py:413
  254.5 5.7 %collective-permute-start.37 = (f32[192,128]{1,0:T(8,128)S(1)}, f32[192,128]{1,0:T(8,128)S(1)}, u32[]{:S(2)}, u32[]{:S(2)}) collective-permute-start(f32[192,128]{1,0:T(8,128)S(1)} %get-tuple-element.84), channel_id=1, source_target_pairs={{0,2},{1,3},{2,0},{3,1},{4,6},{5,7},{6,4},{7,5},{8,10},{9,11},{10,... | collective-permute-start | bytes 294920 | tf_op jit(solution)/shard_map/ppermute | solution.py:413
  254.9 6.8 %collective-permute-start.38 = (f32[192,128]{1,0:T(8,128)S(1)}, f32[192,128]{1,0:T(8,128)S(1)}, u32[]{:S(2)}, u32[]{:S(2)}) collective-permute-start(f32[192,128]{1,0:T(8,128)S(1)} %get-tuple-element.85), channel_id=1, source_target_pairs={{0,3},{1,2},{2,1},{3,0},{4,7},{5,6},{6,5},{7,4},{8,11},{9,10},{10,... | collective-permute-start | bytes 294920 | tf_op jit(solution)/shard_map/ppermute | solution.py:413
  261.7 6.6 %collective-permute-start.39 = (f32[192,128]{1,0:T(8,128)S(1)}, f32[192,128]{1,0:T(8,128)S(1)}, u32[]{:S(2)}, u32[]{:S(2)}) collective-permute-start(f32[192,128]{1,0:T(8,128)S(1)} %shard_map.121.refs_0_), channel_id=1, source_target_pairs={{0,4},{1,5},{2,6},{3,7},{4,0},{5,1},{6,2},{7,3},{8,12},{9,13},{10,... | collective-permute-start | bytes 294920 | tf_op jit(solution)/shard_map/ppermute | solution.py:419
  268.4 4.7 %collective-permute-start.40 = (f32[192,128]{1,0:T(8,128)S(1)}, f32[192,128]{1,0:T(8,128)S(1)}, u32[]{:S(2)}, u32[]{:S(2)}) collective-permute-start(f32[192,128]{1,0:T(8,128)S(1)} %shard_map.122.refs_0_), channel_id=1, source_target_pairs={{0,1},{1,0},{2,3},{3,2},{4,5},{5,4},{6,7},{7,6},{8,9},{9,8},{10,11... | collective-permute-start | bytes 294920 | tf_op jit(solution)/shard_map/ppermute | solution.py:413
  269.6 4.6 %collective-permute-start.41 = (f32[192,128]{1,0:T(8,128)S(1)}, f32[192,128]{1,0:T(8,128)S(1)}, u32[]{:S(2)}, u32[]{:S(2)}) collective-permute-start(f32[192,128]{1,0:T(8,128)S(1)} %shard_map.122.refs_0_), channel_id=1, source_target_pairs={{0,2},{1,3},{2,0},{3,1},{4,6},{5,7},{6,4},{7,5},{8,10},{9,11},{10,... | collective-permute-start | bytes 294920 | tf_op jit(solution)/shard_map/ppermute | solution.py:413
  269.9 5.7 %collective-permute-start.42 = (f32[192,128]{1,0:T(8,128)S(1)}, f32[192,128]{1,0:T(8,128)S(1)}, u32[]{:S(2)}, u32[]{:S(2)}) collective-permute-start(f32[192,128]{1,0:T(8,128)S(1)} %shard_map.122.refs_0_), channel_id=1, source_target_pairs={{0,3},{1,2},{2,1},{3,0},{4,7},{5,6},{6,5},{7,4},{8,11},{9,10},{10,... | collective-permute-start | bytes 294920 | tf_op jit(solution)/shard_map/ppermute | solution.py:413
  278.2 1.4 collective-permute-start.43
  279.6 5.6 %collective-permute-start.44 = (f32[256,128]{1,0:T(8,128)S(1)}, f32[256,128]{1,0:T(8,128)S(1)}, u32[]{:S(2)}, u32[]{:S(2)}) collective-permute-start(f32[256,128]{1,0:T(8,128)S(1)} %add.48), channel_id=1, source_target_pairs={{0,16},{8,24},{16,0},{24,8},{1,17},{9,25},{17,1},{25,9},{2,18},{10... | collective-permute-start | bytes 393224 | tf_op jit(solution)/shard_map/ppermute | solution.py:443
  315.4 14.5 %all-to-all-start.10 = ((f32[8,16,768]{2,1,0:T(8,128)}), f32[8,16,768]{2,1,0:T(8,128)S(1)}, u32[]{:S(2)}, u32[]{:S(2)}) async-start(f32[8,16,768]{2,1,0:T(8,128)} %reshape.49), calls=%async_computation.10 | async-start | bytes 786432 | tf_op jit(solution)/shard_map/all_to_all | solution.py:400
  (4 other events, 10.0 us)
where the time goes:
time: 330 us; the launch traced here: 331 us
  blocking collectives  124 us (38%)
  waiting for transfers between devices  107 us (32%)
  starting transfers between devices  51.1 us (15%)
  Pallas kernels  41.2 us (12%)
  local copies, waits for them, and re-layouts  5.07 us (2%)
    all_to_all x10, blocking collectives, swap(): return lax.all_to_all(x, axis, 0, 0, axis_index_groups=groups)  124 us
    pallas_call x32, Pallas kernels, placed(): run(*(pltpu.with_memory_space_constraint(x, spaces[kind]) if kind in 'vm'...  41.2 us
    ppermute x30, waiting for transfers between devices, to_place(): return lax.ppermute(x, 'fas', [(i, i ^ s) for i in range(n_fas)])  38.5 us
    ppermute x30, starting transfers between devices, to_place(): return lax.ppermute(x, 'fas', [(i, i ^ s) for i in range(n_fas)])  35.5 us
    ppermute x10, waiting for transfers between devices, local(): lax.ppermute(gradient, 'vox', [(i, i ^ bit) for i in range(n_vox)])  29.5 us
    ppermute x5, waiting for transfers between devices, sum_all(): other = lax.ppermute(mine, 'fas', across)  28.4 us
    all_to_all x1, waiting for transfers between devices, swap(): return lax.all_to_all(x, axis, 0, 0, axis_index_groups=groups)  10.4 us
  transfers between devices with their start and end apart: 46, of which 42 were waited for; matrix products, arithmetic and copies ran while one was open for 0% of the time, Pallas kernels for 0%

commit v1 on v0

--- a/solution.py
+++ b/solution.py
@@ -201,7 +201,8 @@
     pack_rows(acc_ref, out_refs)
 
 
-def image_kernel(cap, meta_ref, g_ref, w_ref, cp_ref, a_ref, out_ref, p_ref, sq_ref, table_ref, acc_ref):
+def image_kernel(cap, meta_ref, g_ref, w_ref, cp_ref, a_ref, p_ref, sq_ref, *refs):
+    *out_refs, table_ref, acc_ref = refs
     gradient = g_ref[...]
     projected = jnp.where((w_ref[...] > 0) | (gradient < 0), gradient, 0.0)
     p_ref[...] = projected
@@ -209,7 +210,7 @@
     spread_table(projected, table_ref)
     acc_ref[...] = jnp.zeros_like(acc_ref)
     run_forward(cap, meta_ref, cp_ref, a_ref, table_ref, acc_ref)
-    pack_rows(acc_ref, [out_ref])
+    pack_rows(acc_ref, out_refs)
 
 
 def update_kernel(
@@ -308,10 +309,23 @@
         out_ref[i] = total
 
 
-def norm_kernel(shares_ref, sq_ref, out_ref):
-    image = jnp.sum(shares_ref[...], axis=0)
+def join_kernel(sq_ref, *refs):
+    *in_refs, out_ref = refs
+    total = in_refs[0][...]
+    for ref in in_refs[1:]:
+        total = total + ref[...]
+    if len(total.shape) == 3:
+        total = jnp.sum(total, axis=0)
+    rows = total.shape[0]
+    out_ref[:rows, :] = total
+    out_ref[rows:, :] = sq_ref[...]
+
+
+def norm_kernel(mine_ref, other_ref, out_ref):
+    rows = mine_ref.shape[0] - 8
+    image = mine_ref[:rows, :] + other_ref[:rows, :]
     image_sq = jnp.sum(image * image, axis=0, keepdims=True)
-    proj_sq = jnp.sum(sq_ref[...], axis=0, keepdims=True)
+    proj_sq = jnp.sum(mine_ref[rows:, :] + other_ref[rows:, :], axis=0, keepdims=True)
     image_sq = image_sq + pltpu.roll(image_sq, BF, 1)
     proj_sq = proj_sq + pltpu.roll(proj_sq, BF, 1)
     sums = jnp.where(lane_ids(1) < BF, image_sq, proj_sq)
@@ -401,8 +415,8 @@
 
     half = n_fas // 2
     halves = [list(range(half)), list(range(half, n_fas))]
+    both_axes = [[i * n_fas + f for i in range(n_vox) for f in group] for group in halves]
     across = [(i, (i + half) % n_fas) for i in range(n_fas)]
-    share_rows = image_rows // n_fas
     half_share = image_rows // half
 
     parts = half if half <= 4 else 1
@@ -412,15 +426,19 @@
     def to_place(x, s):
         return lax.ppermute(x, "fas", [(i, i ^ s) for i in range(n_fas)])
 
+    def gather_shares(partial):
+        if parts > 1:
+            return [partial[0]] + [to_place(partial[s], s) for s in range(1, parts)]
+        return [swap(partial[0].reshape(half, half_share, LANES), "fas", halves)]
+
     def sum_all(partial):
+        shares = gather_shares(partial)
         if parts > 1:
-            shares = [partial[0]] + [to_place(partial[s], s) for s in range(1, parts)]
             (mine,) = call(sum_kernel, [share_out], "v" * parts)(*shares)
             other = lax.ppermute(mine, "fas", across)
             (total,) = call(sum_kernel, [share_out], "vv")(mine, other)
             return [total] + [to_place(total, s) for s in range(1, parts)]
-        shares = swap(partial[0].reshape(half, half_share, LANES), "fas", halves)
-        (mine,) = call(share_kernel, [share_out], "v")(shares)
+        (mine,) = call(share_kernel, [share_out], "v")(*shares)
         other = lax.ppermute(mine, "fas", across)
         (total,) = call(spread_kernel, [((half, half_share, LANES), f32, "v")], "vv")(mine, other)
         return [swap(total, "fas", halves).reshape(image_rows, LANES)]
@@ -444,15 +462,19 @@
                 gradient, "vox", [(i, i ^ bit) for i in range(n_vox)]
             )
             bit *= 2
-        image, projected, proj_sq = call(
+        projected, proj_sq, *image = call(
             functools.partial(image_kernel, cap),
-            [image_out, flat_out, ((8, LANES), f32, "v")],
+            [flat_out, ((8, LANES), f32, "v"), *image_outs],
             "mvvvv",
             [table, acc],
         )(meta, gradient, weights, cp, a)
-        shares = swap(image.reshape(n_fas, share_rows, LANES), "fas")
-        (sums,) = call(norm_kernel, [((n_vox * n_fas, 1, LANES), f32, "v")], "vv")(shares, proj_sq)
-        sums = swap(sums, ("vox", "fas"))
+        shares = gather_shares(image)
+        (mine,) = call(
+            join_kernel, [((half_share + 8, LANES), f32, "v")], "v" * (1 + len(shares))
+        )(proj_sq, *shares)
+        other = lax.ppermute(mine, "fas", across)
+        (sums,) = call(norm_kernel, [((n_vox * half, 1, LANES), f32, "v")], "vv")(mine, other)
+        sums = swap(sums, ("vox", "fas"), both_axes)
         outs = [((vox_rows, BV, LANES), f32, "v")] if last else image_outs
         weights, *partial = call(
             functools.partial(update_kernel, cap, n_vox, last),

time: 330 us -> 324 us (0.982)
  blocking collectives: 124 us -> 40.5 us
  starting transfers between devices: 51.1 us -> 97.7 us
  waiting for transfers between devices: 107 us -> 136 us
    all_to_all x10 -> x5, blocking collectives: 124 us -> 40.5 us  [swap(): return lax.all_to_all(x, axis, 0, 0, axis_index_groups=groups)]
    ppermute x0 -> x5, waiting for transfers between devices: none -> 19.4 us  [local(): other = lax.ppermute(mine, 'fas', across)]
    ppermute x30 -> x45, starting transfers between devices: 35.5 us -> 54.2 us  [to_place(): return lax.ppermute(x, 'fas', [(i, i ^ s) for i in range(n_fas)])]
    ppermute x30 -> x45, waiting for transfers between devices: 38.5 us -> 56.5 us  [to_place(): return lax.ppermute(x, 'fas', [(i, i ^ s) for i in range(n_fas)])]
    ppermute x0 -> x5, starting transfers between devices: none -> 16.1 us  [local(): other = lax.ppermute(mine, 'fas', across)]
    ppermute x5, starting transfers between devices: 6.54 us -> 18.5 us  [sum_all(): other = lax.ppermute(mine, 'fas', across)]
    ppermute x5, waiting for transfers between devices: 28.4 us -> 18.9 us  [sum_all(): other = lax.ppermute(mine, 'fas', across)]
    pallas_call x32 -> x37, Pallas kernels: 41.2 us -> 40.9 us  [placed(): run(*(pltpu.with_memory_space_constraint(x, spaces[kind]) if kind in 'vm'...]
  transfers between devices with their start and end apart: 46 -> 66, of which waited for: 42 -> 62; matrix products, arithmetic and copies ran while one was open for 0% -> 0% of each run, Pallas kernels for 0% -> 0%
where the time goes in v1:
time: 324 us; the launch traced here: 323 us
  waiting for transfers between devices  136 us (42%)
  starting transfers between devices  97.7 us (30%)
  Pallas kernels  40.9 us (13%)
  blocking collectives  40.5 us (12%)
  local copies, waits for them, and re-layouts  5.09 us (2%)
    ppermute x45, waiting for transfers between devices, to_place(): return lax.ppermute(x, 'fas', [(i, i ^ s) for i in range(n_fas)])  56.5 us
    ppermute x45, starting transfers between devices, to_place(): return lax.ppermute(x, 'fas', [(i, i ^ s) for i in range(n_fas)])  54.2 us
    pallas_call x37, Pallas kernels, placed(): run(*(pltpu.with_memory_space_constraint(x, spaces[kind]) if kind in 'vm'...  40.9 us
    all_to_all x5, blocking collectives, swap(): return lax.all_to_all(x, axis, 0, 0, axis_index_groups=groups)  40.5 us
    ppermute x10, waiting for transfers between devices, local(): lax.ppermute(gradient, 'vox', [(i, i ^ bit) for i in range(n_vox)])  30.8 us
    ppermute x5, waiting for transfers between devices, local(): other = lax.ppermute(mine, 'fas', across)  19.4 us
    ppermute x5, waiting for transfers between devices, sum_all(): other = lax.ppermute(mine, 'fas', across)  18.9 us
    ppermute x5, starting transfers between devices, sum_all(): other = lax.ppermute(mine, 'fas', across)  18.5 us
  transfers between devices with their start and end apart: 66, of which 62 were waited for; matrix products, arithmetic and copies ran while one was open for 0% of the time, Pallas kernels for 0%

profile of v1, /device:TPU:0, one launch (start us, length us, event | category | flops | bytes accessed | tf_op | source)
XLA Modules:
  0.0 323.4 jit_solution(17553324009670662608)
XLA Ops:
  4.2 5.1 %shard_map.95 = (bf16[76,64,256]{2,1,0:T(8,128)(2,1)S(1)}, bf16[76,128,256]{2,1,0:T(8,128)(2,1)S(1)}, bf16[76,256,128]{2,1,0:T(8,128)(2,1)S(1)}, s32[1,1024]{1,0:T(1,128)S(4)}) custom-call(s32[1,256]{1,0:T(1,128)S(1)} %bitcast.32, s32[256,128]{1,0:T(8,128)S(1)} %pad.12.side_ref, s32[1,1]{1,0:T(1,128)} %bitcast.18.count_ref, ...), custom_call_target="tpu_custom_call" | custom-call | tf_op jit(solution)/shard_map/pallas_call | solution.py:349
  11.5 3.0 collective-permute-start.1
  17.7 2.8 collective-permute-done.2.refs_3_
  20.5 3.1 collective-permute-start.3
  23.7 4.3 %collective-permute-done.3.refs_1_ = f32[192,128]{1,0:T(8,128)S(1)} collective-permute-done((f32[192,128]{1,0:T(8,128)S(1)}, f32[192,128]{1,0:T(8,128)S(1)}, u32[]{:S(2)}, u32[]{:S(2)}) %collective-permute-start.3) | collective-permute-done | bytes 98336 | tf_op jit(solution)/shard_map/ppermute | solution.py:438
  35.7 2.5 shard_map.99
  40.8 4.4 %collective-permute-done.8 = f32[256,128]{1,0:T(8,128)S(1)} collective-permute-done((f32[256,128]{1,0:T(8,128)S(1)}, f32[256,128]{1,0:T(8,128)S(1)}, u32[]{:S(2)}, u32[]{:S(2)}) %collective-permute-start.8) | collective-permute-done | bytes 131104 | tf_op jit(solution)/shard_map/ppermute | solution.py:461
  51.9 2.7 collective-permute-done.11.refs_3_
  54.7 2.9 collective-permute-start.12
  57.6 4.4 %collective-permute-done.12.other_ref = f32[200,128]{1,0:T(8,128)S(1)} collective-permute-done((f32[200,128]{1,0:T(8,128)S(1)}, f32[200,128]{1,0:T(8,128)S(1)}, u32[]{:S(2)}, u32[]{:S(2)}) %collective-permute-start.12) | collective-permute-done | bytes 102432 | tf_op jit(solution)/shard_map/ppermute | solution.py:475
  62.1 8.4 %all_to_all.30.sums_ref = f32[16,1,128]{2,1,0:T(1,128)S(1)} all-to-all(f32[16,1,128]{2,1,0:T(1,128)S(1)} %shard_map.102), channel_id=1, replica_groups={{0,1,2,3,8,9,10,11,16,17,18,19,24,25,26,27},{4,5,6,7,12,13,14,15,20,21,..., dimensions={0} | all-to-all | bytes 16384 | tf_op jit(solution)/shard_map/all_to_all | solution.py:414
  73.4 2.8 collective-permute-start.15
  79.9 3.5 %collective-permute-start.16 = (f32[192,128]{1,0:T(8,128)S(1)}, f32[192,128]{1,0:T(8,128)S(1)}, u32[]{:S(2)}, u32[]{:S(2)}) collective-permute-start(f32[192,128]{1,0:T(8,128)S(1)} %shard_map.104.refs_0_), channel_id=1, source_target_pairs={{0,4},{1,5},{2,6},{3,7},{4,0},{5,1},{6,2},{7,3},{8,12},{9,13},{10,... | collective-permute-start | bytes 294920 | tf_op jit(solution)/shard_map/ppermute | solution.py:438
  83.4 3.6 %collective-permute-done.16.refs_1_ = f32[192,128]{1,0:T(8,128)S(1)} collective-permute-done((f32[192,128]{1,0:T(8,128)S(1)}, f32[192,128]{1,0:T(8,128)S(1)}, u32[]{:S(2)}, u32[]{:S(2)}) %collective-permute-start.16) | collective-permute-done | bytes 98336 | tf_op jit(solution)/shard_map/ppermute | solution.py:438
  94.2 2.5 shard_map.106
  99.0 4.8 %collective-permute-done.21 = f32[256,128]{1,0:T(8,128)S(1)} collective-permute-done((f32[256,128]{1,0:T(8,128)S(1)}, f32[256,128]{1,0:T(8,128)S(1)}, u32[]{:S(2)}, u32[]{:S(2)}) %collective-permute-start.21) | collective-permute-done | bytes 131104 | tf_op jit(solution)/shard_map/ppermute | solution.py:461
  113.0 3.3 %collective-permute-start.25 = (f32[200,128]{1,0:T(8,128)S(1)}, f32[200,128]{1,0:T(8,128)S(1)}, u32[]{:S(2)}, u32[]{:S(2)}) collective-permute-start(f32[200,128]{1,0:T(8,128)S(1)} %shard_map.108.mine_ref), channel_id=1, source_target_pairs={{0,4},{1,5},{2,6},{3,7},{4,0},{5,1},{6,2},{7,3},{8,12},{9,13},{10,... | collective-permute-start | bytes 307208 | tf_op jit(solution)/shard_map/ppermute | solution.py:475
  116.3 3.7 %collective-permute-done.25.other_ref = f32[200,128]{1,0:T(8,128)S(1)} collective-permute-done((f32[200,128]{1,0:T(8,128)S(1)}, f32[200,128]{1,0:T(8,128)S(1)}, u32[]{:S(2)}, u32[]{:S(2)}) %collective-permute-start.25) | collective-permute-done | bytes 102432 | tf_op jit(solution)/shard_map/ppermute | solution.py:475
  120.1 8.0 %all_to_all.31.sums_ref = f32[16,1,128]{2,1,0:T(1,128)S(1)} all-to-all(f32[16,1,128]{2,1,0:T(1,128)S(1)} %shard_map.109), channel_id=1, replica_groups={{0,1,2,3,8,9,10,11,16,17,18,19,24,25,26,27},{4,5,6,7,12,13,14,15,20,21,..., dimensions={0} | all-to-all | bytes 16384 | tf_op jit(solution)/shard_map/all_to_all | solution.py:414
  128.2 2.3 shard_map.110
  131.2 2.8 collective-permute-start.28
  137.7 4.0 %collective-permute-start.29 = (f32[192,128]{1,0:T(8,128)S(1)}, f32[192,128]{1,0:T(8,128)S(1)}, u32[]{:S(2)}, u32[]{:S(2)}) collective-permute-start(f32[192,128]{1,0:T(8,128)S(1)} %shard_map.111.refs_0_), channel_id=1, source_target_pairs={{0,4},{1,5},{2,6},{3,7},{4,0},{5,1},{6,2},{7,3},{8,12},{9,13},{10,... | collective-permute-start | bytes 294920 | tf_op jit(solution)/shard_map/ppermute | solution.py:438
  141.6 3.6 %collective-permute-done.29.refs_1_ = f32[192,128]{1,0:T(8,128)S(1)} collective-permute-done((f32[192,128]{1,0:T(8,128)S(1)}, f32[192,128]{1,0:T(8,128)S(1)}, u32[]{:S(2)}, u32[]{:S(2)}) %collective-permute-start.29) | collective-permute-done | bytes 98336 | tf_op jit(solution)/shard_map/ppermute | solution.py:438
  152.5 2.5 shard_map.113
  157.1 5.0 %collective-permute-done.34 = f32[256,128]{1,0:T(8,128)S(1)} collective-permute-done((f32[256,128]{1,0:T(8,128)S(1)}, f32[256,128]{1,0:T(8,128)S(1)}, u32[]{:S(2)}, u32[]{:S(2)}) %collective-permute-start.34) | collective-permute-done | bytes 131104 | tf_op jit(solution)/shard_map/ppermute | solution.py:461
  171.3 3.3 %collective-permute-start.38 = (f32[200,128]{1,0:T(8,128)S(1)}, f32[200,128]{1,0:T(8,128)S(1)}, u32[]{:S(2)}, u32[]{:S(2)}) collective-permute-start(f32[200,128]{1,0:T(8,128)S(1)} %shard_map.115.mine_ref), channel_id=1, source_target_pairs={{0,4},{1,5},{2,6},{3,7},{4,0},{5,1},{6,2},{7,3},{8,12},{9,13},{10,... | collective-permute-start | bytes 307208 | tf_op jit(solution)/shard_map/ppermute | solution.py:475
  174.6 3.7 %collective-permute-done.38.other_ref = f32[200,128]{1,0:T(8,128)S(1)} collective-permute-done((f32[200,128]{1,0:T(8,128)S(1)}, f32[200,128]{1,0:T(8,128)S(1)}, u32[]{:S(2)}, u32[]{:S(2)}) %collective-permute-start.38) | collective-permute-done | bytes 102432 | tf_op jit(solution)/shard_map/ppermute | solution.py:475
  178.4 8.0 %all_to_all.32.sums_ref = f32[16,1,128]{2,1,0:T(1,128)S(1)} all-to-all(f32[16,1,128]{2,1,0:T(1,128)S(1)} %shard_map.116), channel_id=1, replica_groups={{0,1,2,3,8,9,10,11,16,17,18,19,24,25,26,27},{4,5,6,7,12,13,14,15,20,21,..., dimensions={0} | all-to-all | bytes 16384 | tf_op jit(solution)/shard_map/all_to_all | solution.py:414
  189.3 2.8 collective-permute-start.41
  195.8 4.0 %collective-permute-start.42 = (f32[192,128]{1,0:T(8,128)S(1)}, f32[192,128]{1,0:T(8,128)S(1)}, u32[]{:S(2)}, u32[]{:S(2)}) collective-permute-start(f32[192,128]{1,0:T(8,128)S(1)} %shard_map.118.refs_0_), channel_id=1, source_target_pairs={{0,4},{1,5},{2,6},{3,7},{4,0},{5,1},{6,2},{7,3},{8,12},{9,13},{10,... | collective-permute-start | bytes 294920 | tf_op jit(solution)/shard_map/ppermute | solution.py:438
  199.7 3.6 %collective-permute-done.42.refs_1_ = f32[192,128]{1,0:T(8,128)S(1)} collective-permute-done((f32[192,128]{1,0:T(8,128)S(1)}, f32[192,128]{1,0:T(8,128)S(1)}, u32[]{:S(2)}, u32[]{:S(2)}) %collective-permute-start.42) | collective-permute-done | bytes 98336 | tf_op jit(solution)/shard_map/ppermute | solution.py:438
  210.6 2.5 shard_map.120
  215.2 5.0 %collective-permute-done.47 = f32[256,128]{1,0:T(8,128)S(1)} collective-permute-done((f32[256,128]{1,0:T(8,128)S(1)}, f32[256,128]{1,0:T(8,128)S(1)}, u32[]{:S(2)}, u32[]{:S(2)}) %collective-permute-start.47) | collective-permute-done | bytes 131104 | tf_op jit(solution)/shard_map/ppermute | solution.py:461
  223.5 2.2 collective-permute-start.50
  229.3 3.3 %collective-permute-start.51 = (f32[200,128]{1,0:T(8,128)S(1)}, f32[200,128]{1,0:T(8,128)S(1)}, u32[]{:S(2)}, u32[]{:S(2)}) collective-permute-start(f32[200,128]{1,0:T(8,128)S(1)} %shard_map.122.mine_ref), channel_id=1, source_target_pairs={{0,4},{1,5},{2,6},{3,7},{4,0},{5,1},{6,2},{7,3},{8,12},{9,13},{10,... | collective-permute-start | bytes 307208 | tf_op jit(solution)/shard_map/ppermute | solution.py:475
  232.7 3.7 %collective-permute-done.51.other_ref = f32[200,128]{1,0:T(8,128)S(1)} collective-permute-done((f32[200,128]{1,0:T(8,128)S(1)}, f32[200,128]{1,0:T(8,128)S(1)}, u32[]{:S(2)}, u32[]{:S(2)}) %collective-permute-start.51) | collective-permute-done | bytes 102432 | tf_op jit(solution)/shard_map/ppermute | solution.py:475
  236.5 8.0 %all_to_all.33.sums_ref = f32[16,1,128]{2,1,0:T(1,128)S(1)} all-to-all(f32[16,1,128]{2,1,0:T(1,128)S(1)} %shard_map.123), channel_id=1, replica_groups={{0,1,2,3,8,9,10,11,16,17,18,19,24,25,26,27},{4,5,6,7,12,13,14,15,20,21,..., dimensions={0} | all-to-all | bytes 16384 | tf_op jit(solution)/shard_map/all_to_all | solution.py:414
  247.3 2.8 collective-permute-start.54
  253.9 4.0 %collective-permute-start.55 = (f32[192,128]{1,0:T(8,128)S(1)}, f32[192,128]{1,0:T(8,128)S(1)}, u32[]{:S(2)}, u32[]{:S(2)}) collective-permute-start(f32[192,128]{1,0:T(8,128)S(1)} %shard_map.125.refs_0_), channel_id=1, source_target_pairs={{0,4},{1,5},{2,6},{3,7},{4,0},{5,1},{6,2},{7,3},{8,12},{9,13},{10,... | collective-permute-start | bytes 294920 | tf_op jit(solution)/shard_map/ppermute | solution.py:438
  257.8 3.6 %collective-permute-done.55.refs_1_ = f32[192,128]{1,0:T(8,128)S(1)} collective-permute-done((f32[192,128]{1,0:T(8,128)S(1)}, f32[192,128]{1,0:T(8,128)S(1)}, u32[]{:S(2)}, u32[]{:S(2)}) %collective-permute-start.55) | collective-permute-done | bytes 98336 | tf_op jit(solution)/shard_map/ppermute | solution.py:438
  268.7 2.7 shard_map.127
  273.4 5.0 %collective-permute-done.60 = f32[256,128]{1,0:T(8,128)S(1)} collective-permute-done((f32[256,128]{1,0:T(8,128)S(1)}, f32[256,128]{1,0:T(8,128)S(1)}, u32[]{:S(2)}, u32[]{:S(2)}) %collective-permute-start.60) | collective-permute-done | bytes 131104 | tf_op jit(solution)/shard_map/ppermute | solution.py:461
  281.7 2.2 collective-permute-start.63
  287.6 3.3 %collective-permute-start.64 = (f32[200,128]{1,0:T(8,128)S(1)}, f32[200,128]{1,0:T(8,128)S(1)}, u32[]{:S(2)}, u32[]{:S(2)}) collective-permute-start(f32[200,128]{1,0:T(8,128)S(1)} %shard_map.129.mine_ref), channel_id=1, source_target_pairs={{0,4},{1,5},{2,6},{3,7},{4,0},{5,1},{6,2},{7,3},{8,12},{9,13},{10,... | collective-permute-start | bytes 307208 | tf_op jit(solution)/shard_map/ppermute | solution.py:475
  290.9 3.7 %collective-permute-done.64.other_ref = f32[200,128]{1,0:T(8,128)S(1)} collective-permute-done((f32[200,128]{1,0:T(8,128)S(1)}, f32[200,128]{1,0:T(8,128)S(1)}, u32[]{:S(2)}, u32[]{:S(2)}) %collective-permute-start.64) | collective-permute-done | bytes 102432 | tf_op jit(solution)/shard_map/ppermute | solution.py:475
  294.8 8.0 %all_to_all.34.sums_ref = f32[16,1,128]{2,1,0:T(1,128)S(1)} all-to-all(f32[16,1,128]{2,1,0:T(1,128)S(1)} %shard_map.130), channel_id=1, replica_groups={{0,1,2,3,8,9,10,11,16,17,18,19,24,25,26,27},{4,5,6,7,12,13,14,15,20,21,..., dimensions={0} | all-to-all | bytes 16384 | tf_op jit(solution)/shard_map/all_to_all | solution.py:414
  306.6 4.5 %all-to-all-start.5 = ((f32[8,16,768]{2,1,0:T(8,128)}), f32[8,16,768]{2,1,0:T(8,128)S(1)}, u32[]{:S(2)}, u32[]{:S(2)}) async-start(f32[8,16,768]{2,1,0:T(8,128)} %reshape.29), calls=%async_computation.5 | async-start | bytes 786432 | tf_op jit(solution)/shard_map/all_to_all | solution.py:414
  311.8 11.0 %all-to-all-done.5 = f32[8,16,768]{2,1,0:T(8,128)S(1)} async-done(((f32[8,16,768]{2,1,0:T(8,128)}), f32[8,16,768]{2,1,0:T(8,128)S(1)}, u32[]{:S(2)}, u32[]{:S(2)}) %all-to-all-start.5) | async-done | bytes 393248 | tf_op jit(solution)/shard_map/all_to_all | solution.py:414
  (164 shorter events, 124.5 us)
Async XLA Ops:
  11.3 5.7 %collective-permute-start = (f32[192,128]{1,0:T(8,128)S(1)}, f32[192,128]{1,0:T(8,128)S(1)}, u32[]{:S(2)}, u32[]{:S(2)}) collective-permute-start(f32[192,128]{1,0:T(8,128)S(1)} %get-tuple-element.67), channel_id=1, source_target_pairs={{0,1},{1,0},{2,3},{3,2},{4,5},{5,4},{6,7},{7,6},{8,9},{9,8},{10,11... | collective-permute-start | bytes 294920 | tf_op jit(solution)/shard_map/ppermute | solution.py:427
  11.5 6.3 %collective-permute-start.1 = (f32[192,128]{1,0:T(8,128)S(1)}, f32[192,128]{1,0:T(8,128)S(1)}, u32[]{:S(2)}, u32[]{:S(2)}) collective-permute-start(f32[192,128]{1,0:T(8,128)S(1)} %get-tuple-element.68), channel_id=1, source_target_pairs={{0,2},{1,3},{2,0},{3,1},{4,6},{5,7},{6,4},{7,5},{8,10},{9,11},{10,... | collective-permute-start | bytes 294920 | tf_op jit(solution)/shard_map/ppermute | solution.py:427
  14.5 6.1 %collective-permute-start.2 = (f32[192,128]{1,0:T(8,128)S(1)}, f32[192,128]{1,0:T(8,128)S(1)}, u32[]{:S(2)}, u32[]{:S(2)}) collective-permute-start(f32[192,128]{1,0:T(8,128)S(1)} %get-tuple-element.69), channel_id=1, source_target_pairs={{0,3},{1,2},{2,1},{3,0},{4,7},{5,6},{6,5},{7,4},{8,11},{9,10},{10,... | collective-permute-start | bytes 294920 | tf_op jit(solution)/shard_map/ppermute | solution.py:427
  20.5 7.4 %collective-permute-start.3 = (f32[192,128]{1,0:T(8,128)S(1)}, f32[192,128]{1,0:T(8,128)S(1)}, u32[]{:S(2)}, u32[]{:S(2)}) collective-permute-start(f32[192,128]{1,0:T(8,128)S(1)} %shard_map.97.refs_0_), channel_id=1, source_target_pairs={{0,4},{1,5},{2,6},{3,7},{4,0},{5,1},{6,2},{7,3},{8,12},{9,13},{10,... | collective-permute-start | bytes 294920 | tf_op jit(solution)/shard_map/ppermute | solution.py:438
  29.8 5.9 %collective-permute-start.6 = (f32[192,128]{1,0:T(8,128)S(1)}, f32[192,128]{1,0:T(8,128)S(1)}, u32[]{:S(2)}, u32[]{:S(2)}) collective-permute-start(f32[192,128]{1,0:T(8,128)S(1)} %shard_map.98.refs_0_), channel_id=1, source_target_pairs={{0,3},{1,2},{2,1},{3,0},{4,7},{5,6},{6,5},{7,4},{8,11},{9,10},{10,... | collective-permute-start | bytes 294920 | tf_op jit(solution)/shard_map/ppermute | solution.py:427
  39.6 5.6 %collective-permute-start.8 = (f32[256,128]{1,0:T(8,128)S(1)}, f32[256,128]{1,0:T(8,128)S(1)}, u32[]{:S(2)}, u32[]{:S(2)}) collective-permute-start(f32[256,128]{1,0:T(8,128)S(1)} %add.40), channel_id=1, source_target_pairs={{0,16},{8,24},{16,0},{24,8},{1,17},{9,25},{17,1},{25,9},{2,18},{10... | collective-permute-start | bytes 393224 | tf_op jit(solution)/shard_map/ppermute | solution.py:461
  49.0 5.6 %collective-permute-start.11 = (f32[192,128]{1,0:T(8,128)S(1)}, f32[192,128]{1,0:T(8,128)S(1)}, u32[]{:S(2)}, u32[]{:S(2)}) collective-permute-start(f32[192,128]{1,0:T(8,128)S(1)} %get-tuple-element.74), channel_id=1, source_target_pairs={{0,3},{1,2},{2,1},{3,0},{4,7},{5,6},{6,5},{7,4},{8,11},{9,10},{10,... | collective-permute-start | bytes 294920 | tf_op jit(solution)/shard_map/ppermute | solution.py:427
  49.0 5.7 %collective-permute-start.9 = (f32[192,128]{1,0:T(8,128)S(1)}, f32[192,128]{1,0:T(8,128)S(1)}, u32[]{:S(2)}, u32[]{:S(2)}) collective-permute-start(f32[192,128]{1,0:T(8,128)S(1)} %get-tuple-element.72), channel_id=1, source_target_pairs={{0,1},{1,0},{2,3},{3,2},{4,5},{5,4},{6,7},{7,6},{8,9},{9,8},{10,11... | collective-permute-start | bytes 294920 | tf_op jit(solution)/shard_map/ppermute | solution.py:427
  54.7 7.3 %collective-permute-start.12 = (f32[200,128]{1,0:T(8,128)S(1)}, f32[200,128]{1,0:T(8,128)S(1)}, u32[]{:S(2)}, u32[]{:S(2)}) collective-permute-start(f32[200,128]{1,0:T(8,128)S(1)} %shard_map.101.mine_ref), channel_id=1, source_target_pairs={{0,4},{1,5},{2,6},{3,7},{4,0},{5,1},{6,2},{7,3},{8,12},{9,13},{10,... | collective-permute-start | bytes 307208 | tf_op jit(solution)/shard_map/ppermute | solution.py:475
  72.7 5.7 %collective-permute-start.13 = (f32[192,128]{1,0:T(8,128)S(1)}, f32[192,128]{1,0:T(8,128)S(1)}, u32[]{:S(2)}, u32[]{:S(2)}) collective-permute-start(f32[192,128]{1,0:T(8,128)S(1)} %get-tuple-element.77), channel_id=1, source_target_pairs={{0,1},{1,0},{2,3},{3,2},{4,5},{5,4},{6,7},{7,6},{8,9},{9,8},{10,11... | collective-permute-start | bytes 294920 | tf_op jit(solution)/shard_map/ppermute | solution.py:427
  72.7 5.7 %collective-permute-start.14 = (f32[192,128]{1,0:T(8,128)S(1)}, f32[192,128]{1,0:T(8,128)S(1)}, u32[]{:S(2)}, u32[]{:S(2)}) collective-permute-start(f32[192,128]{1,0:T(8,128)S(1)} %get-tuple-element.78), channel_id=1, source_target_pairs={{0,2},{1,3},{2,0},{3,1},{4,6},{5,7},{6,4},{7,5},{8,10},{9,11},{10,... | collective-permute-start | bytes 294920 | tf_op jit(solution)/shard_map/ppermute | solution.py:427
  73.4 6.5 %collective-permute-start.15 = (f32[192,128]{1,0:T(8,128)S(1)}, f32[192,128]{1,0:T(8,128)S(1)}, u32[]{:S(2)}, u32[]{:S(2)}) collective-permute-start(f32[192,128]{1,0:T(8,128)S(1)} %get-tuple-element.79), channel_id=1, source_target_pairs={{0,3},{1,2},{2,1},{3,0},{4,7},{5,6},{6,5},{7,4},{8,11},{9,10},{10,... | collective-permute-start | bytes 294920 | tf_op jit(solution)/shard_map/ppermute | solution.py:427
  79.9 7.1 %collective-permute-start.16 = (f32[192,128]{1,0:T(8,128)S(1)}, f32[192,128]{1,0:T(8,128)S(1)}, u32[]{:S(2)}, u32[]{:S(2)}) collective-permute-start(f32[192,128]{1,0:T(8,128)S(1)} %shard_map.104.refs_0_), channel_id=1, source_target_pairs={{0,4},{1,5},{2,6},{3,7},{4,0},{5,1},{6,2},{7,3},{8,12},{9,13},{10,... | collective-permute-start | bytes 294920 | tf_op jit(solution)/shard_map/ppermute | solution.py:438
  88.4 5.8 %collective-permute-start.19 = (f32[192,128]{1,0:T(8,128)S(1)}, f32[192,128]{1,0:T(8,128)S(1)}, u32[]{:S(2)}, u32[]{:S(2)}) collective-permute-start(f32[192,128]{1,0:T(8,128)S(1)} %shard_map.105.refs_0_), channel_id=1, source_target_pairs={{0,3},{1,2},{2,1},{3,0},{4,7},{5,6},{6,5},{7,4},{8,11},{9,10},{10,... | collective-permute-start | bytes 294920 | tf_op jit(solution)/shard_map/ppermute | solution.py:427
  98.1 5.6 %collective-permute-start.21 = (f32[256,128]{1,0:T(8,128)S(1)}, f32[256,128]{1,0:T(8,128)S(1)}, u32[]{:S(2)}, u32[]{:S(2)}) collective-permute-start(f32[256,128]{1,0:T(8,128)S(1)} %add.42), channel_id=1, source_target_pairs={{0,16},{8,24},{16,0},{24,8},{1,17},{9,25},{17,1},{25,9},{2,18},{10... | collective-permute-start | bytes 393224 | tf_op jit(solution)/shard_map/ppermute | solution.py:461
  105.8 5.5 %collective-permute-start.22 = (f32[192,128]{1,0:T(8,128)S(1)}, f32[192,128]{1,0:T(8,128)S(1)}, u32[]{:S(2)}, u32[]{:S(2)}) collective-permute-start(f32[192,128]{1,0:T(8,128)S(1)} %get-tuple-element.83), channel_id=1, source_target_pairs={{0,1},{1,0},{2,3},{3,2},{4,5},{5,4},{6,7},{7,6},{8,9},{9,8},{10,11... | collective-permute-start | bytes 294920 | tf_op jit(solution)/shard_map/ppermute | solution.py:427
  105.8 5.4 %collective-permute-start.23 = (f32[192,128]{1,0:T(8,128)S(1)}, f32[192,128]{1,0:T(8,128)S(1)}, u32[]{:S(2)}, u32[]{:S(2)}) collective-permute-start(f32[192,128]{1,0:T(8,128)S(1)} %get-tuple-element.84), channel_id=1, source_target_pairs={{0,2},{1,3},{2,0},{3,1},{4,6},{5,7},{6,4},{7,5},{8,10},{9,11},{10,... | collective-permute-start | bytes 294920 | tf_op jit(solution)/shard_map/ppermute | solution.py:427
  107.1 5.8 %collective-permute-start.24 = (f32[192,128]{1,0:T(8,128)S(1)}, f32[192,128]{1,0:T(8,128)S(1)}, u32[]{:S(2)}, u32[]{:S(2)}) collective-permute-start(f32[192,128]{1,0:T(8,128)S(1)} %get-tuple-element.85), channel_id=1, source_target_pairs={{0,3},{1,2},{2,1},{3,0},{4,7},{5,6},{6,5},{7,4},{8,11},{9,10},{10,... | collective-permute-start | bytes 294920 | tf_op jit(solution)/shard_map/ppermute | solution.py:427
  113.0 7.0 %collective-permute-start.25 = (f32[200,128]{1,0:T(8,128)S(1)}, f32[200,128]{1,0:T(8,128)S(1)}, u32[]{:S(2)}, u32[]{:S(2)}) collective-permute-start(f32[200,128]{1,0:T(8,128)S(1)} %shard_map.108.mine_ref), channel_id=1, source_target_pairs={{0,4},{1,5},{2,6},{3,7},{4,0},{5,1},{6,2},{7,3},{8,12},{9,13},{10,... | collective-permute-start | bytes 307208 | tf_op jit(solution)/shard_map/ppermute | solution.py:475
  130.4 5.7 %collective-permute-start.26 = (f32[192,128]{1,0:T(8,128)S(1)}, f32[192,128]{1,0:T(8,128)S(1)}, u32[]{:S(2)}, u32[]{:S(2)}) collective-permute-start(f32[192,128]{1,0:T(8,128)S(1)} %get-tuple-element.88), channel_id=1, source_target_pairs={{0,1},{1,0},{2,3},{3,2},{4,5},{5,4},{6,7},{7,6},{8,9},{9,8},{10,11... | collective-permute-start | bytes 294920 | tf_op jit(solution)/shard_map/ppermute | solution.py:427
  130.5 5.7 %collective-permute-start.27 = (f32[192,128]{1,0:T(8,128)S(1)}, f32[192,128]{1,0:T(8,128)S(1)}, u32[]{:S(2)}, u32[]{:S(2)}) collective-permute-start(f32[192,128]{1,0:T(8,128)S(1)} %get-tuple-element.89), channel_id=1, source_target_pairs={{0,2},{1,3},{2,0},{3,1},{4,6},{5,7},{6,4},{7,5},{8,10},{9,11},{10,... | collective-permute-start | bytes 294920 | tf_op jit(solution)/shard_map/ppermute | solution.py:427
  131.2 6.5 %collective-permute-start.28 = (f32[192,128]{1,0:T(8,128)S(1)}, f32[192,128]{1,0:T(8,128)S(1)}, u32[]{:S(2)}, u32[]{:S(2)}) collective-permute-start(f32[192,128]{1,0:T(8,128)S(1)} %get-tuple-element.90), channel_id=1, source_target_pairs={{0,3},{1,2},{2,1},{3,0},{4,7},{5,6},{6,5},{7,4},{8,11},{9,10},{10,... | collective-permute-start | bytes 294920 | tf_op jit(solution)/shard_map/ppermute | solution.py:427
  137.7 7.6 %collective-permute-start.29 = (f32[192,128]{1,0:T(8,128)S(1)}, f32[192,128]{1,0:T(8,128)S(1)}, u32[]{:S(2)}, u32[]{:S(2)}) collective-permute-start(f32[192,128]{1,0:T(8,128)S(1)} %shard_map.111.refs_0_), channel_id=1, source_target_pairs={{0,4},{1,5},{2,6},{3,7},{4,0},{5,1},{6,2},{7,3},{8,12},{9,13},{10,... | collective-permute-start | bytes 294920 | tf_op jit(solution)/shard_map/ppermute | solution.py:438
  146.7 5.8 %collective-permute-start.32 = (f32[192,128]{1,0:T(8,128)S(1)}, f32[192,128]{1,0:T(8,128)S(1)}, u32[]{:S(2)}, u32[]{:S(2)}) collective-permute-start(f32[192,128]{1,0:T(8,128)S(1)} %shard_map.112.refs_0_), channel_id=1, source_target_pairs={{0,3},{1,2},{2,1},{3,0},{4,7},{5,6},{6,5},{7,4},{8,11},{9,10},{10,... | collective-permute-start | bytes 294920 | tf_op jit(solution)/shard_map/ppermute | solution.py:427
  156.4 5.6 %collective-permute-start.34 = (f32[256,128]{1,0:T(8,128)S(1)}, f32[256,128]{1,0:T(8,128)S(1)}, u32[]{:S(2)}, u32[]{:S(2)}) collective-permute-start(f32[256,128]{1,0:T(8,128)S(1)} %add.44), channel_id=1, source_target_pairs={{0,16},{8,24},{16,0},{24,8},{1,17},{9,25},{17,1},{25,9},{2,18},{10... | collective-permute-start | bytes 393224 | tf_op jit(solution)/shard_map/ppermute | solution.py:461
  164.0 5.5 %collective-permute-start.35 = (f32[192,128]{1,0:T(8,128)S(1)}, f32[192,128]{1,0:T(8,128)S(1)}, u32[]{:S(2)}, u32[]{:S(2)}) collective-permute-start(f32[192,128]{1,0:T(8,128)S(1)} %get-tuple-element.94), channel_id=1, source_target_pairs={{0,1},{1,0},{2,3},{3,2},{4,5},{5,4},{6,7},{7,6},{8,9},{9,8},{10,11... | collective-permute-start | bytes 294920 | tf_op jit(solution)/shard_map/ppermute | solution.py:427
  165.4 5.9 %collective-permute-start.37 = (f32[192,128]{1,0:T(8,128)S(1)}, f32[192,128]{1,0:T(8,128)S(1)}, u32[]{:S(2)}, u32[]{:S(2)}) collective-permute-start(f32[192,128]{1,0:T(8,128)S(1)} %get-tuple-element.96), channel_id=1, source_target_pairs={{0,3},{1,2},{2,1},{3,0},{4,7},{5,6},{6,5},{7,4},{8,11},{9,10},{10,... | collective-permute-start | bytes 294920 | tf_op jit(solution)/shard_map/ppermute | solution.py:427
  171.3 7.0 %collective-permute-start.38 = (f32[200,128]{1,0:T(8,128)S(1)}, f32[200,128]{1,0:T(8,128)S(1)}, u32[]{:S(2)}, u32[]{:S(2)}) collective-permute-start(f32[200,128]{1,0:T(8,128)S(1)} %shard_map.115.mine_ref), channel_id=1, source_target_pairs={{0,4},{1,5},{2,6},{3,7},{4,0},{5,1},{6,2},{7,3},{8,12},{9,13},{10,... | collective-permute-start | bytes 307208 | tf_op jit(solution)/shard_map/ppermute | solution.py:475
  188.5 5.7 %collective-permute-start.39 = (f32[192,128]{1,0:T(8,128)S(1)}, f32[192,128]{1,0:T(8,128)S(1)}, u32[]{:S(2)}, u32[]{:S(2)}) collective-permute-start(f32[192,128]{1,0:T(8,128)S(1)} %get-tuple-element.99), channel_id=1, source_target_pairs={{0,1},{1,0},{2,3},{3,2},{4,5},{5,4},{6,7},{7,6},{8,9},{9,8},{10,11... | collective-permute-start | bytes 294920 | tf_op jit(solution)/shard_map/ppermute | solution.py:427
  188.6 5.7 %collective-permute-start.40 = (f32[192,128]{1,0:T(8,128)S(1)}, f32[192,128]{1,0:T(8,128)S(1)}, u32[]{:S(2)}, u32[]{:S(2)}) collective-permute-start(f32[192,128]{1,0:T(8,128)S(1)} %get-tuple-element.100), channel_id=1, source_target_pairs={{0,2},{1,3},{2,0},{3,1},{4,6},{5,7},{6,4},{7,5},{8,10},{9,11},{10,... | collective-permute-start | bytes 294920 | tf_op jit(solution)/shard_map/ppermute | solution.py:427
  189.3 6.5 %collective-permute-start.41 = (f32[192,128]{1,0:T(8,128)S(1)}, f32[192,128]{1,0:T(8,128)S(1)}, u32[]{:S(2)}, u32[]{:S(2)}) collective-permute-start(f32[192,128]{1,0:T(8,128)S(1)} %get-tuple-element.101), channel_id=1, source_target_pairs={{0,3},{1,2},{2,1},{3,0},{4,7},{5,6},{6,5},{7,4},{8,11},{9,10},{10,... | collective-permute-start | bytes 294920 | tf_op jit(solution)/shard_map/ppermute | solution.py:427
  195.8 7.6 %collective-permute-start.42 = (f32[192,128]{1,0:T(8,128)S(1)}, f32[192,128]{1,0:T(8,128)S(1)}, u32[]{:S(2)}, u32[]{:S(2)}) collective-permute-start(f32[192,128]{1,0:T(8,128)S(1)} %shard_map.118.refs_0_), channel_id=1, source_target_pairs={{0,4},{1,5},{2,6},{3,7},{4,0},{5,1},{6,2},{7,3},{8,12},{9,13},{10,... | collective-permute-start | bytes 294920 | tf_op jit(solution)/shard_map/ppermute | solution.py:438
  204.8 5.8 %collective-permute-start.45 = (f32[192,128]{1,0:T(8,128)S(1)}, f32[192,128]{1,0:T(8,128)S(1)}, u32[]{:S(2)}, u32[]{:S(2)}) collective-permute-start(f32[192,128]{1,0:T(8,128)S(1)} %shard_map.119.refs_0_), channel_id=1, source_target_pairs={{0,3},{1,2},{2,1},{3,0},{4,7},{5,6},{6,5},{7,4},{8,11},{9,10},{10,... | collective-permute-start | bytes 294920 | tf_op jit(solution)/shard_map/ppermute | solution.py:427
  214.5 5.6 %collective-permute-start.47 = (f32[256,128]{1,0:T(8,128)S(1)}, f32[256,128]{1,0:T(8,128)S(1)}, u32[]{:S(2)}, u32[]{:S(2)}) collective-permute-start(f32[256,128]{1,0:T(8,128)S(1)} %add.46), channel_id=1, source_target_pairs={{0,16},{8,24},{16,0},{24,8},{1,17},{9,25},{17,1},{25,9},{2,18},{10... | collective-permute-start | bytes 393224 | tf_op jit(solution)/shard_map/ppermute | solution.py:461
  222.1 5.5 %collective-permute-start.48 = (f32[192,128]{1,0:T(8,128)S(1)}, f32[192,128]{1,0:T(8,128)S(1)}, u32[]{:S(2)}, u32[]{:S(2)}) collective-permute-start(f32[192,128]{1,0:T(8,128)S(1)} %get-tuple-element.105), channel_id=1, source_target_pairs={{0,1},{1,0},{2,3},{3,2},{4,5},{5,4},{6,7},{7,6},{8,9},{9,8},{10,11... | collective-permute-start | bytes 294920 | tf_op jit(solution)/shard_map/ppermute | solution.py:427
  223.5 5.9 %collective-permute-start.50 = (f32[192,128]{1,0:T(8,128)S(1)}, f32[192,128]{1,0:T(8,128)S(1)}, u32[]{:S(2)}, u32[]{:S(2)}) collective-permute-start(f32[192,128]{1,0:T(8,128)S(1)} %get-tuple-element.107), channel_id=1, source_target_pairs={{0,3},{1,2},{2,1},{3,0},{4,7},{5,6},{6,5},{7,4},{8,11},{9,10},{10,... | collective-permute-start | bytes 294920 | tf_op jit(solution)/shard_map/ppermute | solution.py:427
  229.3 7.0 %collective-permute-start.51 = (f32[200,128]{1,0:T(8,128)S(1)}, f32[200,128]{1,0:T(8,128)S(1)}, u32[]{:S(2)}, u32[]{:S(2)}) collective-permute-start(f32[200,128]{1,0:T(8,128)S(1)} %shard_map.122.mine_ref), channel_id=1, source_target_pairs={{0,4},{1,5},{2,6},{3,7},{4,0},{5,1},{6,2},{7,3},{8,12},{9,13},{10,... | collective-permute-start | bytes 307208 | tf_op jit(solution)/shard_map/ppermute | solution.py:475
  246.6 5.7 %collective-permute-start.52 = (f32[192,128]{1,0:T(8,128)S(1)}, f32[192,128]{1,0:T(8,128)S(1)}, u32[]{:S(2)}, u32[]{:S(2)}) collective-permute-start(f32[192,128]{1,0:T(8,128)S(1)} %get-tuple-element.110), channel_id=1, source_target_pairs={{0,1},{1,0},{2,3},{3,2},{4,5},{5,4},{6,7},{7,6},{8,9},{9,8},{10,11... | collective-permute-start | bytes 294920 | tf_op jit(solution)/shard_map/ppermute | solution.py:427
  246.7 5.7 %collective-permute-start.53 = (f32[192,128]{1,0:T(8,128)S(1)}, f32[192,128]{1,0:T(8,128)S(1)}, u32[]{:S(2)}, u32[]{:S(2)}) collective-permute-start(f32[192,128]{1,0:T(8,128)S(1)} %get-tuple-element.111), channel_id=1, source_target_pairs={{0,2},{1,3},{2,0},{3,1},{4,6},{5,7},{6,4},{7,5},{8,10},{9,11},{10,... | collective-permute-start | bytes 294920 | tf_op jit(solution)/shard_map/ppermute | solution.py:427
  247.3 6.5 %collective-permute-start.54 = (f32[192,128]{1,0:T(8,128)S(1)}, f32[192,128]{1,0:T(8,128)S(1)}, u32[]{:S(2)}, u32[]{:S(2)}) collective-permute-start(f32[192,128]{1,0:T(8,128)S(1)} %get-tuple-element.112), channel_id=1, source_target_pairs={{0,3},{1,2},{2,1},{3,0},{4,7},{5,6},{6,5},{7,4},{8,11},{9,10},{10,... | collective-permute-start | bytes 294920 | tf_op jit(solution)/shard_map/ppermute | solution.py:427
  253.9 7.6 %collective-permute-start.55 = (f32[192,128]{1,0:T(8,128)S(1)}, f32[192,128]{1,0:T(8,128)S(1)}, u32[]{:S(2)}, u32[]{:S(2)}) collective-permute-start(f32[192,128]{1,0:T(8,128)S(1)} %shard_map.125.refs_0_), channel_id=1, source_target_pairs={{0,4},{1,5},{2,6},{3,7},{4,0},{5,1},{6,2},{7,3},{8,12},{9,13},{10,... | collective-permute-start | bytes 294920 | tf_op jit(solution)/shard_map/ppermute | solution.py:438
  262.9 5.8 %collective-permute-start.58 = (f32[192,128]{1,0:T(8,128)S(1)}, f32[192,128]{1,0:T(8,128)S(1)}, u32[]{:S(2)}, u32[]{:S(2)}) collective-permute-start(f32[192,128]{1,0:T(8,128)S(1)} %shard_map.126.refs_0_), channel_id=1, source_target_pairs={{0,3},{1,2},{2,1},{3,0},{4,7},{5,6},{6,5},{7,4},{8,11},{9,10},{10,... | collective-permute-start | bytes 294920 | tf_op jit(solution)/shard_map/ppermute | solution.py:427
  272.8 5.6 %collective-permute-start.60 = (f32[256,128]{1,0:T(8,128)S(1)}, f32[256,128]{1,0:T(8,128)S(1)}, u32[]{:S(2)}, u32[]{:S(2)}) collective-permute-start(f32[256,128]{1,0:T(8,128)S(1)} %add.48), channel_id=1, source_target_pairs={{0,16},{8,24},{16,0},{24,8},{1,17},{9,25},{17,1},{25,9},{2,18},{10... | collective-permute-start | bytes 393224 | tf_op jit(solution)/shard_map/ppermute | solution.py:461
  280.4 5.5 %collective-permute-start.61 = (f32[192,128]{1,0:T(8,128)S(1)}, f32[192,128]{1,0:T(8,128)S(1)}, u32[]{:S(2)}, u32[]{:S(2)}) collective-permute-start(f32[192,128]{1,0:T(8,128)S(1)} %get-tuple-element.116), channel_id=1, source_target_pairs={{0,1},{1,0},{2,3},{3,2},{4,5},{5,4},{6,7},{7,6},{8,9},{9,8},{10,11... | collective-permute-start | bytes 294920 | tf_op jit(solution)/shard_map/ppermute | solution.py:427
  280.5 5.4 %collective-permute-start.62 = (f32[192,128]{1,0:T(8,128)S(1)}, f32[192,128]{1,0:T(8,128)S(1)}, u32[]{:S(2)}, u32[]{:S(2)}) collective-permute-start(f32[192,128]{1,0:T(8,128)S(1)} %get-tuple-element.117), channel_id=1, source_target_pairs={{0,2},{1,3},{2,0},{3,1},{4,6},{5,7},{6,4},{7,5},{8,10},{9,11},{10,... | collective-permute-start | bytes 294920 | tf_op jit(solution)/shard_map/ppermute | solution.py:427
  281.7 5.9 %collective-permute-start.63 = (f32[192,128]{1,0:T(8,128)S(1)}, f32[192,128]{1,0:T(8,128)S(1)}, u32[]{:S(2)}, u32[]{:S(2)}) collective-permute-start(f32[192,128]{1,0:T(8,128)S(1)} %get-tuple-element.118), channel_id=1, source_target_pairs={{0,3},{1,2},{2,1},{3,0},{4,7},{5,6},{6,5},{7,4},{8,11},{9,10},{10,... | collective-permute-start | bytes 294920 | tf_op jit(solution)/shard_map/ppermute | solution.py:427
  287.6 7.0 %collective-permute-start.64 = (f32[200,128]{1,0:T(8,128)S(1)}, f32[200,128]{1,0:T(8,128)S(1)}, u32[]{:S(2)}, u32[]{:S(2)}) collective-permute-start(f32[200,128]{1,0:T(8,128)S(1)} %shard_map.129.mine_ref), channel_id=1, source_target_pairs={{0,4},{1,5},{2,6},{3,7},{4,0},{5,1},{6,2},{7,3},{8,12},{9,13},{10,... | collective-permute-start | bytes 307208 | tf_op jit(solution)/shard_map/ppermute | solution.py:475
  306.6 16.2 %all-to-all-start.5 = ((f32[8,16,768]{2,1,0:T(8,128)}), f32[8,16,768]{2,1,0:T(8,128)S(1)}, u32[]{:S(2)}, u32[]{:S(2)}) async-start(f32[8,16,768]{2,1,0:T(8,128)} %reshape.29), calls=%async_computation.5 | async-start | bytes 786432 | tf_op jit(solution)/shard_map/all_to_all | solution.py:414
  (24 other events, 89.0 us)

commit v2 on v1

--- a/solution.py
+++ b/solution.py
@@ -123,7 +123,7 @@
         marked = jnp.concatenate(marks, axis=1)
         table = jnp.dot(dict_ref[...], marked, preferred_element_type=jnp.float32)
         at_ref[q] = table.astype(jnp.bfloat16)
-        a_ref[q] = table.T.astype(jnp.bfloat16)
+        a_ref[q] = table.astype(jnp.bfloat16).T
 
     def turn(t, carry):
         for n in range(BUILD):
@@ -191,6 +191,34 @@
             r = (place ^ s) * rows + n if parts > 1 else n
             for i, piece in enumerate(packed_row(acc_ref, r)):
                 out_refs[s][pl.ds(n * PACK + i * QUART, QUART), :] = piece
+
+
+def flat_rows(acc_ref, f, out_ref):
+    lane = lane_ids(acc_ref.shape[0])
+    voxels = out_ref.shape[1] // DIRS
+    for g in range(voxels // 4):
+        first = f * (voxels // 2) + 2 * g
+        x = [acc_ref[:, i % 2 * HALF + i // 2 + first, :] for i in range(4)]
+        tiles = [
+            jnp.where(lane < 96, x[0], pltpu.roll(x[1], 96, 1)),
+            jnp.where(lane < 64, pltpu.roll(x[1], 96, 1), pltpu.roll(x[2], 64, 1)),
+            jnp.where(lane < 32, pltpu.roll(x[2], 64, 1), pltpu.roll(x[3], 32, 1)),
+        ]
+        out_ref[:, 4 * g * DIRS : 4 * (g + 1) * DIRS] = jnp.concatenate(tiles, axis=1)
+
+
+def flat_parts(acc_ref, out_refs):
+    parts = len(out_refs)
+    if parts == 1:
+        for f in range(out_refs[0].shape[0]):
+            flat_rows(acc_ref, f, out_refs[0].at[f])
+        return
+    me = lax.axis_index("fas")
+    place = lax.rem(me, parts)
+    for s in range(parts):
+        for other in range(2):
+            f = ((me // parts) ^ other) * parts + (place ^ s)
+            flat_rows(acc_ref, f, out_refs[s].at[other])
 
 
 def first_kernel(cap, meta_ref, w_ref, sig_ref, cp_ref, a_ref, *refs):
@@ -239,13 +267,13 @@
     acc_ref[...] = sig_ref[...]
     run_forward(cap, meta_ref, cp_ref, a_ref, table_ref, acc_ref)
     if last:
-        out_refs[0][...] = acc_ref[...]
+        flat_parts(acc_ref, out_refs)
     else:
         pack_rows(acc_ref, out_refs)
 
 
 def backward_kernel(cap, vox_rows, meta_ref, cp_ref, at_ref, *refs):
-    *res_refs, out_ref, split_ref, table_ref = refs
+    *res_refs, out_ref, split_ref, left_ref, right_ref = refs
     lane = lane_ids(QUART)
     parts = len(res_refs)
     rows = vox_rows // parts
@@ -260,8 +288,8 @@
         high = whole.astype(jnp.bfloat16)
         low = (whole - high.astype(jnp.float32)).astype(jnp.bfloat16)
         split_ref[r] = jnp.concatenate([high, low], axis=0)
-    table_ref[...] = jnp.zeros_like(table_ref)
-    left = lane_ids(1) < BF
+    left_ref[...] = jnp.zeros_like(left_ref)
+    right_ref[...] = jnp.zeros_like(right_ref)
     _, row_at, turns_at = plan_spots(cap)
 
     def turn(t, carry):
@@ -277,18 +305,19 @@
                 p = (t * UNROLL + n) * GROUP + 2 * pair
                 row = sums[n][:, pair * LANES : (pair + 1) * LANES]
                 c0 = pl.ds(meta_ref[0, p], 1)
-                table_ref[c0, :] = table_ref[c0, :] + jnp.where(left, row, 0.0)
+                left_ref[c0, :] = left_ref[c0, :] + row
                 c1 = pl.ds(meta_ref[0, p + 1], 1)
-                table_ref[c1, :] = table_ref[c1, :] + jnp.where(left, 0.0, row)
+                right_ref[c1, :] = right_ref[c1, :] + row
         return carry
 
     lax.fori_loop(0, meta_ref[0, turns_at], turn, 0)
     rows = out_ref.shape[0]
-    even = table_ref[pl.ds(0, rows, stride=2), :]
-    odd = table_ref[pl.ds(1, rows, stride=2), :]
-    even = even + pltpu.roll(even, BF, 1)
-    odd = odd + pltpu.roll(odd, BF, 1)
-    out_ref[...] = jnp.where(lane_ids(rows) < BF, even, odd)
+    left = lane_ids(rows) < BF
+    even = [ref[pl.ds(0, rows, stride=2), :] for ref in (left_ref, right_ref)]
+    odd = [ref[pl.ds(1, rows, stride=2), :] for ref in (left_ref, right_ref)]
+    even = even[0] + pltpu.roll(even[1], BF, 1)
+    odd = pltpu.roll(odd[0], BF, 1) + odd[1]
+    out_ref[...] = jnp.where(left, even, odd)
 
 
 def share_kernel(shares_ref, out_ref):
@@ -301,6 +330,15 @@
     for ref in in_refs[1:]:
         total = total + ref[...]
     out_ref[...] = total
+
+
+def split_kernel(*refs):
+    *in_refs, own_ref, send_ref = refs
+    for i, out_ref in enumerate((own_ref, send_ref)):
+        total = in_refs[0][i]
+        for ref in in_refs[1:]:
+            total = total + ref[i]
+        out_ref[...] = total
 
 
 def spread_kernel(mine_ref, other_ref, out_ref):
@@ -337,7 +375,8 @@
     run = pl.pallas_call(
         kernel,
         out_shape=tuple(
-            spaces[kind](shape, dtype) for shape, dtype, kind in outs
+            jax.ShapeDtypeStruct(shape, dtype) if kind == "n" else spaces[kind](shape, dtype)
+            for shape, dtype, kind in outs
         ),
         in_specs=[pl.BlockSpec(memory_space=spaces[kind]) for kind in ins],
         out_specs=tuple(pl.BlockSpec(memory_space=spaces[kind]) for _, _, kind in outs),
@@ -419,9 +458,12 @@
     across = [(i, (i + half) % n_fas) for i in range(n_fas)]
     half_share = image_rows // half
 
-    parts = half if half <= 4 else 1
+    parts = half if half in (2, 4) else 1
     share_out = ((half_share, LANES), f32, "v")
     image_outs = [share_out] * parts if parts > 1 else [image_out]
+
+    flat_count = 2 if parts > 1 else n_fas
+    flat_outs = [((flat_count, *signal.shape), f32, "v")] * parts
 
     def to_place(x, s):
         return lax.ppermute(x, "fas", [(i, i ^ s) for i in range(n_fas)])
@@ -454,7 +496,7 @@
             functools.partial(backward_kernel, cap, vox_rows),
             [flat_out],
             "mvv" + "v" * parts,
-            [pltpu.VMEM((vox_rows, 2 * BV, LANES), bf16), table],
+            [pltpu.VMEM((vox_rows, 2 * BV, LANES), bf16), table, table],
         )(meta, cp, at, *whole)
         bit = 1
         while bit < n_vox:
@@ -475,16 +517,22 @@
         other = lax.ppermute(mine, "fas", across)
         (sums,) = call(norm_kernel, [((n_vox * half, 1, LANES), f32, "v")], "vv")(mine, other)
         sums = swap(sums, ("vox", "fas"), both_axes)
-        outs = [((vox_rows, BV, LANES), f32, "v")] if last else image_outs
+        outs = flat_outs if last else image_outs
         weights, *partial = call(
             functools.partial(update_kernel, cap, n_vox, last),
-            [flat_out, *outs],
+            [flat_out if not last else (*flat_out[:2], "n"), *outs],
             "mvvvvvv",
             [table, acc],
         )(meta, sums, projected, weights, sig, cp, a)
-    final = partial[0].reshape(vox_rows, 2, n_fas, own, LANES)[..., :DIRS].transpose(2, 0, 3, 1, 4)
-    final = swap(final.reshape(n_fas, vox_rows, own * 2 * DIRS), "fas")
-    return (weights.reshape(-1), jnp.sum(final, axis=0))
+    if parts > 1:
+        shares = [partial[0]] + [to_place(partial[s], s) for s in range(1, parts)]
+        piece = (signal.shape, f32, "v")
+        own, send = call(split_kernel, [piece, piece], "v" * parts)(*shares)
+        other = lax.ppermute(send, "fas", across)
+        (final,) = call(sum_kernel, [(signal.shape, f32, "n")], "vv")(own, other)
+    else:
+        final = jnp.sum(swap(partial[0], "fas"), axis=0)
+    return (weights.reshape(-1), final)
 
 
 def solution(mesh):

time: 324 us -> 319 us (0.985)
  waiting for transfers between devices: 136 us -> 163 us
  Pallas kernels: 40.9 us -> 25.1 us
  starting transfers between devices: 97.7 us -> 86.4 us
    ppermute x45 -> x48, waiting for transfers between devices: 56.5 us -> 75 us  [to_place(): return lax.ppermute(x, 'fas', [(i, i ^ s) for i in range(n_fas)])]
    pallas_call x37 -> x39, Pallas kernels: 40.9 us -> 25.1 us  [placed(): run(*(pltpu.with_memory_space_constraint(x, spaces[kind]) if kind in 'vm'...]
    ppermute x5, starting transfers between devices: 18.5 us -> 6.54 us  [sum_all(): other = lax.ppermute(mine, 'fas', across)]
    all_to_all x1 -> x0, waiting for transfers between devices: 11 us -> none  [swap(): return lax.all_to_all(x, axis, 0, 0, axis_index_groups=groups)]
    ppermute x45 -> x48, starting transfers between devices: 54.2 us -> 65.2 us  [to_place(): return lax.ppermute(x, 'fas', [(i, i ^ s) for i in range(n_fas)])]
    ppermute x5, starting transfers between devices: 16.1 us -> 6.91 us  [local(): other = lax.ppermute(mine, 'fas', across)]
    ppermute x5, waiting for transfers between devices: 18.9 us -> 27.2 us  [sum_all(): other = lax.ppermute(mine, 'fas', across)]
    ppermute x5, waiting for transfers between devices: 19.4 us -> 27 us  [local(): other = lax.ppermute(mine, 'fas', across)]
  transfers between devices with their start and end apart: 66 -> 69, of which waited for: 62 -> 68; matrix products, arithmetic and copies ran while one was open for 0% -> 0% of each run, Pallas kernels for 0% -> 0%
where the time goes in v2:
time: 319 us; the launch traced here: 320 us
  waiting for transfers between devices  163 us (51%)
  starting transfers between devices  86.4 us (27%)
  blocking collectives  40.7 us (13%)
  Pallas kernels  25.1 us (8%)
    ppermute x48, waiting for transfers between devices, to_place(): return lax.ppermute(x, 'fas', [(i, i ^ s) for i in range(n_fas)])  75 us
    ppermute x48, starting transfers between devices, to_place(): return lax.ppermute(x, 'fas', [(i, i ^ s) for i in range(n_fas)])  65.2 us
    all_to_all x5, blocking collectives, swap(): return lax.all_to_all(x, axis, 0, 0, axis_index_groups=groups)  40.7 us
    ppermute x10, waiting for transfers between devices, local(): lax.ppermute(gradient, 'vox', [(i, i ^ bit) for i in range(n_vox)])  28.1 us
    ppermute x5, waiting for transfers between devices, sum_all(): other = lax.ppermute(mine, 'fas', across)  27.2 us
    ppermute x5, waiting for transfers between devices, local(): other = lax.ppermute(mine, 'fas', across)  27 us
    pallas_call x39, Pallas kernels, placed(): run(*(pltpu.with_memory_space_constraint(x, spaces[kind]) if kind in 'vm'...  25.1 us
    ppermute x10, starting transfers between devices, local(): lax.ppermute(gradient, 'vox', [(i, i ^ bit) for i in range(n_vox)])  7.66 us
  transfers between devices with their start and end apart: 69, of which 68 were waited for; matrix products, arithmetic and copies ran while one was open for 0% of the time, Pallas kernels for 0%

profile of v2, /device:TPU:0, one launch (start us, length us, event | category | flops | bytes accessed | tf_op | source)
XLA Modules:
  0.0 319.6 jit_solution(11609417560252996831)
XLA Ops:
  4.2 3.1 shard_map.95
  8.5 3.0 collective-permute-start
  11.5 4.4 %collective-permute-start.1 = (f32[192,128]{1,0:T(8,128)S(1)}, f32[192,128]{1,0:T(8,128)S(1)}, u32[]{:S(2)}, u32[]{:S(2)}) collective-permute-start(f32[192,128]{1,0:T(8,128)S(1)} %get-tuple-element.73), channel_id=1, source_target_pairs={{0,2},{1,3},{2,0},{3,1},{4,6},{5,7},{6,4},{7,5},{8,10},{9,11},{10,... | collective-permute-start | bytes 294920 | tf_op jit(solution)/shard_map/ppermute | solution.py:469
  15.9 3.5 %collective-permute-done.1.refs_2_ = f32[192,128]{1,0:T(8,128)S(1)} collective-permute-done((f32[192,128]{1,0:T(8,128)S(1)}, f32[192,128]{1,0:T(8,128)S(1)}, u32[]{:S(2)}, u32[]{:S(2)}) %collective-permute-start.1) | collective-permute-done | bytes 98336 | tf_op jit(solution)/shard_map/ppermute | solution.py:469
  21.4 2.6 collective-permute-start.3
  24.0 4.0 %collective-permute-done.3.refs_1_ = f32[192,128]{1,0:T(8,128)S(1)} collective-permute-done((f32[192,128]{1,0:T(8,128)S(1)}, f32[192,128]{1,0:T(8,128)S(1)}, u32[]{:S(2)}, u32[]{:S(2)}) %collective-permute-start.3) | collective-permute-done | bytes 98336 | tf_op jit(solution)/shard_map/ppermute | solution.py:480
  37.9 2.4 collective-permute-start.8
  40.4 3.8 %collective-permute-done.8 = f32[256,128]{1,0:T(8,128)S(1)} collective-permute-done((f32[256,128]{1,0:T(8,128)S(1)}, f32[256,128]{1,0:T(8,128)S(1)}, u32[]{:S(2)}, u32[]{:S(2)}) %collective-permute-start.8) | collective-permute-done | bytes 131104 | tf_op jit(solution)/shard_map/ppermute | solution.py:503
  45.3 2.7 collective-permute-start.10
  54.1 3.5 %collective-permute-start.12 = (f32[200,128]{1,0:T(8,128)S(1)}, f32[200,128]{1,0:T(8,128)S(1)}, u32[]{:S(2)}, u32[]{:S(2)}) collective-permute-start(f32[200,128]{1,0:T(8,128)S(1)} %shard_map.101.mine_ref), channel_id=1, source_target_pairs={{0,4},{1,5},{2,6},{3,7},{4,0},{5,1},{6,2},{7,3},{8,12},{9,13},{10,... | collective-permute-start | bytes 307208 | tf_op jit(solution)/shard_map/ppermute | solution.py:517
  57.6 3.7 %collective-permute-done.12.other_ref = f32[200,128]{1,0:T(8,128)S(1)} collective-permute-done((f32[200,128]{1,0:T(8,128)S(1)}, f32[200,128]{1,0:T(8,128)S(1)}, u32[]{:S(2)}, u32[]{:S(2)}) %collective-permute-start.12) | collective-permute-done | bytes 102432 | tf_op jit(solution)/shard_map/ppermute | solution.py:517
  61.4 8.6 %all_to_all.25.sums_ref = f32[16,1,128]{2,1,0:T(1,128)S(1)} all-to-all(f32[16,1,128]{2,1,0:T(1,128)S(1)} %shard_map.102), channel_id=1, replica_groups={{0,1,2,3,8,9,10,11,16,17,18,19,24,25,26,27},{4,5,6,7,12,13,14,15,20,21,..., dimensions={0} | all-to-all | bytes 16384 | tf_op jit(solution)/shard_map/all_to_all | solution.py:453
  77.6 2.5 collective-permute-done.15.refs_3_
  80.1 2.3 collective-permute-start.16
  82.4 4.9 %collective-permute-done.16.refs_1_ = f32[192,128]{1,0:T(8,128)S(1)} collective-permute-done((f32[192,128]{1,0:T(8,128)S(1)}, f32[192,128]{1,0:T(8,128)S(1)}, u32[]{:S(2)}, u32[]{:S(2)}) %collective-permute-start.16) | collective-permute-done | bytes 98336 | tf_op jit(solution)/shard_map/ppermute | solution.py:480
  88.1 2.8 collective-permute-start.19
  98.1 5.2 %collective-permute-done.21 = f32[256,128]{1,0:T(8,128)S(1)} collective-permute-done((f32[256,128]{1,0:T(8,128)S(1)}, f32[256,128]{1,0:T(8,128)S(1)}, u32[]{:S(2)}, u32[]{:S(2)}) %collective-permute-start.21) | collective-permute-done | bytes 131104 | tf_op jit(solution)/shard_map/ppermute | solution.py:503
  104.9 3.3 %collective-permute-start.23 = (f32[192,128]{1,0:T(8,128)S(1)}, f32[192,128]{1,0:T(8,128)S(1)}, u32[]{:S(2)}, u32[]{:S(2)}) collective-permute-start(f32[192,128]{1,0:T(8,128)S(1)} %get-tuple-element.89), channel_id=1, source_target_pairs={{0,2},{1,3},{2,0},{3,1},{4,6},{5,7},{6,4},{7,5},{8,10},{9,11},{10,... | collective-permute-start | bytes 294920 | tf_op jit(solution)/shard_map/ppermute | solution.py:469
  109.4 2.3 collective-permute-done.23.refs_2_
  115.5 4.8 %collective-permute-done.25.other_ref = f32[200,128]{1,0:T(8,128)S(1)} collective-permute-done((f32[200,128]{1,0:T(8,128)S(1)}, f32[200,128]{1,0:T(8,128)S(1)}, u32[]{:S(2)}, u32[]{:S(2)}) %collective-permute-start.25) | collective-permute-done | bytes 102432 | tf_op jit(solution)/shard_map/ppermute | solution.py:517
  120.4 8.0 %all_to_all.26.sums_ref = f32[16,1,128]{2,1,0:T(1,128)S(1)} all-to-all(f32[16,1,128]{2,1,0:T(1,128)S(1)} %shard_map.109), channel_id=1, replica_groups={{0,1,2,3,8,9,10,11,16,17,18,19,24,25,26,27},{4,5,6,7,12,13,14,15,20,21,..., dimensions={0} | all-to-all | bytes 16384 | tf_op jit(solution)/shard_map/all_to_all | solution.py:453
  136.1 2.5 collective-permute-done.28.refs_3_
  139.8 5.5 %collective-permute-done.29.refs_1_ = f32[192,128]{1,0:T(8,128)S(1)} collective-permute-done((f32[192,128]{1,0:T(8,128)S(1)}, f32[192,128]{1,0:T(8,128)S(1)}, u32[]{:S(2)}, u32[]{:S(2)}) %collective-permute-start.29) | collective-permute-done | bytes 98336 | tf_op jit(solution)/shard_map/ppermute | solution.py:480
  146.4 2.5 collective-permute-start.32
  156.7 4.1 %collective-permute-done.34 = f32[256,128]{1,0:T(8,128)S(1)} collective-permute-done((f32[256,128]{1,0:T(8,128)S(1)}, f32[256,128]{1,0:T(8,128)S(1)}, u32[]{:S(2)}, u32[]{:S(2)}) %collective-permute-start.34) | collective-permute-done | bytes 131104 | tf_op jit(solution)/shard_map/ppermute | solution.py:503
  163.1 3.0 collective-permute-start.36
  166.9 2.6 collective-permute-done.36.refs_2_
  172.8 5.6 %collective-permute-done.38.other_ref = f32[200,128]{1,0:T(8,128)S(1)} collective-permute-done((f32[200,128]{1,0:T(8,128)S(1)}, f32[200,128]{1,0:T(8,128)S(1)}, u32[]{:S(2)}, u32[]{:S(2)}) %collective-permute-start.38) | collective-permute-done | bytes 102432 | tf_op jit(solution)/shard_map/ppermute | solution.py:517
  178.5 8.0 %all_to_all.27.sums_ref = f32[16,1,128]{2,1,0:T(1,128)S(1)} all-to-all(f32[16,1,128]{2,1,0:T(1,128)S(1)} %shard_map.116), channel_id=1, replica_groups={{0,1,2,3,8,9,10,11,16,17,18,19,24,25,26,27},{4,5,6,7,12,13,14,15,20,21,..., dimensions={0} | all-to-all | bytes 16384 | tf_op jit(solution)/shard_map/all_to_all | solution.py:453
  194.0 2.5 collective-permute-done.41.refs_3_
  197.0 6.2 %collective-permute-done.42.refs_1_ = f32[192,128]{1,0:T(8,128)S(1)} collective-permute-done((f32[192,128]{1,0:T(8,128)S(1)}, f32[192,128]{1,0:T(8,128)S(1)}, u32[]{:S(2)}, u32[]{:S(2)}) %collective-permute-start.42) | collective-permute-done | bytes 98336 | tf_op jit(solution)/shard_map/ppermute | solution.py:480
  204.3 2.5 collective-permute-start.45
  214.6 4.1 %collective-permute-done.47 = f32[256,128]{1,0:T(8,128)S(1)} collective-permute-done((f32[256,128]{1,0:T(8,128)S(1)}, f32[256,128]{1,0:T(8,128)S(1)}, u32[]{:S(2)}, u32[]{:S(2)}) %collective-permute-start.47) | collective-permute-done | bytes 131104 | tf_op jit(solution)/shard_map/ppermute | solution.py:503
  221.1 3.0 collective-permute-start.49
  224.8 2.6 collective-permute-done.49.refs_2_
  227.4 2.2 collective-permute-done.50.refs_3_
  230.0 6.3 %collective-permute-done.51.other_ref = f32[200,128]{1,0:T(8,128)S(1)} collective-permute-done((f32[200,128]{1,0:T(8,128)S(1)}, f32[200,128]{1,0:T(8,128)S(1)}, u32[]{:S(2)}, u32[]{:S(2)}) %collective-permute-start.51) | collective-permute-done | bytes 102432 | tf_op jit(solution)/shard_map/ppermute | solution.py:517
  236.5 8.0 %all_to_all.28.sums_ref = f32[16,1,128]{2,1,0:T(1,128)S(1)} all-to-all(f32[16,1,128]{2,1,0:T(1,128)S(1)} %shard_map.123), channel_id=1, replica_groups={{0,1,2,3,8,9,10,11,16,17,18,19,24,25,26,27},{4,5,6,7,12,13,14,15,20,21,..., dimensions={0} | all-to-all | bytes 16384 | tf_op jit(solution)/shard_map/all_to_all | solution.py:453
  252.0 2.5 collective-permute-done.54.refs_3_
  254.6 6.6 %collective-permute-done.55.refs_1_ = f32[192,128]{1,0:T(8,128)S(1)} collective-permute-done((f32[192,128]{1,0:T(8,128)S(1)}, f32[192,128]{1,0:T(8,128)S(1)}, u32[]{:S(2)}, u32[]{:S(2)}) %collective-permute-start.55) | collective-permute-done | bytes 98336 | tf_op jit(solution)/shard_map/ppermute | solution.py:480
  262.2 2.5 collective-permute-start.58
  272.5 4.1 %collective-permute-done.60 = f32[256,128]{1,0:T(8,128)S(1)} collective-permute-done((f32[256,128]{1,0:T(8,128)S(1)}, f32[256,128]{1,0:T(8,128)S(1)}, u32[]{:S(2)}, u32[]{:S(2)}) %collective-permute-start.60) | collective-permute-done | bytes 131104 | tf_op jit(solution)/shard_map/ppermute | solution.py:503
  279.2 3.0 collective-permute-start.62
  282.9 2.6 collective-permute-done.62.refs_2_
  288.0 6.5 %collective-permute-done.64.other_ref = f32[200,128]{1,0:T(8,128)S(1)} collective-permute-done((f32[200,128]{1,0:T(8,128)S(1)}, f32[200,128]{1,0:T(8,128)S(1)}, u32[]{:S(2)}, u32[]{:S(2)}) %collective-permute-start.64) | collective-permute-done | bytes 102432 | tf_op jit(solution)/shard_map/ppermute | solution.py:517
  294.6 8.0 %all_to_all.29.sums_ref = f32[16,1,128]{2,1,0:T(1,128)S(1)} all-to-all(f32[16,1,128]{2,1,0:T(1,128)S(1)} %shard_map.130), channel_id=1, replica_groups={{0,1,2,3,8,9,10,11,16,17,18,19,24,25,26,27},{4,5,6,7,12,13,14,15,20,21,..., dimensions={0} | all-to-all | bytes 16384 | tf_op jit(solution)/shard_map/all_to_all | solution.py:453
  310.8 2.5 collective-permute-done.67.refs_3_
  313.5 5.5 %collective-permute-done.68.refs_1_ = f32[16,768]{1,0:T(8,128)S(1)} collective-permute-done((f32[16,768]{1,0:T(8,128)S(1)}, f32[16,768]{1,0:T(8,128)S(1)}, u32[]{:S(2)}, u32[]{:S(2)}) %collective-permute-start.68) | collective-permute-done | bytes 49184 | tf_op jit(solution)/shard_map/ppermute | solution.py:531
  (168 shorter events, 120.9 us)
Async XLA Ops:
  8.5 7.4 %collective-permute-start = (f32[192,128]{1,0:T(8,128)S(1)}, f32[192,128]{1,0:T(8,128)S(1)}, u32[]{:S(2)}, u32[]{:S(2)}) collective-permute-start(f32[192,128]{1,0:T(8,128)S(1)} %get-tuple-element.72), channel_id=1, source_target_pairs={{0,1},{1,0},{2,3},{3,2},{4,5},{5,4},{6,7},{7,6},{8,9},{9,8},{10,11... | collective-permute-start | bytes 294920 | tf_op jit(solution)/shard_map/ppermute | solution.py:469
  11.5 7.9 %collective-permute-start.1 = (f32[192,128]{1,0:T(8,128)S(1)}, f32[192,128]{1,0:T(8,128)S(1)}, u32[]{:S(2)}, u32[]{:S(2)}) collective-permute-start(f32[192,128]{1,0:T(8,128)S(1)} %get-tuple-element.73), channel_id=1, source_target_pairs={{0,2},{1,3},{2,0},{3,1},{4,6},{5,7},{6,4},{7,5},{8,10},{9,11},{10,... | collective-permute-start | bytes 294920 | tf_op jit(solution)/shard_map/ppermute | solution.py:469
  15.8 5.5 %collective-permute-start.2 = (f32[192,128]{1,0:T(8,128)S(1)}, f32[192,128]{1,0:T(8,128)S(1)}, u32[]{:S(2)}, u32[]{:S(2)}) collective-permute-start(f32[192,128]{1,0:T(8,128)S(1)} %get-tuple-element.74), channel_id=1, source_target_pairs={{0,3},{1,2},{2,1},{3,0},{4,7},{5,6},{6,5},{7,4},{8,11},{9,10},{10,... | collective-permute-start | bytes 294920 | tf_op jit(solution)/shard_map/ppermute | solution.py:469
  21.4 6.6 %collective-permute-start.3 = (f32[192,128]{1,0:T(8,128)S(1)}, f32[192,128]{1,0:T(8,128)S(1)}, u32[]{:S(2)}, u32[]{:S(2)}) collective-permute-start(f32[192,128]{1,0:T(8,128)S(1)} %shard_map.97.refs_0_), channel_id=1, source_target_pairs={{0,4},{1,5},{2,6},{3,7},{4,0},{5,1},{6,2},{7,3},{8,12},{9,13},{10,... | collective-permute-start | bytes 294920 | tf_op jit(solution)/shard_map/ppermute | solution.py:480
  29.5 5.7 %collective-permute-start.6 = (f32[192,128]{1,0:T(8,128)S(1)}, f32[192,128]{1,0:T(8,128)S(1)}, u32[]{:S(2)}, u32[]{:S(2)}) collective-permute-start(f32[192,128]{1,0:T(8,128)S(1)} %shard_map.98.refs_0_), channel_id=1, source_target_pairs={{0,3},{1,2},{2,1},{3,0},{4,7},{5,6},{6,5},{7,4},{8,11},{9,10},{10,... | collective-permute-start | bytes 294920 | tf_op jit(solution)/shard_map/ppermute | solution.py:469
  37.9 6.3 %collective-permute-start.8 = (f32[256,128]{1,0:T(8,128)S(1)}, f32[256,128]{1,0:T(8,128)S(1)}, u32[]{:S(2)}, u32[]{:S(2)}) collective-permute-start(f32[256,128]{1,0:T(8,128)S(1)} %add.40), channel_id=1, source_target_pairs={{0,16},{8,24},{16,0},{24,8},{1,17},{9,25},{17,1},{25,9},{2,18},{10... | collective-permute-start | bytes 393224 | tf_op jit(solution)/shard_map/ppermute | solution.py:503
  45.3 6.3 %collective-permute-start.10 = (f32[192,128]{1,0:T(8,128)S(1)}, f32[192,128]{1,0:T(8,128)S(1)}, u32[]{:S(2)}, u32[]{:S(2)}) collective-permute-start(f32[192,128]{1,0:T(8,128)S(1)} %get-tuple-element.78), channel_id=1, source_target_pairs={{0,2},{1,3},{2,0},{3,1},{4,6},{5,7},{6,4},{7,5},{8,10},{9,11},{10,... | collective-permute-start | bytes 294920 | tf_op jit(solution)/shard_map/ppermute | solution.py:469
  48.1 5.6 %collective-permute-start.11 = (f32[192,128]{1,0:T(8,128)S(1)}, f32[192,128]{1,0:T(8,128)S(1)}, u32[]{:S(2)}, u32[]{:S(2)}) collective-permute-start(f32[192,128]{1,0:T(8,128)S(1)} %get-tuple-element.79), channel_id=1, source_target_pairs={{0,3},{1,2},{2,1},{3,0},{4,7},{5,6},{6,5},{7,4},{8,11},{9,10},{10,... | collective-permute-start | bytes 294920 | tf_op jit(solution)/shard_map/ppermute | solution.py:469
  48.4 5.7 %collective-permute-start.9 = (f32[192,128]{1,0:T(8,128)S(1)}, f32[192,128]{1,0:T(8,128)S(1)}, u32[]{:S(2)}, u32[]{:S(2)}) collective-permute-start(f32[192,128]{1,0:T(8,128)S(1)} %get-tuple-element.77), channel_id=1, source_target_pairs={{0,1},{1,0},{2,3},{3,2},{4,5},{5,4},{6,7},{7,6},{8,9},{9,8},{10,11... | collective-permute-start | bytes 294920 | tf_op jit(solution)/shard_map/ppermute | solution.py:469
  54.1 7.2 %collective-permute-start.12 = (f32[200,128]{1,0:T(8,128)S(1)}, f32[200,128]{1,0:T(8,128)S(1)}, u32[]{:S(2)}, u32[]{:S(2)}) collective-permute-start(f32[200,128]{1,0:T(8,128)S(1)} %shard_map.101.mine_ref), channel_id=1, source_target_pairs={{0,4},{1,5},{2,6},{3,7},{4,0},{5,1},{6,2},{7,3},{8,12},{9,13},{10,... | collective-permute-start | bytes 307208 | tf_op jit(solution)/shard_map/ppermute | solution.py:517
  72.0 5.6 %collective-permute-start.14 = (f32[192,128]{1,0:T(8,128)S(1)}, f32[192,128]{1,0:T(8,128)S(1)}, u32[]{:S(2)}, u32[]{:S(2)}) collective-permute-start(f32[192,128]{1,0:T(8,128)S(1)} %get-tuple-element.83), channel_id=1, source_target_pairs={{0,2},{1,3},{2,0},{3,1},{4,6},{5,7},{6,4},{7,5},{8,10},{9,11},{10,... | collective-permute-start | bytes 294920 | tf_op jit(solution)/shard_map/ppermute | solution.py:469
  73.4 6.7 %collective-permute-start.15 = (f32[192,128]{1,0:T(8,128)S(1)}, f32[192,128]{1,0:T(8,128)S(1)}, u32[]{:S(2)}, u32[]{:S(2)}) collective-permute-start(f32[192,128]{1,0:T(8,128)S(1)} %get-tuple-element.84), channel_id=1, source_target_pairs={{0,3},{1,2},{2,1},{3,0},{4,7},{5,6},{6,5},{7,4},{8,11},{9,10},{10,... | collective-permute-start | bytes 294920 | tf_op jit(solution)/shard_map/ppermute | solution.py:469
  80.1 7.2 %collective-permute-start.16 = (f32[192,128]{1,0:T(8,128)S(1)}, f32[192,128]{1,0:T(8,128)S(1)}, u32[]{:S(2)}, u32[]{:S(2)}) collective-permute-start(f32[192,128]{1,0:T(8,128)S(1)} %shard_map.104.refs_0_), channel_id=1, source_target_pairs={{0,4},{1,5},{2,6},{3,7},{4,0},{5,1},{6,2},{7,3},{8,12},{9,13},{10,... | collective-permute-start | bytes 294920 | tf_op jit(solution)/shard_map/ppermute | solution.py:480
  88.1 6.9 %collective-permute-start.19 = (f32[192,128]{1,0:T(8,128)S(1)}, f32[192,128]{1,0:T(8,128)S(1)}, u32[]{:S(2)}, u32[]{:S(2)}) collective-permute-start(f32[192,128]{1,0:T(8,128)S(1)} %shard_map.105.refs_0_), channel_id=1, source_target_pairs={{0,3},{1,2},{2,1},{3,0},{4,7},{5,6},{6,5},{7,4},{8,11},{9,10},{10,... | collective-permute-start | bytes 294920 | tf_op jit(solution)/shard_map/ppermute | solution.py:469
  97.7 5.6 %collective-permute-start.21 = (f32[256,128]{1,0:T(8,128)S(1)}, f32[256,128]{1,0:T(8,128)S(1)}, u32[]{:S(2)}, u32[]{:S(2)}) collective-permute-start(f32[256,128]{1,0:T(8,128)S(1)} %add.42), channel_id=1, source_target_pairs={{0,16},{8,24},{16,0},{24,8},{1,17},{9,25},{17,1},{25,9},{2,18},{10... | collective-permute-start | bytes 393224 | tf_op jit(solution)/shard_map/ppermute | solution.py:503
  104.9 6.8 %collective-permute-start.23 = (f32[192,128]{1,0:T(8,128)S(1)}, f32[192,128]{1,0:T(8,128)S(1)}, u32[]{:S(2)}, u32[]{:S(2)}) collective-permute-start(f32[192,128]{1,0:T(8,128)S(1)} %get-tuple-element.89), channel_id=1, source_target_pairs={{0,2},{1,3},{2,0},{3,1},{4,6},{5,7},{6,4},{7,5},{8,10},{9,11},{10,... | collective-permute-start | bytes 294920 | tf_op jit(solution)/shard_map/ppermute | solution.py:469
  108.2 5.5 %collective-permute-start.24 = (f32[192,128]{1,0:T(8,128)S(1)}, f32[192,128]{1,0:T(8,128)S(1)}, u32[]{:S(2)}, u32[]{:S(2)}) collective-permute-start(f32[192,128]{1,0:T(8,128)S(1)} %get-tuple-element.90), channel_id=1, source_target_pairs={{0,3},{1,2},{2,1},{3,0},{4,7},{5,6},{6,5},{7,4},{8,11},{9,10},{10,... | collective-permute-start | bytes 294920 | tf_op jit(solution)/shard_map/ppermute | solution.py:469
  113.8 6.5 %collective-permute-start.25 = (f32[200,128]{1,0:T(8,128)S(1)}, f32[200,128]{1,0:T(8,128)S(1)}, u32[]{:S(2)}, u32[]{:S(2)}) collective-permute-start(f32[200,128]{1,0:T(8,128)S(1)} %shard_map.108.mine_ref), channel_id=1, source_target_pairs={{0,4},{1,5},{2,6},{3,7},{4,0},{5,1},{6,2},{7,3},{8,12},{9,13},{10,... | collective-permute-start | bytes 307208 | tf_op jit(solution)/shard_map/ppermute | solution.py:517
  130.5 5.6 %collective-permute-start.27 = (f32[192,128]{1,0:T(8,128)S(1)}, f32[192,128]{1,0:T(8,128)S(1)}, u32[]{:S(2)}, u32[]{:S(2)}) collective-permute-start(f32[192,128]{1,0:T(8,128)S(1)} %get-tuple-element.94), channel_id=1, source_target_pairs={{0,2},{1,3},{2,0},{3,1},{4,6},{5,7},{6,4},{7,5},{8,10},{9,11},{10,... | collective-permute-start | bytes 294920 | tf_op jit(solution)/shard_map/ppermute | solution.py:469
  131.9 6.7 %collective-permute-start.28 = (f32[192,128]{1,0:T(8,128)S(1)}, f32[192,128]{1,0:T(8,128)S(1)}, u32[]{:S(2)}, u32[]{:S(2)}) collective-permute-start(f32[192,128]{1,0:T(8,128)S(1)} %get-tuple-element.95), channel_id=1, source_target_pairs={{0,3},{1,2},{2,1},{3,0},{4,7},{5,6},{6,5},{7,4},{8,11},{9,10},{10,... | collective-permute-start | bytes 294920 | tf_op jit(solution)/shard_map/ppermute | solution.py:469
  138.6 6.6 %collective-permute-start.29 = (f32[192,128]{1,0:T(8,128)S(1)}, f32[192,128]{1,0:T(8,128)S(1)}, u32[]{:S(2)}, u32[]{:S(2)}) collective-permute-start(f32[192,128]{1,0:T(8,128)S(1)} %shard_map.111.refs_0_), channel_id=1, source_target_pairs={{0,4},{1,5},{2,6},{3,7},{4,0},{5,1},{6,2},{7,3},{8,12},{9,13},{10,... | collective-permute-start | bytes 294920 | tf_op jit(solution)/shard_map/ppermute | solution.py:480
  145.3 5.6 %collective-permute-start.30 = (f32[192,128]{1,0:T(8,128)S(1)}, f32[192,128]{1,0:T(8,128)S(1)}, u32[]{:S(2)}, u32[]{:S(2)}) collective-permute-start(f32[192,128]{1,0:T(8,128)S(1)} %shard_map.112.refs_0_), channel_id=1, source_target_pairs={{0,1},{1,0},{2,3},{3,2},{4,5},{5,4},{6,7},{7,6},{8,9},{9,8},{10,11... | collective-permute-start | bytes 294920 | tf_op jit(solution)/shard_map/ppermute | solution.py:469
  146.4 6.1 %collective-permute-start.32 = (f32[192,128]{1,0:T(8,128)S(1)}, f32[192,128]{1,0:T(8,128)S(1)}, u32[]{:S(2)}, u32[]{:S(2)}) collective-permute-start(f32[192,128]{1,0:T(8,128)S(1)} %shard_map.112.refs_0_), channel_id=1, source_target_pairs={{0,3},{1,2},{2,1},{3,0},{4,7},{5,6},{6,5},{7,4},{8,11},{9,10},{10,... | collective-permute-start | bytes 294920 | tf_op jit(solution)/shard_map/ppermute | solution.py:469
  155.2 5.6 %collective-permute-start.34 = (f32[256,128]{1,0:T(8,128)S(1)}, f32[256,128]{1,0:T(8,128)S(1)}, u32[]{:S(2)}, u32[]{:S(2)}) collective-permute-start(f32[256,128]{1,0:T(8,128)S(1)} %add.44), channel_id=1, source_target_pairs={{0,16},{8,24},{16,0},{24,8},{1,17},{9,25},{17,1},{25,9},{2,18},{10... | collective-permute-start | bytes 393224 | tf_op jit(solution)/shard_map/ppermute | solution.py:503
  163.1 6.4 %collective-permute-start.36 = (f32[192,128]{1,0:T(8,128)S(1)}, f32[192,128]{1,0:T(8,128)S(1)}, u32[]{:S(2)}, u32[]{:S(2)}) collective-permute-start(f32[192,128]{1,0:T(8,128)S(1)} %get-tuple-element.100), channel_id=1, source_target_pairs={{0,2},{1,3},{2,0},{3,1},{4,6},{5,7},{6,4},{7,5},{8,10},{9,11},{10,... | collective-permute-start | bytes 294920 | tf_op jit(solution)/shard_map/ppermute | solution.py:469
  166.2 5.5 %collective-permute-start.37 = (f32[192,128]{1,0:T(8,128)S(1)}, f32[192,128]{1,0:T(8,128)S(1)}, u32[]{:S(2)}, u32[]{:S(2)}) collective-permute-start(f32[192,128]{1,0:T(8,128)S(1)} %get-tuple-element.101), channel_id=1, source_target_pairs={{0,3},{1,2},{2,1},{3,0},{4,7},{5,6},{6,5},{7,4},{8,11},{9,10},{10,... | collective-permute-start | bytes 294920 | tf_op jit(solution)/shard_map/ppermute | solution.py:469
  171.7 6.7 %collective-permute-start.38 = (f32[200,128]{1,0:T(8,128)S(1)}, f32[200,128]{1,0:T(8,128)S(1)}, u32[]{:S(2)}, u32[]{:S(2)}) collective-permute-start(f32[200,128]{1,0:T(8,128)S(1)} %shard_map.115.mine_ref), channel_id=1, source_target_pairs={{0,4},{1,5},{2,6},{3,7},{4,0},{5,1},{6,2},{7,3},{8,12},{9,13},{10,... | collective-permute-start | bytes 307208 | tf_op jit(solution)/shard_map/ppermute | solution.py:517
  188.4 5.6 %collective-permute-start.40 = (f32[192,128]{1,0:T(8,128)S(1)}, f32[192,128]{1,0:T(8,128)S(1)}, u32[]{:S(2)}, u32[]{:S(2)}) collective-permute-start(f32[192,128]{1,0:T(8,128)S(1)} %get-tuple-element.105), channel_id=1, source_target_pairs={{0,2},{1,3},{2,0},{3,1},{4,6},{5,7},{6,4},{7,5},{8,10},{9,11},{10,... | collective-permute-start | bytes 294920 | tf_op jit(solution)/shard_map/ppermute | solution.py:469
  189.9 6.7 %collective-permute-start.41 = (f32[192,128]{1,0:T(8,128)S(1)}, f32[192,128]{1,0:T(8,128)S(1)}, u32[]{:S(2)}, u32[]{:S(2)}) collective-permute-start(f32[192,128]{1,0:T(8,128)S(1)} %get-tuple-element.106), channel_id=1, source_target_pairs={{0,3},{1,2},{2,1},{3,0},{4,7},{5,6},{6,5},{7,4},{8,11},{9,10},{10,... | collective-permute-start | bytes 294920 | tf_op jit(solution)/shard_map/ppermute | solution.py:469
  196.6 6.6 %collective-permute-start.42 = (f32[192,128]{1,0:T(8,128)S(1)}, f32[192,128]{1,0:T(8,128)S(1)}, u32[]{:S(2)}, u32[]{:S(2)}) collective-permute-start(f32[192,128]{1,0:T(8,128)S(1)} %shard_map.118.refs_0_), channel_id=1, source_target_pairs={{0,4},{1,5},{2,6},{3,7},{4,0},{5,1},{6,2},{7,3},{8,12},{9,13},{10,... | collective-permute-start | bytes 294920 | tf_op jit(solution)/shard_map/ppermute | solution.py:480
  203.2 5.7 %collective-permute-start.43 = (f32[192,128]{1,0:T(8,128)S(1)}, f32[192,128]{1,0:T(8,128)S(1)}, u32[]{:S(2)}, u32[]{:S(2)}) collective-permute-start(f32[192,128]{1,0:T(8,128)S(1)} %shard_map.119.refs_0_), channel_id=1, source_target_pairs={{0,1},{1,0},{2,3},{3,2},{4,5},{5,4},{6,7},{7,6},{8,9},{9,8},{10,11... | collective-permute-start | bytes 294920 | tf_op jit(solution)/shard_map/ppermute | solution.py:469
  204.3 6.1 %collective-permute-start.45 = (f32[192,128]{1,0:T(8,128)S(1)}, f32[192,128]{1,0:T(8,128)S(1)}, u32[]{:S(2)}, u32[]{:S(2)}) collective-permute-start(f32[192,128]{1,0:T(8,128)S(1)} %shard_map.119.refs_0_), channel_id=1, source_target_pairs={{0,3},{1,2},{2,1},{3,0},{4,7},{5,6},{6,5},{7,4},{8,11},{9,10},{10,... | collective-permute-start | bytes 294920 | tf_op jit(solution)/shard_map/ppermute | solution.py:469
  213.1 5.6 %collective-permute-start.47 = (f32[256,128]{1,0:T(8,128)S(1)}, f32[256,128]{1,0:T(8,128)S(1)}, u32[]{:S(2)}, u32[]{:S(2)}) collective-permute-start(f32[256,128]{1,0:T(8,128)S(1)} %add.46), channel_id=1, source_target_pairs={{0,16},{8,24},{16,0},{24,8},{1,17},{9,25},{17,1},{25,9},{2,18},{10... | collective-permute-start | bytes 393224 | tf_op jit(solution)/shard_map/ppermute | solution.py:503
  221.1 6.3 %collective-permute-start.49 = (f32[192,128]{1,0:T(8,128)S(1)}, f32[192,128]{1,0:T(8,128)S(1)}, u32[]{:S(2)}, u32[]{:S(2)}) collective-permute-start(f32[192,128]{1,0:T(8,128)S(1)} %get-tuple-element.111), channel_id=1, source_target_pairs={{0,2},{1,3},{2,0},{3,1},{4,6},{5,7},{6,4},{7,5},{8,10},{9,11},{10,... | collective-permute-start | bytes 294920 | tf_op jit(solution)/shard_map/ppermute | solution.py:469
  224.1 5.5 %collective-permute-start.50 = (f32[192,128]{1,0:T(8,128)S(1)}, f32[192,128]{1,0:T(8,128)S(1)}, u32[]{:S(2)}, u32[]{:S(2)}) collective-permute-start(f32[192,128]{1,0:T(8,128)S(1)} %get-tuple-element.112), channel_id=1, source_target_pairs={{0,3},{1,2},{2,1},{3,0},{4,7},{5,6},{6,5},{7,4},{8,11},{9,10},{10,... | collective-permute-start | bytes 294920 | tf_op jit(solution)/shard_map/ppermute | solution.py:469
  229.6 6.7 %collective-permute-start.51 = (f32[200,128]{1,0:T(8,128)S(1)}, f32[200,128]{1,0:T(8,128)S(1)}, u32[]{:S(2)}, u32[]{:S(2)}) collective-permute-start(f32[200,128]{1,0:T(8,128)S(1)} %shard_map.122.mine_ref), channel_id=1, source_target_pairs={{0,4},{1,5},{2,6},{3,7},{4,0},{5,1},{6,2},{7,3},{8,12},{9,13},{10,... | collective-permute-start | bytes 307208 | tf_op jit(solution)/shard_map/ppermute | solution.py:517
  246.4 5.6 %collective-permute-start.53 = (f32[192,128]{1,0:T(8,128)S(1)}, f32[192,128]{1,0:T(8,128)S(1)}, u32[]{:S(2)}, u32[]{:S(2)}) collective-permute-start(f32[192,128]{1,0:T(8,128)S(1)} %get-tuple-element.116), channel_id=1, source_target_pairs={{0,2},{1,3},{2,0},{3,1},{4,6},{5,7},{6,4},{7,5},{8,10},{9,11},{10,... | collective-permute-start | bytes 294920 | tf_op jit(solution)/shard_map/ppermute | solution.py:469
  247.8 6.7 %collective-permute-start.54 = (f32[192,128]{1,0:T(8,128)S(1)}, f32[192,128]{1,0:T(8,128)S(1)}, u32[]{:S(2)}, u32[]{:S(2)}) collective-permute-start(f32[192,128]{1,0:T(8,128)S(1)} %get-tuple-element.117), channel_id=1, source_target_pairs={{0,3},{1,2},{2,1},{3,0},{4,7},{5,6},{6,5},{7,4},{8,11},{9,10},{10,... | collective-permute-start | bytes 294920 | tf_op jit(solution)/shard_map/ppermute | solution.py:469
  254.5 6.6 %collective-permute-start.55 = (f32[192,128]{1,0:T(8,128)S(1)}, f32[192,128]{1,0:T(8,128)S(1)}, u32[]{:S(2)}, u32[]{:S(2)}) collective-permute-start(f32[192,128]{1,0:T(8,128)S(1)} %shard_map.125.refs_0_), channel_id=1, source_target_pairs={{0,4},{1,5},{2,6},{3,7},{4,0},{5,1},{6,2},{7,3},{8,12},{9,13},{10,... | collective-permute-start | bytes 294920 | tf_op jit(solution)/shard_map/ppermute | solution.py:480
  261.2 5.7 %collective-permute-start.56 = (f32[192,128]{1,0:T(8,128)S(1)}, f32[192,128]{1,0:T(8,128)S(1)}, u32[]{:S(2)}, u32[]{:S(2)}) collective-permute-start(f32[192,128]{1,0:T(8,128)S(1)} %shard_map.126.refs_0_), channel_id=1, source_target_pairs={{0,1},{1,0},{2,3},{3,2},{4,5},{5,4},{6,7},{7,6},{8,9},{9,8},{10,11... | collective-permute-start | bytes 294920 | tf_op jit(solution)/shard_map/ppermute | solution.py:469
  262.2 6.1 %collective-permute-start.58 = (f32[192,128]{1,0:T(8,128)S(1)}, f32[192,128]{1,0:T(8,128)S(1)}, u32[]{:S(2)}, u32[]{:S(2)}) collective-permute-start(f32[192,128]{1,0:T(8,128)S(1)} %shard_map.126.refs_0_), channel_id=1, source_target_pairs={{0,3},{1,2},{2,1},{3,0},{4,7},{5,6},{6,5},{7,4},{8,11},{9,10},{10,... | collective-permute-start | bytes 294920 | tf_op jit(solution)/shard_map/ppermute | solution.py:469
  271.0 5.6 %collective-permute-start.60 = (f32[256,128]{1,0:T(8,128)S(1)}, f32[256,128]{1,0:T(8,128)S(1)}, u32[]{:S(2)}, u32[]{:S(2)}) collective-permute-start(f32[256,128]{1,0:T(8,128)S(1)} %add.48), channel_id=1, source_target_pairs={{0,16},{8,24},{16,0},{24,8},{1,17},{9,25},{17,1},{25,9},{2,18},{10... | collective-permute-start | bytes 393224 | tf_op jit(solution)/shard_map/ppermute | solution.py:503
  279.2 6.4 %collective-permute-start.62 = (f32[192,128]{1,0:T(8,128)S(1)}, f32[192,128]{1,0:T(8,128)S(1)}, u32[]{:S(2)}, u32[]{:S(2)}) collective-permute-start(f32[192,128]{1,0:T(8,128)S(1)} %get-tuple-element.122), channel_id=1, source_target_pairs={{0,2},{1,3},{2,0},{3,1},{4,6},{5,7},{6,4},{7,5},{8,10},{9,11},{10,... | collective-permute-start | bytes 294920 | tf_op jit(solution)/shard_map/ppermute | solution.py:469
  282.2 5.5 %collective-permute-start.63 = (f32[192,128]{1,0:T(8,128)S(1)}, f32[192,128]{1,0:T(8,128)S(1)}, u32[]{:S(2)}, u32[]{:S(2)}) collective-permute-start(f32[192,128]{1,0:T(8,128)S(1)} %get-tuple-element.123), channel_id=1, source_target_pairs={{0,3},{1,2},{2,1},{3,0},{4,7},{5,6},{6,5},{7,4},{8,11},{9,10},{10,... | collective-permute-start | bytes 294920 | tf_op jit(solution)/shard_map/ppermute | solution.py:469
  287.8 6.7 %collective-permute-start.64 = (f32[200,128]{1,0:T(8,128)S(1)}, f32[200,128]{1,0:T(8,128)S(1)}, u32[]{:S(2)}, u32[]{:S(2)}) collective-permute-start(f32[200,128]{1,0:T(8,128)S(1)} %shard_map.129.mine_ref), channel_id=1, source_target_pairs={{0,4},{1,5},{2,6},{3,7},{4,0},{5,1},{6,2},{7,3},{8,12},{9,13},{10,... | collective-permute-start | bytes 307208 | tf_op jit(solution)/shard_map/ppermute | solution.py:517
  305.2 5.6 %collective-permute-start.66 = (f32[2,16,768]{2,1,0:T(8,128)S(1)}, f32[2,16,768]{2,1,0:T(8,128)S(1)}, u32[]{:S(2)}, u32[]{:S(2)}) collective-permute-start(f32[2,16,768]{2,1,0:T(8,128)S(1)} %get-tuple-element.128), channel_id=1, source_target_pairs={{0,2},{1,3},{2,0},{3,1},{4,6},{5,7},{6,4},{7,5},{8,10},{9,11},{10,... | collective-permute-start | bytes 294920 | tf_op jit(solution)/shard_map/ppermute | solution.py:469
  306.7 6.7 %collective-permute-start.67 = (f32[2,16,768]{2,1,0:T(8,128)S(1)}, f32[2,16,768]{2,1,0:T(8,128)S(1)}, u32[]{:S(2)}, u32[]{:S(2)}) collective-permute-start(f32[2,16,768]{2,1,0:T(8,128)S(1)} %get-tuple-element.129), channel_id=1, source_target_pairs={{0,3},{1,2},{2,1},{3,0},{4,7},{5,6},{6,5},{7,4},{8,11},{9,10},{10,... | collective-permute-start | bytes 294920 | tf_op jit(solution)/shard_map/ppermute | solution.py:469
  313.4 5.6 %collective-permute-start.68 = (f32[16,768]{1,0:T(8,128)S(1)}, f32[16,768]{1,0:T(8,128)S(1)}, u32[]{:S(2)}, u32[]{:S(2)}) collective-permute-start(f32[16,768]{1,0:T(8,128)S(1)} %get-tuple-element.131), channel_id=1, source_target_pairs={{0,4},{1,5},{2,6},{3,7},{4,0},{5,1},{6,2},{7,3},{8,12},{9,13},{10,... | collective-permute-start | bytes 147464 | tf_op jit(solution)/shard_map/ppermute | solution.py:531
  (27 other events, 106.0 us)

commit v3 on v2

--- a/solution.py
+++ b/solution.py
@@ -18,6 +18,7 @@
 PACK = BV * DIRS // LANES
 HALF = BV // 2
 QUART = BV // 4
+TURN = (0, 3, 1, 2)
 VMEM_LIMIT = 16 * 1024 * 1024
 
 
@@ -188,7 +189,7 @@
     place = lax.rem(lax.axis_index("fas"), parts) if parts > 1 else 0
     for s in range(parts):
         for n in range(rows):
-            r = (place ^ s) * rows + n if parts > 1 else n
+            r = (place ^ TURN[s]) * rows + n if parts > 1 else n
             for i, piece in enumerate(packed_row(acc_ref, r)):
                 out_refs[s][pl.ds(n * PACK + i * QUART, QUART), :] = piece
 
@@ -217,7 +218,7 @@
     place = lax.rem(me, parts)
     for s in range(parts):
         for other in range(2):
-            f = ((me // parts) ^ other) * parts + (place ^ s)
+            f = ((me // parts) ^ other) * parts + (place ^ TURN[s])
             flat_rows(acc_ref, f, out_refs[s].at[other])
 
 
@@ -279,7 +280,7 @@
     rows = vox_rows // parts
     place = lax.rem(lax.axis_index("fas"), parts) if parts > 1 else 0
     for s, n in [(s, n) for s in range(parts) for n in range(rows)]:
-        r = (place ^ s) * rows + n if parts > 1 else n
+        r = (place ^ TURN[s]) * rows + n if parts > 1 else n
         packed = [res_refs[s][pl.ds(n * PACK + i * QUART, QUART), :] for i in range(3)]
         turned = [pltpu.roll(packed[i], 32 * (i + 1), 1) for i in range(3)]
         last = jnp.where(lane < 32, turned[0], jnp.where(lane < 64, turned[1], turned[2]))
@@ -458,7 +459,7 @@
     across = [(i, (i + half) % n_fas) for i in range(n_fas)]
     half_share = image_rows // half
 
-    parts = half if half in (2, 4) else 1
+    parts = half if half == 4 else 1
     share_out = ((half_share, LANES), f32, "v")
     image_outs = [share_out] * parts if parts > 1 else [image_out]
 
@@ -466,7 +467,7 @@
     flat_outs = [((flat_count, *signal.shape), f32, "v")] * parts
 
     def to_place(x, s):
-        return lax.ppermute(x, "fas", [(i, i ^ s) for i in range(n_fas)])
+        return lax.ppermute(x, "fas", [(i, i ^ TURN[s]) for i in range(n_fas)])
 
     def gather_shares(partial):
         if parts > 1:

time: 319 us -> 314 us (0.984)
  waiting for transfers between devices: 163 us -> 131 us
  Pallas kernels: 25.1 us -> 40.8 us
  starting transfers between devices: 86.4 us -> 91.8 us
  blocking collectives: 40.7 us -> 45.1 us
    ppermute x48, waiting for transfers between devices: 75 us -> 55.9 us  [to_place(): return lax.ppermute(x, 'fas', [(i, i ^ TURN[s]) for i in range(n_fas)])]
    pallas_call x39, Pallas kernels: 25.1 us -> 40.8 us  [placed(): run(*(pltpu.with_memory_space_constraint(x, spaces[kind]) if kind in 'vm'...]
    ppermute x5, waiting for transfers between devices: 27 us -> 15.7 us  [local(): other = lax.ppermute(mine, 'fas', across)]
    ppermute x5, starting transfers between devices: 6.54 us -> 15.5 us  [sum_all(): other = lax.ppermute(mine, 'fas', across)]
    ppermute x48, starting transfers between devices: 65.2 us -> 57.7 us  [to_place(): return lax.ppermute(x, 'fas', [(i, i ^ TURN[s]) for i in range(n_fas)])]
    ppermute x5, starting transfers between devices: 6.91 us -> 13.5 us  [local(): other = lax.ppermute(mine, 'fas', across)]
    ppermute x10, starting transfers between devices: 7.66 us -> 1.97 us  [local(): lax.ppermute(gradient, 'vox', [(i, i ^ bit) for i in range(n_vox)])]
    ppermute x10, waiting for transfers between devices: 28.1 us -> 33.1 us  [local(): lax.ppermute(gradient, 'vox', [(i, i ^ bit) for i in range(n_vox)])]
  transfers between devices with their start and end apart: 69 -> 69, of which waited for: 68 -> 56; matrix products, arithmetic and copies ran while one was open for 0% -> 0% of each run, Pallas kernels for 0% -> 0%
where the time goes in v3:
time: 314 us; the launch traced here: 313 us
  waiting for transfers between devices  131 us (42%)
  starting transfers between devices  91.8 us (29%)
  blocking collectives  45.1 us (14%)
  Pallas kernels  40.8 us (13%)
    ppermute x48, starting transfers between devices, to_place(): return lax.ppermute(x, 'fas', [(i, i ^ TURN[s]) for i in range(n_fas)])  57.7 us
    ppermute x48, waiting for transfers between devices, to_place(): return lax.ppermute(x, 'fas', [(i, i ^ TURN[s]) for i in range(n_fas)])  55.9 us
    all_to_all x5, blocking collectives, swap(): return lax.all_to_all(x, axis, 0, 0, axis_index_groups=groups)  45.1 us
    pallas_call x39, Pallas kernels, placed(): run(*(pltpu.with_memory_space_constraint(x, spaces[kind]) if kind in 'vm'...  40.8 us
    ppermute x10, waiting for transfers between devices, local(): lax.ppermute(gradient, 'vox', [(i, i ^ bit) for i in range(n_vox)])  33.1 us
    ppermute x5, waiting for transfers between devices, sum_all(): other = lax.ppermute(mine, 'fas', across)  23.4 us
    ppermute x5, waiting for transfers between devices, local(): other = lax.ppermute(mine, 'fas', across)  15.7 us
    ppermute x5, starting transfers between devices, sum_all(): other = lax.ppermute(mine, 'fas', across)  15.5 us
  transfers between devices with their start and end apart: 69, of which 56 were waited for; matrix products, arithmetic and copies ran while one was open for 0% of the time, Pallas kernels for 0%

profile of v3, /device:TPU:0, one launch (start us, length us, event | category | flops | bytes accessed | tf_op | source)
XLA Modules:
  0.0 313.5 jit_solution(3249004557764412992)
XLA Ops:
  4.2 5.1 %shard_map.95 = (bf16[76,64,256]{2,1,0:T(8,128)(2,1)S(1)}, bf16[76,128,256]{2,1,0:T(8,128)(2,1)S(1)}, bf16[76,256,128]{2,1,0:T(8,128)(2,1)S(1)}, s32[1,1024]{1,0:T(1,128)S(4)}) custom-call(s32[1,256]{1,0:T(1,128)S(1)} %bitcast.25, s32[256,128]{1,0:T(8,128)S(1)} %pad.12.side_ref, s32[1,1]{1,0:T(1,128)} %bitcast.13.count_ref, ...), custom_call_target="tpu_custom_call" | custom-call | tf_op jit(solution)/shard_map/pallas_call | solution.py:389
  20.5 2.7 collective-permute-start.3
  23.1 4.8 %collective-permute-done.3.refs_1_ = f32[192,128]{1,0:T(8,128)S(1)} collective-permute-done((f32[192,128]{1,0:T(8,128)S(1)}, f32[192,128]{1,0:T(8,128)S(1)}, u32[]{:S(2)}, u32[]{:S(2)}) %collective-permute-start.3) | collective-permute-done | bytes 98336 | tf_op jit(solution)/shard_map/ppermute | solution.py:481
  39.7 4.3 %collective-permute-done.8 = f32[256,128]{1,0:T(8,128)S(1)} collective-permute-done((f32[256,128]{1,0:T(8,128)S(1)}, f32[256,128]{1,0:T(8,128)S(1)}, u32[]{:S(2)}, u32[]{:S(2)}) %collective-permute-start.8) | collective-permute-done | bytes 131104 | tf_op jit(solution)/shard_map/ppermute | solution.py:504
  53.9 2.8 collective-permute-start.12
  56.7 3.9 %collective-permute-done.12.other_ref = f32[200,128]{1,0:T(8,128)S(1)} collective-permute-done((f32[200,128]{1,0:T(8,128)S(1)}, f32[200,128]{1,0:T(8,128)S(1)}, u32[]{:S(2)}, u32[]{:S(2)}) %collective-permute-start.12) | collective-permute-done | bytes 102432 | tf_op jit(solution)/shard_map/ppermute | solution.py:518
  60.7 8.2 %all_to_all.25.sums_ref = f32[16,1,128]{2,1,0:T(1,128)S(1)} all-to-all(f32[16,1,128]{2,1,0:T(1,128)S(1)} %shard_map.102), channel_id=1, replica_groups={{0,1,2,3,8,9,10,11,16,17,18,19,24,25,26,27},{4,5,6,7,12,13,14,15,20,21,..., dimensions={0} | all-to-all | bytes 16384 | tf_op jit(solution)/shard_map/all_to_all | solution.py:454
  74.5 2.6 collective-permute-done.13.refs_1_
  77.8 3.7 %collective-permute-start.16 = (f32[192,128]{1,0:T(8,128)S(1)}, f32[192,128]{1,0:T(8,128)S(1)}, u32[]{:S(2)}, u32[]{:S(2)}) collective-permute-start(f32[192,128]{1,0:T(8,128)S(1)} %shard_map.104.refs_0_), channel_id=1, source_target_pairs={{0,4},{1,5},{2,6},{3,7},{4,0},{5,1},{6,2},{7,3},{8,12},{9,13},{10,... | collective-permute-start | bytes 294920 | tf_op jit(solution)/shard_map/ppermute | solution.py:481
  81.5 4.5 %collective-permute-done.16.refs_1_ = f32[192,128]{1,0:T(8,128)S(1)} collective-permute-done((f32[192,128]{1,0:T(8,128)S(1)}, f32[192,128]{1,0:T(8,128)S(1)}, u32[]{:S(2)}, u32[]{:S(2)}) %collective-permute-start.16) | collective-permute-done | bytes 98336 | tf_op jit(solution)/shard_map/ppermute | solution.py:481
  89.6 2.9 collective-permute-done.17.refs_1_
  97.5 5.5 %collective-permute-done.21 = f32[256,128]{1,0:T(8,128)S(1)} collective-permute-done((f32[256,128]{1,0:T(8,128)S(1)}, f32[256,128]{1,0:T(8,128)S(1)}, u32[]{:S(2)}, u32[]{:S(2)}) %collective-permute-start.21) | collective-permute-done | bytes 131104 | tf_op jit(solution)/shard_map/ppermute | solution.py:504
  105.8 2.8 collective-permute-start.24
  111.3 2.7 collective-permute-start.25
  114.0 3.0 collective-permute-done.25.other_ref
  117.1 9.2 %all_to_all.26.sums_ref = f32[16,1,128]{2,1,0:T(1,128)S(1)} all-to-all(f32[16,1,128]{2,1,0:T(1,128)S(1)} %shard_map.109), channel_id=1, replica_groups={{0,1,2,3,8,9,10,11,16,17,18,19,24,25,26,27},{4,5,6,7,12,13,14,15,20,21,..., dimensions={0} | all-to-all | bytes 16384 | tf_op jit(solution)/shard_map/all_to_all | solution.py:454
  132.1 2.6 collective-permute-done.26.refs_1_
  135.4 3.1 collective-permute-start.29
  138.5 4.7 %collective-permute-done.29.refs_1_ = f32[192,128]{1,0:T(8,128)S(1)} collective-permute-done((f32[192,128]{1,0:T(8,128)S(1)}, f32[192,128]{1,0:T(8,128)S(1)}, u32[]{:S(2)}, u32[]{:S(2)}) %collective-permute-start.29) | collective-permute-done | bytes 98336 | tf_op jit(solution)/shard_map/ppermute | solution.py:481
  146.7 3.0 collective-permute-done.30.refs_1_
  154.5 5.5 %collective-permute-done.34 = f32[256,128]{1,0:T(8,128)S(1)} collective-permute-done((f32[256,128]{1,0:T(8,128)S(1)}, f32[256,128]{1,0:T(8,128)S(1)}, u32[]{:S(2)}, u32[]{:S(2)}) %collective-permute-start.34) | collective-permute-done | bytes 131104 | tf_op jit(solution)/shard_map/ppermute | solution.py:504
  162.8 2.8 collective-permute-start.37
  168.3 2.7 collective-permute-start.38
  171.0 2.9 collective-permute-done.38.other_ref
  174.0 9.2 %all_to_all.27.sums_ref = f32[16,1,128]{2,1,0:T(1,128)S(1)} all-to-all(f32[16,1,128]{2,1,0:T(1,128)S(1)} %shard_map.116), channel_id=1, replica_groups={{0,1,2,3,8,9,10,11,16,17,18,19,24,25,26,27},{4,5,6,7,12,13,14,15,20,21,..., dimensions={0} | all-to-all | bytes 16384 | tf_op jit(solution)/shard_map/all_to_all | solution.py:454
  186.7 2.3 collective-permute-start.41
  189.0 2.6 collective-permute-done.39.refs_1_
  192.2 3.1 collective-permute-start.42
  195.3 4.7 %collective-permute-done.42.refs_1_ = f32[192,128]{1,0:T(8,128)S(1)} collective-permute-done((f32[192,128]{1,0:T(8,128)S(1)}, f32[192,128]{1,0:T(8,128)S(1)}, u32[]{:S(2)}, u32[]{:S(2)}) %collective-permute-start.42) | collective-permute-done | bytes 98336 | tf_op jit(solution)/shard_map/ppermute | solution.py:481
  203.5 3.0 collective-permute-done.43.refs_1_
  211.3 5.5 %collective-permute-done.47 = f32[256,128]{1,0:T(8,128)S(1)} collective-permute-done((f32[256,128]{1,0:T(8,128)S(1)}, f32[256,128]{1,0:T(8,128)S(1)}, u32[]{:S(2)}, u32[]{:S(2)}) %collective-permute-start.47) | collective-permute-done | bytes 131104 | tf_op jit(solution)/shard_map/ppermute | solution.py:504
  219.6 2.8 collective-permute-start.50
  225.1 2.7 collective-permute-start.51
  227.8 2.9 collective-permute-done.51.other_ref
  230.9 9.3 %all_to_all.28.sums_ref = f32[16,1,128]{2,1,0:T(1,128)S(1)} all-to-all(f32[16,1,128]{2,1,0:T(1,128)S(1)} %shard_map.123), channel_id=1, replica_groups={{0,1,2,3,8,9,10,11,16,17,18,19,24,25,26,27},{4,5,6,7,12,13,14,15,20,21,..., dimensions={0} | all-to-all | bytes 16384 | tf_op jit(solution)/shard_map/all_to_all | solution.py:454
  245.8 2.6 collective-permute-done.52.refs_1_
  249.1 3.1 collective-permute-start.55
  252.1 4.7 %collective-permute-done.55.refs_1_ = f32[192,128]{1,0:T(8,128)S(1)} collective-permute-done((f32[192,128]{1,0:T(8,128)S(1)}, f32[192,128]{1,0:T(8,128)S(1)}, u32[]{:S(2)}, u32[]{:S(2)}) %collective-permute-start.55) | collective-permute-done | bytes 98336 | tf_op jit(solution)/shard_map/ppermute | solution.py:481
  260.4 3.0 collective-permute-done.56.refs_1_
  268.2 5.5 %collective-permute-done.60 = f32[256,128]{1,0:T(8,128)S(1)} collective-permute-done((f32[256,128]{1,0:T(8,128)S(1)}, f32[256,128]{1,0:T(8,128)S(1)}, u32[]{:S(2)}, u32[]{:S(2)}) %collective-permute-start.60) | collective-permute-done | bytes 131104 | tf_op jit(solution)/shard_map/ppermute | solution.py:504
  276.6 2.8 collective-permute-start.63
  282.2 2.7 collective-permute-start.64
  284.9 2.9 collective-permute-done.64.other_ref
  287.9 9.2 %all_to_all.29.sums_ref = f32[16,1,128]{2,1,0:T(1,128)S(1)} all-to-all(f32[16,1,128]{2,1,0:T(1,128)S(1)} %shard_map.130), channel_id=1, replica_groups={{0,1,2,3,8,9,10,11,16,17,18,19,24,25,26,27},{4,5,6,7,12,13,14,15,20,21,..., dimensions={0} | all-to-all | bytes 16384 | tf_op jit(solution)/shard_map/all_to_all | solution.py:454
  297.2 2.9 shard_map.131
  303.6 2.6 collective-permute-done.65.refs_1_
  306.8 3.1 collective-permute-start.68
  309.9 3.0 collective-permute-done.68.refs_1_
  (168 shorter events, 119.7 us)
Async XLA Ops:
  11.3 6.5 %collective-permute-start = (f32[192,128]{1,0:T(8,128)S(1)}, f32[192,128]{1,0:T(8,128)S(1)}, u32[]{:S(2)}, u32[]{:S(2)}) collective-permute-start(f32[192,128]{1,0:T(8,128)S(1)} %get-tuple-element.72), channel_id=1, source_target_pairs={{0,3},{1,2},{2,1},{3,0},{4,7},{5,6},{6,5},{7,4},{8,11},{9,10},{10,... | collective-permute-start | bytes 294920 | tf_op jit(solution)/shard_map/ppermute | solution.py:470
  12.5 7.4 %collective-permute-start.1 = (f32[192,128]{1,0:T(8,128)S(1)}, f32[192,128]{1,0:T(8,128)S(1)}, u32[]{:S(2)}, u32[]{:S(2)}) collective-permute-start(f32[192,128]{1,0:T(8,128)S(1)} %get-tuple-element.73), channel_id=1, source_target_pairs={{0,1},{1,0},{2,3},{3,2},{4,5},{5,4},{6,7},{7,6},{8,9},{9,8},{10,11... | collective-permute-start | bytes 294920 | tf_op jit(solution)/shard_map/ppermute | solution.py:470
  14.3 6.1 %collective-permute-start.2 = (f32[192,128]{1,0:T(8,128)S(1)}, f32[192,128]{1,0:T(8,128)S(1)}, u32[]{:S(2)}, u32[]{:S(2)}) collective-permute-start(f32[192,128]{1,0:T(8,128)S(1)} %get-tuple-element.74), channel_id=1, source_target_pairs={{0,2},{1,3},{2,0},{3,1},{4,6},{5,7},{6,4},{7,5},{8,10},{9,11},{10,... | collective-permute-start | bytes 294920 | tf_op jit(solution)/shard_map/ppermute | solution.py:470
  20.5 7.5 %collective-permute-start.3 = (f32[192,128]{1,0:T(8,128)S(1)}, f32[192,128]{1,0:T(8,128)S(1)}, u32[]{:S(2)}, u32[]{:S(2)}) collective-permute-start(f32[192,128]{1,0:T(8,128)S(1)} %shard_map.97.refs_0_), channel_id=1, source_target_pairs={{0,4},{1,5},{2,6},{3,7},{4,0},{5,1},{6,2},{7,3},{8,12},{9,13},{10,... | collective-permute-start | bytes 294920 | tf_op jit(solution)/shard_map/ppermute | solution.py:481
  28.0 5.8 %collective-permute-start.4 = (f32[192,128]{1,0:T(8,128)S(1)}, f32[192,128]{1,0:T(8,128)S(1)}, u32[]{:S(2)}, u32[]{:S(2)}) collective-permute-start(f32[192,128]{1,0:T(8,128)S(1)} %shard_map.98.refs_0_), channel_id=1, source_target_pairs={{0,3},{1,2},{2,1},{3,0},{4,7},{5,6},{6,5},{7,4},{8,11},{9,10},{10,... | collective-permute-start | bytes 294920 | tf_op jit(solution)/shard_map/ppermute | solution.py:470
  28.6 5.7 %collective-permute-start.5 = (f32[192,128]{1,0:T(8,128)S(1)}, f32[192,128]{1,0:T(8,128)S(1)}, u32[]{:S(2)}, u32[]{:S(2)}) collective-permute-start(f32[192,128]{1,0:T(8,128)S(1)} %shard_map.98.refs_0_), channel_id=1, source_target_pairs={{0,1},{1,0},{2,3},{3,2},{4,5},{5,4},{6,7},{7,6},{8,9},{9,8},{10,11... | collective-permute-start | bytes 294920 | tf_op jit(solution)/shard_map/ppermute | solution.py:470
  38.3 5.6 %collective-permute-start.8 = (f32[256,128]{1,0:T(8,128)S(1)}, f32[256,128]{1,0:T(8,128)S(1)}, u32[]{:S(2)}, u32[]{:S(2)}) collective-permute-start(f32[256,128]{1,0:T(8,128)S(1)} %add.40), channel_id=1, source_target_pairs={{0,16},{8,24},{16,0},{24,8},{1,17},{9,25},{17,1},{25,9},{2,18},{10... | collective-permute-start | bytes 393224 | tf_op jit(solution)/shard_map/ppermute | solution.py:504
  47.3 6.5 %collective-permute-start.9 = (f32[192,128]{1,0:T(8,128)S(1)}, f32[192,128]{1,0:T(8,128)S(1)}, u32[]{:S(2)}, u32[]{:S(2)}) collective-permute-start(f32[192,128]{1,0:T(8,128)S(1)} %get-tuple-element.77), channel_id=1, source_target_pairs={{0,3},{1,2},{2,1},{3,0},{4,7},{5,6},{6,5},{7,4},{8,11},{9,10},{10,... | collective-permute-start | bytes 294920 | tf_op jit(solution)/shard_map/ppermute | solution.py:470
  53.9 6.7 %collective-permute-start.12 = (f32[200,128]{1,0:T(8,128)S(1)}, f32[200,128]{1,0:T(8,128)S(1)}, u32[]{:S(2)}, u32[]{:S(2)}) collective-permute-start(f32[200,128]{1,0:T(8,128)S(1)} %shard_map.101.mine_ref), channel_id=1, source_target_pairs={{0,4},{1,5},{2,6},{3,7},{4,0},{5,1},{6,2},{7,3},{8,12},{9,13},{10,... | collective-permute-start | bytes 307208 | tf_op jit(solution)/shard_map/ppermute | solution.py:518
  71.0 6.1 %collective-permute-start.13 = (f32[192,128]{1,0:T(8,128)S(1)}, f32[192,128]{1,0:T(8,128)S(1)}, u32[]{:S(2)}, u32[]{:S(2)}) collective-permute-start(f32[192,128]{1,0:T(8,128)S(1)} %get-tuple-element.82), channel_id=1, source_target_pairs={{0,3},{1,2},{2,1},{3,0},{4,7},{5,6},{6,5},{7,4},{8,11},{9,10},{10,... | collective-permute-start | bytes 294920 | tf_op jit(solution)/shard_map/ppermute | solution.py:470
  71.1 6.7 %collective-permute-start.14 = (f32[192,128]{1,0:T(8,128)S(1)}, f32[192,128]{1,0:T(8,128)S(1)}, u32[]{:S(2)}, u32[]{:S(2)}) collective-permute-start(f32[192,128]{1,0:T(8,128)S(1)} %get-tuple-element.83), channel_id=1, source_target_pairs={{0,1},{1,0},{2,3},{3,2},{4,5},{5,4},{6,7},{7,6},{8,9},{9,8},{10,11... | collective-permute-start | bytes 294920 | tf_op jit(solution)/shard_map/ppermute | solution.py:470
  77.8 8.2 %collective-permute-start.16 = (f32[192,128]{1,0:T(8,128)S(1)}, f32[192,128]{1,0:T(8,128)S(1)}, u32[]{:S(2)}, u32[]{:S(2)}) collective-permute-start(f32[192,128]{1,0:T(8,128)S(1)} %shard_map.104.refs_0_), channel_id=1, source_target_pairs={{0,4},{1,5},{2,6},{3,7},{4,0},{5,1},{6,2},{7,3},{8,12},{9,13},{10,... | collective-permute-start | bytes 294920 | tf_op jit(solution)/shard_map/ppermute | solution.py:481
  86.0 6.4 %collective-permute-start.17 = (f32[192,128]{1,0:T(8,128)S(1)}, f32[192,128]{1,0:T(8,128)S(1)}, u32[]{:S(2)}, u32[]{:S(2)}) collective-permute-start(f32[192,128]{1,0:T(8,128)S(1)} %shard_map.105.refs_0_), channel_id=1, source_target_pairs={{0,3},{1,2},{2,1},{3,0},{4,7},{5,6},{6,5},{7,4},{8,11},{9,10},{10,... | collective-permute-start | bytes 294920 | tf_op jit(solution)/shard_map/ppermute | solution.py:470
  86.8 5.7 %collective-permute-start.18 = (f32[192,128]{1,0:T(8,128)S(1)}, f32[192,128]{1,0:T(8,128)S(1)}, u32[]{:S(2)}, u32[]{:S(2)}) collective-permute-start(f32[192,128]{1,0:T(8,128)S(1)} %shard_map.105.refs_0_), channel_id=1, source_target_pairs={{0,1},{1,0},{2,3},{3,2},{4,5},{5,4},{6,7},{7,6},{8,9},{9,8},{10,11... | collective-permute-start | bytes 294920 | tf_op jit(solution)/shard_map/ppermute | solution.py:470
  87.7 6.1 %collective-permute-start.19 = (f32[192,128]{1,0:T(8,128)S(1)}, f32[192,128]{1,0:T(8,128)S(1)}, u32[]{:S(2)}, u32[]{:S(2)}) collective-permute-start(f32[192,128]{1,0:T(8,128)S(1)} %shard_map.105.refs_0_), channel_id=1, source_target_pairs={{0,2},{1,3},{2,0},{3,1},{4,6},{5,7},{6,4},{7,5},{8,10},{9,11},{10,... | collective-permute-start | bytes 294920 | tf_op jit(solution)/shard_map/ppermute | solution.py:470
  105.0 5.7 %collective-permute-start.22 = (f32[192,128]{1,0:T(8,128)S(1)}, f32[192,128]{1,0:T(8,128)S(1)}, u32[]{:S(2)}, u32[]{:S(2)}) collective-permute-start(f32[192,128]{1,0:T(8,128)S(1)} %get-tuple-element.88), channel_id=1, source_target_pairs={{0,3},{1,2},{2,1},{3,0},{4,7},{5,6},{6,5},{7,4},{8,11},{9,10},{10,... | collective-permute-start | bytes 294920 | tf_op jit(solution)/shard_map/ppermute | solution.py:470
  105.1 6.2 %collective-permute-start.23 = (f32[192,128]{1,0:T(8,128)S(1)}, f32[192,128]{1,0:T(8,128)S(1)}, u32[]{:S(2)}, u32[]{:S(2)}) collective-permute-start(f32[192,128]{1,0:T(8,128)S(1)} %get-tuple-element.89), channel_id=1, source_target_pairs={{0,1},{1,0},{2,3},{3,2},{4,5},{5,4},{6,7},{7,6},{8,9},{9,8},{10,11... | collective-permute-start | bytes 294920 | tf_op jit(solution)/shard_map/ppermute | solution.py:470
  111.3 5.6 %collective-permute-start.25 = (f32[200,128]{1,0:T(8,128)S(1)}, f32[200,128]{1,0:T(8,128)S(1)}, u32[]{:S(2)}, u32[]{:S(2)}) collective-permute-start(f32[200,128]{1,0:T(8,128)S(1)} %shard_map.108.mine_ref), channel_id=1, source_target_pairs={{0,4},{1,5},{2,6},{3,7},{4,0},{5,1},{6,2},{7,3},{8,12},{9,13},{10,... | collective-permute-start | bytes 307208 | tf_op jit(solution)/shard_map/ppermute | solution.py:518
  128.6 6.1 %collective-permute-start.26 = (f32[192,128]{1,0:T(8,128)S(1)}, f32[192,128]{1,0:T(8,128)S(1)}, u32[]{:S(2)}, u32[]{:S(2)}) collective-permute-start(f32[192,128]{1,0:T(8,128)S(1)} %get-tuple-element.93), channel_id=1, source_target_pairs={{0,3},{1,2},{2,1},{3,0},{4,7},{5,6},{6,5},{7,4},{8,11},{9,10},{10,... | collective-permute-start | bytes 294920 | tf_op jit(solution)/shard_map/ppermute | solution.py:470
  128.7 6.7 %collective-permute-start.27 = (f32[192,128]{1,0:T(8,128)S(1)}, f32[192,128]{1,0:T(8,128)S(1)}, u32[]{:S(2)}, u32[]{:S(2)}) collective-permute-start(f32[192,128]{1,0:T(8,128)S(1)} %get-tuple-element.94), channel_id=1, source_target_pairs={{0,1},{1,0},{2,3},{3,2},{4,5},{5,4},{6,7},{7,6},{8,9},{9,8},{10,11... | collective-permute-start | bytes 294920 | tf_op jit(solution)/shard_map/ppermute | solution.py:470
  135.4 7.7 %collective-permute-start.29 = (f32[192,128]{1,0:T(8,128)S(1)}, f32[192,128]{1,0:T(8,128)S(1)}, u32[]{:S(2)}, u32[]{:S(2)}) collective-permute-start(f32[192,128]{1,0:T(8,128)S(1)} %shard_map.111.refs_0_), channel_id=1, source_target_pairs={{0,4},{1,5},{2,6},{3,7},{4,0},{5,1},{6,2},{7,3},{8,12},{9,13},{10,... | collective-permute-start | bytes 294920 | tf_op jit(solution)/shard_map/ppermute | solution.py:481
  143.1 6.5 %collective-permute-start.30 = (f32[192,128]{1,0:T(8,128)S(1)}, f32[192,128]{1,0:T(8,128)S(1)}, u32[]{:S(2)}, u32[]{:S(2)}) collective-permute-start(f32[192,128]{1,0:T(8,128)S(1)} %shard_map.112.refs_0_), channel_id=1, source_target_pairs={{0,3},{1,2},{2,1},{3,0},{4,7},{5,6},{6,5},{7,4},{8,11},{9,10},{10,... | collective-permute-start | bytes 294920 | tf_op jit(solution)/shard_map/ppermute | solution.py:470
  143.8 5.9 %collective-permute-start.31 = (f32[192,128]{1,0:T(8,128)S(1)}, f32[192,128]{1,0:T(8,128)S(1)}, u32[]{:S(2)}, u32[]{:S(2)}) collective-permute-start(f32[192,128]{1,0:T(8,128)S(1)} %shard_map.112.refs_0_), channel_id=1, source_target_pairs={{0,1},{1,0},{2,3},{3,2},{4,5},{5,4},{6,7},{7,6},{8,9},{9,8},{10,11... | collective-permute-start | bytes 294920 | tf_op jit(solution)/shard_map/ppermute | solution.py:470
  144.7 6.1 %collective-permute-start.32 = (f32[192,128]{1,0:T(8,128)S(1)}, f32[192,128]{1,0:T(8,128)S(1)}, u32[]{:S(2)}, u32[]{:S(2)}) collective-permute-start(f32[192,128]{1,0:T(8,128)S(1)} %shard_map.112.refs_0_), channel_id=1, source_target_pairs={{0,2},{1,3},{2,0},{3,1},{4,6},{5,7},{6,4},{7,5},{8,10},{9,11},{10,... | collective-permute-start | bytes 294920 | tf_op jit(solution)/shard_map/ppermute | solution.py:470
  162.0 5.7 %collective-permute-start.35 = (f32[192,128]{1,0:T(8,128)S(1)}, f32[192,128]{1,0:T(8,128)S(1)}, u32[]{:S(2)}, u32[]{:S(2)}) collective-permute-start(f32[192,128]{1,0:T(8,128)S(1)} %get-tuple-element.99), channel_id=1, source_target_pairs={{0,3},{1,2},{2,1},{3,0},{4,7},{5,6},{6,5},{7,4},{8,11},{9,10},{10,... | collective-permute-start | bytes 294920 | tf_op jit(solution)/shard_map/ppermute | solution.py:470
  162.1 6.1 %collective-permute-start.36 = (f32[192,128]{1,0:T(8,128)S(1)}, f32[192,128]{1,0:T(8,128)S(1)}, u32[]{:S(2)}, u32[]{:S(2)}) collective-permute-start(f32[192,128]{1,0:T(8,128)S(1)} %get-tuple-element.100), channel_id=1, source_target_pairs={{0,1},{1,0},{2,3},{3,2},{4,5},{5,4},{6,7},{7,6},{8,9},{9,8},{10,11... | collective-permute-start | bytes 294920 | tf_op jit(solution)/shard_map/ppermute | solution.py:470
  168.3 5.6 %collective-permute-start.38 = (f32[200,128]{1,0:T(8,128)S(1)}, f32[200,128]{1,0:T(8,128)S(1)}, u32[]{:S(2)}, u32[]{:S(2)}) collective-permute-start(f32[200,128]{1,0:T(8,128)S(1)} %shard_map.115.mine_ref), channel_id=1, source_target_pairs={{0,4},{1,5},{2,6},{3,7},{4,0},{5,1},{6,2},{7,3},{8,12},{9,13},{10,... | collective-permute-start | bytes 307208 | tf_op jit(solution)/shard_map/ppermute | solution.py:518
  185.4 6.1 %collective-permute-start.39 = (f32[192,128]{1,0:T(8,128)S(1)}, f32[192,128]{1,0:T(8,128)S(1)}, u32[]{:S(2)}, u32[]{:S(2)}) collective-permute-start(f32[192,128]{1,0:T(8,128)S(1)} %get-tuple-element.104), channel_id=1, source_target_pairs={{0,3},{1,2},{2,1},{3,0},{4,7},{5,6},{6,5},{7,4},{8,11},{9,10},{10,... | collective-permute-start | bytes 294920 | tf_op jit(solution)/shard_map/ppermute | solution.py:470
  185.5 6.7 %collective-permute-start.40 = (f32[192,128]{1,0:T(8,128)S(1)}, f32[192,128]{1,0:T(8,128)S(1)}, u32[]{:S(2)}, u32[]{:S(2)}) collective-permute-start(f32[192,128]{1,0:T(8,128)S(1)} %get-tuple-element.105), channel_id=1, source_target_pairs={{0,1},{1,0},{2,3},{3,2},{4,5},{5,4},{6,7},{7,6},{8,9},{9,8},{10,11... | collective-permute-start | bytes 294920 | tf_op jit(solution)/shard_map/ppermute | solution.py:470
  192.2 7.7 %collective-permute-start.42 = (f32[192,128]{1,0:T(8,128)S(1)}, f32[192,128]{1,0:T(8,128)S(1)}, u32[]{:S(2)}, u32[]{:S(2)}) collective-permute-start(f32[192,128]{1,0:T(8,128)S(1)} %shard_map.118.refs_0_), channel_id=1, source_target_pairs={{0,4},{1,5},{2,6},{3,7},{4,0},{5,1},{6,2},{7,3},{8,12},{9,13},{10,... | collective-permute-start | bytes 294920 | tf_op jit(solution)/shard_map/ppermute | solution.py:481
  200.0 6.5 %collective-permute-start.43 = (f32[192,128]{1,0:T(8,128)S(1)}, f32[192,128]{1,0:T(8,128)S(1)}, u32[]{:S(2)}, u32[]{:S(2)}) collective-permute-start(f32[192,128]{1,0:T(8,128)S(1)} %shard_map.119.refs_0_), channel_id=1, source_target_pairs={{0,3},{1,2},{2,1},{3,0},{4,7},{5,6},{6,5},{7,4},{8,11},{9,10},{10,... | collective-permute-start | bytes 294920 | tf_op jit(solution)/shard_map/ppermute | solution.py:470
  200.6 5.9 %collective-permute-start.44 = (f32[192,128]{1,0:T(8,128)S(1)}, f32[192,128]{1,0:T(8,128)S(1)}, u32[]{:S(2)}, u32[]{:S(2)}) collective-permute-start(f32[192,128]{1,0:T(8,128)S(1)} %shard_map.119.refs_0_), channel_id=1, source_target_pairs={{0,1},{1,0},{2,3},{3,2},{4,5},{5,4},{6,7},{7,6},{8,9},{9,8},{10,11... | collective-permute-start | bytes 294920 | tf_op jit(solution)/shard_map/ppermute | solution.py:470
  201.6 6.1 %collective-permute-start.45 = (f32[192,128]{1,0:T(8,128)S(1)}, f32[192,128]{1,0:T(8,128)S(1)}, u32[]{:S(2)}, u32[]{:S(2)}) collective-permute-start(f32[192,128]{1,0:T(8,128)S(1)} %shard_map.119.refs_0_), channel_id=1, source_target_pairs={{0,2},{1,3},{2,0},{3,1},{4,6},{5,7},{6,4},{7,5},{8,10},{9,11},{10,... | collective-permute-start | bytes 294920 | tf_op jit(solution)/shard_map/ppermute | solution.py:470
  218.9 5.7 %collective-permute-start.48 = (f32[192,128]{1,0:T(8,128)S(1)}, f32[192,128]{1,0:T(8,128)S(1)}, u32[]{:S(2)}, u32[]{:S(2)}) collective-permute-start(f32[192,128]{1,0:T(8,128)S(1)} %get-tuple-element.110), channel_id=1, source_target_pairs={{0,3},{1,2},{2,1},{3,0},{4,7},{5,6},{6,5},{7,4},{8,11},{9,10},{10,... | collective-permute-start | bytes 294920 | tf_op jit(solution)/shard_map/ppermute | solution.py:470
  219.0 6.1 %collective-permute-start.49 = (f32[192,128]{1,0:T(8,128)S(1)}, f32[192,128]{1,0:T(8,128)S(1)}, u32[]{:S(2)}, u32[]{:S(2)}) collective-permute-start(f32[192,128]{1,0:T(8,128)S(1)} %get-tuple-element.111), channel_id=1, source_target_pairs={{0,1},{1,0},{2,3},{3,2},{4,5},{5,4},{6,7},{7,6},{8,9},{9,8},{10,11... | collective-permute-start | bytes 294920 | tf_op jit(solution)/shard_map/ppermute | solution.py:470
  225.1 5.6 %collective-permute-start.51 = (f32[200,128]{1,0:T(8,128)S(1)}, f32[200,128]{1,0:T(8,128)S(1)}, u32[]{:S(2)}, u32[]{:S(2)}) collective-permute-start(f32[200,128]{1,0:T(8,128)S(1)} %shard_map.122.mine_ref), channel_id=1, source_target_pairs={{0,4},{1,5},{2,6},{3,7},{4,0},{5,1},{6,2},{7,3},{8,12},{9,13},{10,... | collective-permute-start | bytes 307208 | tf_op jit(solution)/shard_map/ppermute | solution.py:518
  242.3 6.1 %collective-permute-start.52 = (f32[192,128]{1,0:T(8,128)S(1)}, f32[192,128]{1,0:T(8,128)S(1)}, u32[]{:S(2)}, u32[]{:S(2)}) collective-permute-start(f32[192,128]{1,0:T(8,128)S(1)} %get-tuple-element.115), channel_id=1, source_target_pairs={{0,3},{1,2},{2,1},{3,0},{4,7},{5,6},{6,5},{7,4},{8,11},{9,10},{10,... | collective-permute-start | bytes 294920 | tf_op jit(solution)/shard_map/ppermute | solution.py:470
  242.3 6.7 %collective-permute-start.53 = (f32[192,128]{1,0:T(8,128)S(1)}, f32[192,128]{1,0:T(8,128)S(1)}, u32[]{:S(2)}, u32[]{:S(2)}) collective-permute-start(f32[192,128]{1,0:T(8,128)S(1)} %get-tuple-element.116), channel_id=1, source_target_pairs={{0,1},{1,0},{2,3},{3,2},{4,5},{5,4},{6,7},{7,6},{8,9},{9,8},{10,11... | collective-permute-start | bytes 294920 | tf_op jit(solution)/shard_map/ppermute | solution.py:470
  249.1 7.7 %collective-permute-start.55 = (f32[192,128]{1,0:T(8,128)S(1)}, f32[192,128]{1,0:T(8,128)S(1)}, u32[]{:S(2)}, u32[]{:S(2)}) collective-permute-start(f32[192,128]{1,0:T(8,128)S(1)} %shard_map.125.refs_0_), channel_id=1, source_target_pairs={{0,4},{1,5},{2,6},{3,7},{4,0},{5,1},{6,2},{7,3},{8,12},{9,13},{10,... | collective-permute-start | bytes 294920 | tf_op jit(solution)/shard_map/ppermute | solution.py:481
  256.8 6.5 %collective-permute-start.56 = (f32[192,128]{1,0:T(8,128)S(1)}, f32[192,128]{1,0:T(8,128)S(1)}, u32[]{:S(2)}, u32[]{:S(2)}) collective-permute-start(f32[192,128]{1,0:T(8,128)S(1)} %shard_map.126.refs_0_), channel_id=1, source_target_pairs={{0,3},{1,2},{2,1},{3,0},{4,7},{5,6},{6,5},{7,4},{8,11},{9,10},{10,... | collective-permute-start | bytes 294920 | tf_op jit(solution)/shard_map/ppermute | solution.py:470
  257.5 5.9 %collective-permute-start.57 = (f32[192,128]{1,0:T(8,128)S(1)}, f32[192,128]{1,0:T(8,128)S(1)}, u32[]{:S(2)}, u32[]{:S(2)}) collective-permute-start(f32[192,128]{1,0:T(8,128)S(1)} %shard_map.126.refs_0_), channel_id=1, source_target_pairs={{0,1},{1,0},{2,3},{3,2},{4,5},{5,4},{6,7},{7,6},{8,9},{9,8},{10,11... | collective-permute-start | bytes 294920 | tf_op jit(solution)/shard_map/ppermute | solution.py:470
  258.4 6.1 %collective-permute-start.58 = (f32[192,128]{1,0:T(8,128)S(1)}, f32[192,128]{1,0:T(8,128)S(1)}, u32[]{:S(2)}, u32[]{:S(2)}) collective-permute-start(f32[192,128]{1,0:T(8,128)S(1)} %shard_map.126.refs_0_), channel_id=1, source_target_pairs={{0,2},{1,3},{2,0},{3,1},{4,6},{5,7},{6,4},{7,5},{8,10},{9,11},{10,... | collective-permute-start | bytes 294920 | tf_op jit(solution)/shard_map/ppermute | solution.py:470
  275.9 5.7 %collective-permute-start.61 = (f32[192,128]{1,0:T(8,128)S(1)}, f32[192,128]{1,0:T(8,128)S(1)}, u32[]{:S(2)}, u32[]{:S(2)}) collective-permute-start(f32[192,128]{1,0:T(8,128)S(1)} %get-tuple-element.121), channel_id=1, source_target_pairs={{0,3},{1,2},{2,1},{3,0},{4,7},{5,6},{6,5},{7,4},{8,11},{9,10},{10,... | collective-permute-start | bytes 294920 | tf_op jit(solution)/shard_map/ppermute | solution.py:470
  276.0 6.1 %collective-permute-start.62 = (f32[192,128]{1,0:T(8,128)S(1)}, f32[192,128]{1,0:T(8,128)S(1)}, u32[]{:S(2)}, u32[]{:S(2)}) collective-permute-start(f32[192,128]{1,0:T(8,128)S(1)} %get-tuple-element.122), channel_id=1, source_target_pairs={{0,1},{1,0},{2,3},{3,2},{4,5},{5,4},{6,7},{7,6},{8,9},{9,8},{10,11... | collective-permute-start | bytes 294920 | tf_op jit(solution)/shard_map/ppermute | solution.py:470
  282.2 5.6 %collective-permute-start.64 = (f32[200,128]{1,0:T(8,128)S(1)}, f32[200,128]{1,0:T(8,128)S(1)}, u32[]{:S(2)}, u32[]{:S(2)}) collective-permute-start(f32[200,128]{1,0:T(8,128)S(1)} %shard_map.129.mine_ref), channel_id=1, source_target_pairs={{0,4},{1,5},{2,6},{3,7},{4,0},{5,1},{6,2},{7,3},{8,12},{9,13},{10,... | collective-permute-start | bytes 307208 | tf_op jit(solution)/shard_map/ppermute | solution.py:518
  300.1 6.1 %collective-permute-start.65 = (f32[2,16,768]{2,1,0:T(8,128)S(1)}, f32[2,16,768]{2,1,0:T(8,128)S(1)}, u32[]{:S(2)}, u32[]{:S(2)}) collective-permute-start(f32[2,16,768]{2,1,0:T(8,128)S(1)} %get-tuple-element.127), channel_id=1, source_target_pairs={{0,3},{1,2},{2,1},{3,0},{4,7},{5,6},{6,5},{7,4},{8,11},{9,10},{10,... | collective-permute-start | bytes 294920 | tf_op jit(solution)/shard_map/ppermute | solution.py:470
  300.1 6.7 %collective-permute-start.66 = (f32[2,16,768]{2,1,0:T(8,128)S(1)}, f32[2,16,768]{2,1,0:T(8,128)S(1)}, u32[]{:S(2)}, u32[]{:S(2)}) collective-permute-start(f32[2,16,768]{2,1,0:T(8,128)S(1)} %get-tuple-element.128), channel_id=1, source_target_pairs={{0,1},{1,0},{2,3},{3,2},{4,5},{5,4},{6,7},{7,6},{8,9},{9,8},{10,11... | collective-permute-start | bytes 294920 | tf_op jit(solution)/shard_map/ppermute | solution.py:470
  306.8 6.0 %collective-permute-start.68 = (f32[16,768]{1,0:T(8,128)S(1)}, f32[16,768]{1,0:T(8,128)S(1)}, u32[]{:S(2)}, u32[]{:S(2)}) collective-permute-start(f32[16,768]{1,0:T(8,128)S(1)} %get-tuple-element.131), channel_id=1, source_target_pairs={{0,4},{1,5},{2,6},{3,7},{4,0},{5,1},{6,2},{7,3},{8,12},{9,13},{10,... | collective-permute-start | bytes 147464 | tf_op jit(solution)/shard_map/ppermute | solution.py:532
  (27 other events, 113.6 us)

commit v4 on v3

--- a/solution.py
+++ b/solution.py
@@ -13,7 +13,7 @@
 ITERS = 5
 LANES = 128
 GROUP = 4
-BUILD = 19
+BUILD = 38
 UNROLL = 38
 PACK = BV * DIRS // LANES
 HALF = BV // 2
@@ -24,7 +24,7 @@
 
 def group_cap(slots, rows):
     groups = (slots + (GROUP - 1) * rows) // GROUP
-    return -(-groups // UNROLL) * UNROLL
+    return -(-groups // (2 * UNROLL)) * 2 * UNROLL
 
 
 def plan_spots(cap):
@@ -71,7 +71,7 @@
     row = jnp.sum(jnp.where(place == heads, rows_down, 0), axis=0, keepdims=True)
     plan_ref[:, row_at : row_at + cap] = row
     total = jnp.sum(groups, axis=1, keepdims=True)
-    turns = (total + UNROLL - 1) // UNROLL
+    turns = (total + 2 * UNROLL - 1) // (2 * UNROLL) * 2
     plan_ref[:, turns_at:] = jnp.broadcast_to(turns, (1, LANES))
 
 
@@ -295,15 +295,15 @@
 
     def turn(t, carry):
         sums = []
-        for n in range(UNROLL):
-            q = t * UNROLL + n
+        for n in range(2 * UNROLL):
+            q = t * 2 * UNROLL + n
             r = meta_ref[0, row_at + q]
             part = jnp.dot(split_ref[r], at_ref[q], preferred_element_type=jnp.float32)
             part = (part[:BV] + part[BV:]) * cp_ref[q].astype(jnp.float32)
             sums.append(jnp.sum(part, axis=0, keepdims=True))
-        for n in range(UNROLL):
+        for n in range(2 * UNROLL):
             for pair in range(GROUP // 2):
-                p = (t * UNROLL + n) * GROUP + 2 * pair
+                p = (t * 2 * UNROLL + n) * GROUP + 2 * pair
                 row = sums[n][:, pair * LANES : (pair + 1) * LANES]
                 c0 = pl.ds(meta_ref[0, p], 1)
                 left_ref[c0, :] = left_ref[c0, :] + row
@@ -311,7 +311,7 @@
                 right_ref[c1, :] = right_ref[c1, :] + row
         return carry
 
-    lax.fori_loop(0, meta_ref[0, turns_at], turn, 0)
+    lax.fori_loop(0, meta_ref[0, turns_at] // 2, turn, 0)
     rows = out_ref.shape[0]
     left = lane_ids(rows) < BF
     even = [ref[pl.ds(0, rows, stride=2), :] for ref in (left_ref, right_ref)]

time: 314 us -> 315 us (level)
  waiting for transfers between devices: 131 us -> 146 us
  starting transfers between devices: 91.8 us -> 83 us
  blocking collectives: 45.1 us -> 40.7 us
    ppermute x5, waiting for transfers between devices: 15.7 us -> 25.5 us  [local(): other = lax.ppermute(mine, 'fas', across)]
    ppermute x5, starting transfers between devices: 13.5 us -> 8.12 us  [local(): other = lax.ppermute(mine, 'fas', across)]
    all_to_all x5, blocking collectives: 45.1 us -> 40.7 us  [swap(): return lax.all_to_all(x, axis, 0, 0, axis_index_groups=groups)]
    ppermute x48, waiting for transfers between devices: 55.9 us -> 60.2 us  [to_place(): return lax.ppermute(x, 'fas', [(i, i ^ TURN[s]) for i in range(n_fas)])]
    ppermute x5, starting transfers between devices: 15.5 us -> 11.3 us  [sum_all(): other = lax.ppermute(mine, 'fas', across)]
  transfers between devices with their start and end apart: 69 -> 69, of which waited for: 56 -> 57; matrix products, arithmetic and copies ran while one was open for 0% -> 0% of each run, Pallas kernels for 0% -> 0%
where the time goes in v4:
time: 315 us; the launch traced here: 314 us
  waiting for transfers between devices  146 us (46%)
  starting transfers between devices  83 us (26%)
  blocking collectives  40.7 us (13%)
  Pallas kernels  39.7 us (13%)
    ppermute x48, waiting for transfers between devices, to_place(): return lax.ppermute(x, 'fas', [(i, i ^ TURN[s]) for i in range(n_fas)])  60.2 us
    ppermute x48, starting transfers between devices, to_place(): return lax.ppermute(x, 'fas', [(i, i ^ TURN[s]) for i in range(n_fas)])  57.9 us
    all_to_all x5, blocking collectives, swap(): return lax.all_to_all(x, axis, 0, 0, axis_index_groups=groups)  40.7 us
    pallas_call x39, Pallas kernels, placed(): run(*(pltpu.with_memory_space_constraint(x, spaces[kind]) if kind in 'vm'...  39.7 us
    ppermute x10, waiting for transfers between devices, local(): lax.ppermute(gradient, 'vox', [(i, i ^ bit) for i in range(n_vox)])  30.6 us
    ppermute x5, waiting for transfers between devices, sum_all(): other = lax.ppermute(mine, 'fas', across)  25.6 us
    ppermute x5, waiting for transfers between devices, local(): other = lax.ppermute(mine, 'fas', across)  25.5 us
    ppermute x5, starting transfers between devices, sum_all(): other = lax.ppermute(mine, 'fas', across)  11.3 us
  transfers between devices with their start and end apart: 69, of which 57 were waited for; matrix products, arithmetic and copies ran while one was open for 0% of the time, Pallas kernels for 0%

profile of v4, /device:TPU:0, one launch (start us, length us, event | category | flops | bytes accessed | tf_op | source)
XLA Modules:
  0.0 313.9 jit_solution(15871775525913262946)
XLA Ops:
  0.7 2.1 copy.22
  4.2 4.8 %shard_map.95 = (bf16[76,64,256]{2,1,0:T(8,128)(2,1)S(1)}, bf16[76,128,256]{2,1,0:T(8,128)(2,1)S(1)}, bf16[76,256,128]{2,1,0:T(8,128)(2,1)S(1)}, s32[1,1024]{1,0:T(1,128)S(4)}) custom-call(s32[1,256]{1,0:T(1,128)S(1)} %bitcast.25, s32[256,128]{1,0:T(8,128)S(1)} %pad.12.side_ref, s32[1,1]{1,0:T(1,128)} %bitcast.13.count_ref, ...), custom_call_target="tpu_custom_call" | custom-call | tf_op jit(solution)/shard_map/pallas_call | solution.py:389
  11.1 4.0 %collective-permute-start = (f32[192,128]{1,0:T(8,128)S(1)}, f32[192,128]{1,0:T(8,128)S(1)}, u32[]{:S(2)}, u32[]{:S(2)}) collective-permute-start(f32[192,128]{1,0:T(8,128)S(1)} %get-tuple-element.72), channel_id=1, source_target_pairs={{0,3},{1,2},{2,1},{3,0},{4,7},{5,6},{6,5},{7,4},{8,11},{9,10},{10,... | collective-permute-start | bytes 294920 | tf_op jit(solution)/shard_map/ppermute | solution.py:470
  15.7 2.5 collective-permute-done.refs_1_
  20.2 2.7 collective-permute-start.3
  22.9 4.9 %collective-permute-done.3.refs_1_ = f32[192,128]{1,0:T(8,128)S(1)} collective-permute-done((f32[192,128]{1,0:T(8,128)S(1)}, f32[192,128]{1,0:T(8,128)S(1)}, u32[]{:S(2)}, u32[]{:S(2)}) %collective-permute-start.3) | collective-permute-done | bytes 98336 | tf_op jit(solution)/shard_map/ppermute | solution.py:481
  31.3 2.1 collective-permute-done.4.refs_1_
  39.6 4.0 %collective-permute-done.8 = f32[256,128]{1,0:T(8,128)S(1)} collective-permute-done((f32[256,128]{1,0:T(8,128)S(1)}, f32[256,128]{1,0:T(8,128)S(1)}, u32[]{:S(2)}, u32[]{:S(2)}) %collective-permute-start.8) | collective-permute-done | bytes 131104 | tf_op jit(solution)/shard_map/ppermute | solution.py:504
  53.6 2.8 collective-permute-start.12
  56.4 3.9 %collective-permute-done.12.other_ref = f32[200,128]{1,0:T(8,128)S(1)} collective-permute-done((f32[200,128]{1,0:T(8,128)S(1)}, f32[200,128]{1,0:T(8,128)S(1)}, u32[]{:S(2)}, u32[]{:S(2)}) %collective-permute-start.12) | collective-permute-done | bytes 102432 | tf_op jit(solution)/shard_map/ppermute | solution.py:518
  60.4 8.7 %all_to_all.25.sums_ref = f32[16,1,128]{2,1,0:T(1,128)S(1)} all-to-all(f32[16,1,128]{2,1,0:T(1,128)S(1)} %shard_map.102), channel_id=1, replica_groups={{0,1,2,3,8,9,10,11,16,17,18,19,24,25,26,27},{4,5,6,7,12,13,14,15,20,21,..., dimensions={0} | all-to-all | bytes 16384 | tf_op jit(solution)/shard_map/all_to_all | solution.py:454
  69.0 2.1 shard_map.103
  74.7 3.0 collective-permute-done.13.refs_1_
  78.2 3.2 %collective-permute-start.16 = (f32[192,128]{1,0:T(8,128)S(1)}, f32[192,128]{1,0:T(8,128)S(1)}, u32[]{:S(2)}, u32[]{:S(2)}) collective-permute-start(f32[192,128]{1,0:T(8,128)S(1)} %shard_map.104.refs_0_), channel_id=1, source_target_pairs={{0,4},{1,5},{2,6},{3,7},{4,0},{5,1},{6,2},{7,3},{8,12},{9,13},{10,... | collective-permute-start | bytes 294920 | tf_op jit(solution)/shard_map/ppermute | solution.py:481
  81.4 4.5 %collective-permute-done.16.refs_1_ = f32[192,128]{1,0:T(8,128)S(1)} collective-permute-done((f32[192,128]{1,0:T(8,128)S(1)}, f32[192,128]{1,0:T(8,128)S(1)}, u32[]{:S(2)}, u32[]{:S(2)}) %collective-permute-start.16) | collective-permute-done | bytes 98336 | tf_op jit(solution)/shard_map/ppermute | solution.py:481
  89.5 2.8 collective-permute-done.17.refs_1_
  97.8 5.0 %collective-permute-done.21 = f32[256,128]{1,0:T(8,128)S(1)} collective-permute-done((f32[256,128]{1,0:T(8,128)S(1)}, f32[256,128]{1,0:T(8,128)S(1)}, u32[]{:S(2)}, u32[]{:S(2)}) %collective-permute-start.21) | collective-permute-done | bytes 131104 | tf_op jit(solution)/shard_map/ppermute | solution.py:504
  102.8 2.2 shard_map.107
  108.5 2.9 collective-permute-done.22.refs_1_
  114.0 4.9 %collective-permute-done.25.other_ref = f32[200,128]{1,0:T(8,128)S(1)} collective-permute-done((f32[200,128]{1,0:T(8,128)S(1)}, f32[200,128]{1,0:T(8,128)S(1)}, u32[]{:S(2)}, u32[]{:S(2)}) %collective-permute-start.25) | collective-permute-done | bytes 102432 | tf_op jit(solution)/shard_map/ppermute | solution.py:518
  118.9 8.0 %all_to_all.26.sums_ref = f32[16,1,128]{2,1,0:T(1,128)S(1)} all-to-all(f32[16,1,128]{2,1,0:T(1,128)S(1)} %shard_map.109), channel_id=1, replica_groups={{0,1,2,3,8,9,10,11,16,17,18,19,24,25,26,27},{4,5,6,7,12,13,14,15,20,21,..., dimensions={0} | all-to-all | bytes 16384 | tf_op jit(solution)/shard_map/all_to_all | solution.py:454
  127.0 2.1 shard_map.110
  132.6 3.0 collective-permute-done.26.refs_1_
  136.1 2.2 collective-permute-start.29
  138.3 5.1 %collective-permute-done.29.refs_1_ = f32[192,128]{1,0:T(8,128)S(1)} collective-permute-done((f32[192,128]{1,0:T(8,128)S(1)}, f32[192,128]{1,0:T(8,128)S(1)}, u32[]{:S(2)}, u32[]{:S(2)}) %collective-permute-start.29) | collective-permute-done | bytes 98336 | tf_op jit(solution)/shard_map/ppermute | solution.py:481
  146.9 3.0 collective-permute-done.30.refs_1_
  155.1 4.9 %collective-permute-done.34 = f32[256,128]{1,0:T(8,128)S(1)} collective-permute-done((f32[256,128]{1,0:T(8,128)S(1)}, f32[256,128]{1,0:T(8,128)S(1)}, u32[]{:S(2)}, u32[]{:S(2)}) %collective-permute-start.34) | collective-permute-done | bytes 131104 | tf_op jit(solution)/shard_map/ppermute | solution.py:504
  165.6 3.0 collective-permute-done.35.refs_1_
  170.7 5.2 %collective-permute-done.38.other_ref = f32[200,128]{1,0:T(8,128)S(1)} collective-permute-done((f32[200,128]{1,0:T(8,128)S(1)}, f32[200,128]{1,0:T(8,128)S(1)}, u32[]{:S(2)}, u32[]{:S(2)}) %collective-permute-start.38) | collective-permute-done | bytes 102432 | tf_op jit(solution)/shard_map/ppermute | solution.py:518
  176.0 8.0 %all_to_all.27.sums_ref = f32[16,1,128]{2,1,0:T(1,128)S(1)} all-to-all(f32[16,1,128]{2,1,0:T(1,128)S(1)} %shard_map.116), channel_id=1, replica_groups={{0,1,2,3,8,9,10,11,16,17,18,19,24,25,26,27},{4,5,6,7,12,13,14,15,20,21,..., dimensions={0} | all-to-all | bytes 16384 | tf_op jit(solution)/shard_map/all_to_all | solution.py:454
  189.7 3.0 collective-permute-done.39.refs_1_
  195.0 5.4 %collective-permute-done.42.refs_1_ = f32[192,128]{1,0:T(8,128)S(1)} collective-permute-done((f32[192,128]{1,0:T(8,128)S(1)}, f32[192,128]{1,0:T(8,128)S(1)}, u32[]{:S(2)}, u32[]{:S(2)}) %collective-permute-start.42) | collective-permute-done | bytes 98336 | tf_op jit(solution)/shard_map/ppermute | solution.py:481
  203.9 3.0 collective-permute-done.43.refs_1_
  212.1 5.0 %collective-permute-done.47 = f32[256,128]{1,0:T(8,128)S(1)} collective-permute-done((f32[256,128]{1,0:T(8,128)S(1)}, f32[256,128]{1,0:T(8,128)S(1)}, u32[]{:S(2)}, u32[]{:S(2)}) %collective-permute-start.47) | collective-permute-done | bytes 131104 | tf_op jit(solution)/shard_map/ppermute | solution.py:504
  222.6 3.0 collective-permute-done.48.refs_1_
  227.4 5.6 %collective-permute-done.51.other_ref = f32[200,128]{1,0:T(8,128)S(1)} collective-permute-done((f32[200,128]{1,0:T(8,128)S(1)}, f32[200,128]{1,0:T(8,128)S(1)}, u32[]{:S(2)}, u32[]{:S(2)}) %collective-permute-start.51) | collective-permute-done | bytes 102432 | tf_op jit(solution)/shard_map/ppermute | solution.py:518
  233.0 8.0 %all_to_all.28.sums_ref = f32[16,1,128]{2,1,0:T(1,128)S(1)} all-to-all(f32[16,1,128]{2,1,0:T(1,128)S(1)} %shard_map.123), channel_id=1, replica_groups={{0,1,2,3,8,9,10,11,16,17,18,19,24,25,26,27},{4,5,6,7,12,13,14,15,20,21,..., dimensions={0} | all-to-all | bytes 16384 | tf_op jit(solution)/shard_map/all_to_all | solution.py:454
  241.0 2.3 shard_map.124
  246.9 3.0 collective-permute-done.52.refs_1_
  251.9 5.7 %collective-permute-done.55.refs_1_ = f32[192,128]{1,0:T(8,128)S(1)} collective-permute-done((f32[192,128]{1,0:T(8,128)S(1)}, f32[192,128]{1,0:T(8,128)S(1)}, u32[]{:S(2)}, u32[]{:S(2)}) %collective-permute-start.55) | collective-permute-done | bytes 98336 | tf_op jit(solution)/shard_map/ppermute | solution.py:481
  261.2 2.9 collective-permute-done.56.refs_1_
  269.4 5.0 %collective-permute-done.60 = f32[256,128]{1,0:T(8,128)S(1)} collective-permute-done((f32[256,128]{1,0:T(8,128)S(1)}, f32[256,128]{1,0:T(8,128)S(1)}, u32[]{:S(2)}, u32[]{:S(2)}) %collective-permute-start.60) | collective-permute-done | bytes 131104 | tf_op jit(solution)/shard_map/ppermute | solution.py:504
  279.9 3.0 collective-permute-done.61.refs_1_
  284.3 5.9 %collective-permute-done.64.other_ref = f32[200,128]{1,0:T(8,128)S(1)} collective-permute-done((f32[200,128]{1,0:T(8,128)S(1)}, f32[200,128]{1,0:T(8,128)S(1)}, u32[]{:S(2)}, u32[]{:S(2)}) %collective-permute-start.64) | collective-permute-done | bytes 102432 | tf_op jit(solution)/shard_map/ppermute | solution.py:518
  290.3 8.0 %all_to_all.29.sums_ref = f32[16,1,128]{2,1,0:T(1,128)S(1)} all-to-all(f32[16,1,128]{2,1,0:T(1,128)S(1)} %shard_map.130), channel_id=1, replica_groups={{0,1,2,3,8,9,10,11,16,17,18,19,24,25,26,27},{4,5,6,7,12,13,14,15,20,21,..., dimensions={0} | all-to-all | bytes 16384 | tf_op jit(solution)/shard_map/all_to_all | solution.py:454
  298.3 2.9 shard_map.131
  304.7 3.0 collective-permute-done.65.refs_1_
  309.3 4.0 %collective-permute-done.68.refs_1_ = f32[16,768]{1,0:T(8,128)S(1)} collective-permute-done((f32[16,768]{1,0:T(8,128)S(1)}, f32[16,768]{1,0:T(8,128)S(1)}, u32[]{:S(2)}, u32[]{:S(2)}) %collective-permute-start.68) | collective-permute-done | bytes 49184 | tf_op jit(solution)/shard_map/ppermute | solution.py:532
  (168 shorter events, 115.5 us)
Async XLA Ops:
  11.1 7.2 %collective-permute-start = (f32[192,128]{1,0:T(8,128)S(1)}, f32[192,128]{1,0:T(8,128)S(1)}, u32[]{:S(2)}, u32[]{:S(2)}) collective-permute-start(f32[192,128]{1,0:T(8,128)S(1)} %get-tuple-element.72), channel_id=1, source_target_pairs={{0,3},{1,2},{2,1},{3,0},{4,7},{5,6},{6,5},{7,4},{8,11},{9,10},{10,... | collective-permute-start | bytes 294920 | tf_op jit(solution)/shard_map/ppermute | solution.py:470
  20.2 7.6 %collective-permute-start.3 = (f32[192,128]{1,0:T(8,128)S(1)}, f32[192,128]{1,0:T(8,128)S(1)}, u32[]{:S(2)}, u32[]{:S(2)}) collective-permute-start(f32[192,128]{1,0:T(8,128)S(1)} %shard_map.97.refs_0_), channel_id=1, source_target_pairs={{0,4},{1,5},{2,6},{3,7},{4,0},{5,1},{6,2},{7,3},{8,12},{9,13},{10,... | collective-permute-start | bytes 294920 | tf_op jit(solution)/shard_map/ppermute | solution.py:481
  27.8 5.7 %collective-permute-start.4 = (f32[192,128]{1,0:T(8,128)S(1)}, f32[192,128]{1,0:T(8,128)S(1)}, u32[]{:S(2)}, u32[]{:S(2)}) collective-permute-start(f32[192,128]{1,0:T(8,128)S(1)} %shard_map.98.refs_0_), channel_id=1, source_target_pairs={{0,3},{1,2},{2,1},{3,0},{4,7},{5,6},{6,5},{7,4},{8,11},{9,10},{10,... | collective-permute-start | bytes 294920 | tf_op jit(solution)/shard_map/ppermute | solution.py:470
  28.5 5.7 %collective-permute-start.5 = (f32[192,128]{1,0:T(8,128)S(1)}, f32[192,128]{1,0:T(8,128)S(1)}, u32[]{:S(2)}, u32[]{:S(2)}) collective-permute-start(f32[192,128]{1,0:T(8,128)S(1)} %shard_map.98.refs_0_), channel_id=1, source_target_pairs={{0,1},{1,0},{2,3},{3,2},{4,5},{5,4},{6,7},{7,6},{8,9},{9,8},{10,11... | collective-permute-start | bytes 294920 | tf_op jit(solution)/shard_map/ppermute | solution.py:470
  38.0 5.6 %collective-permute-start.8 = (f32[256,128]{1,0:T(8,128)S(1)}, f32[256,128]{1,0:T(8,128)S(1)}, u32[]{:S(2)}, u32[]{:S(2)}) collective-permute-start(f32[256,128]{1,0:T(8,128)S(1)} %add.40), channel_id=1, source_target_pairs={{0,16},{8,24},{16,0},{24,8},{1,17},{9,25},{17,1},{25,9},{2,18},{10... | collective-permute-start | bytes 393224 | tf_op jit(solution)/shard_map/ppermute | solution.py:504
  53.6 6.7 %collective-permute-start.12 = (f32[200,128]{1,0:T(8,128)S(1)}, f32[200,128]{1,0:T(8,128)S(1)}, u32[]{:S(2)}, u32[]{:S(2)}) collective-permute-start(f32[200,128]{1,0:T(8,128)S(1)} %shard_map.101.mine_ref), channel_id=1, source_target_pairs={{0,4},{1,5},{2,6},{3,7},{4,0},{5,1},{6,2},{7,3},{8,12},{9,13},{10,... | collective-permute-start | bytes 307208 | tf_op jit(solution)/shard_map/ppermute | solution.py:518
  71.2 6.6 %collective-permute-start.13 = (f32[192,128]{1,0:T(8,128)S(1)}, f32[192,128]{1,0:T(8,128)S(1)}, u32[]{:S(2)}, u32[]{:S(2)}) collective-permute-start(f32[192,128]{1,0:T(8,128)S(1)} %get-tuple-element.82), channel_id=1, source_target_pairs={{0,3},{1,2},{2,1},{3,0},{4,7},{5,6},{6,5},{7,4},{8,11},{9,10},{10,... | collective-permute-start | bytes 294920 | tf_op jit(solution)/shard_map/ppermute | solution.py:470
  71.8 6.4 %collective-permute-start.14 = (f32[192,128]{1,0:T(8,128)S(1)}, f32[192,128]{1,0:T(8,128)S(1)}, u32[]{:S(2)}, u32[]{:S(2)}) collective-permute-start(f32[192,128]{1,0:T(8,128)S(1)} %get-tuple-element.83), channel_id=1, source_target_pairs={{0,1},{1,0},{2,3},{3,2},{4,5},{5,4},{6,7},{7,6},{8,9},{9,8},{10,11... | collective-permute-start | bytes 294920 | tf_op jit(solution)/shard_map/ppermute | solution.py:470
  78.2 7.7 %collective-permute-start.16 = (f32[192,128]{1,0:T(8,128)S(1)}, f32[192,128]{1,0:T(8,128)S(1)}, u32[]{:S(2)}, u32[]{:S(2)}) collective-permute-start(f32[192,128]{1,0:T(8,128)S(1)} %shard_map.104.refs_0_), channel_id=1, source_target_pairs={{0,4},{1,5},{2,6},{3,7},{4,0},{5,1},{6,2},{7,3},{8,12},{9,13},{10,... | collective-permute-start | bytes 294920 | tf_op jit(solution)/shard_map/ppermute | solution.py:481
  85.9 6.4 %collective-permute-start.17 = (f32[192,128]{1,0:T(8,128)S(1)}, f32[192,128]{1,0:T(8,128)S(1)}, u32[]{:S(2)}, u32[]{:S(2)}) collective-permute-start(f32[192,128]{1,0:T(8,128)S(1)} %shard_map.105.refs_0_), channel_id=1, source_target_pairs={{0,3},{1,2},{2,1},{3,0},{4,7},{5,6},{6,5},{7,4},{8,11},{9,10},{10,... | collective-permute-start | bytes 294920 | tf_op jit(solution)/shard_map/ppermute | solution.py:470
  86.7 5.7 %collective-permute-start.18 = (f32[192,128]{1,0:T(8,128)S(1)}, f32[192,128]{1,0:T(8,128)S(1)}, u32[]{:S(2)}, u32[]{:S(2)}) collective-permute-start(f32[192,128]{1,0:T(8,128)S(1)} %shard_map.105.refs_0_), channel_id=1, source_target_pairs={{0,1},{1,0},{2,3},{3,2},{4,5},{5,4},{6,7},{7,6},{8,9},{9,8},{10,11... | collective-permute-start | bytes 294920 | tf_op jit(solution)/shard_map/ppermute | solution.py:470
  87.7 6.1 %collective-permute-start.19 = (f32[192,128]{1,0:T(8,128)S(1)}, f32[192,128]{1,0:T(8,128)S(1)}, u32[]{:S(2)}, u32[]{:S(2)}) collective-permute-start(f32[192,128]{1,0:T(8,128)S(1)} %shard_map.105.refs_0_), channel_id=1, source_target_pairs={{0,2},{1,3},{2,0},{3,1},{4,6},{5,7},{6,4},{7,5},{8,10},{9,11},{10,... | collective-permute-start | bytes 294920 | tf_op jit(solution)/shard_map/ppermute | solution.py:470
  97.2 5.6 %collective-permute-start.21 = (f32[256,128]{1,0:T(8,128)S(1)}, f32[256,128]{1,0:T(8,128)S(1)}, u32[]{:S(2)}, u32[]{:S(2)}) collective-permute-start(f32[256,128]{1,0:T(8,128)S(1)} %add.42), channel_id=1, source_target_pairs={{0,16},{8,24},{16,0},{24,8},{1,17},{9,25},{17,1},{25,9},{2,18},{10... | collective-permute-start | bytes 393224 | tf_op jit(solution)/shard_map/ppermute | solution.py:504
  105.0 6.4 %collective-permute-start.22 = (f32[192,128]{1,0:T(8,128)S(1)}, f32[192,128]{1,0:T(8,128)S(1)}, u32[]{:S(2)}, u32[]{:S(2)}) collective-permute-start(f32[192,128]{1,0:T(8,128)S(1)} %get-tuple-element.88), channel_id=1, source_target_pairs={{0,3},{1,2},{2,1},{3,0},{4,7},{5,6},{6,5},{7,4},{8,11},{9,10},{10,... | collective-permute-start | bytes 294920 | tf_op jit(solution)/shard_map/ppermute | solution.py:470
  106.3 5.7 %collective-permute-start.23 = (f32[192,128]{1,0:T(8,128)S(1)}, f32[192,128]{1,0:T(8,128)S(1)}, u32[]{:S(2)}, u32[]{:S(2)}) collective-permute-start(f32[192,128]{1,0:T(8,128)S(1)} %get-tuple-element.89), channel_id=1, source_target_pairs={{0,1},{1,0},{2,3},{3,2},{4,5},{5,4},{6,7},{7,6},{8,9},{9,8},{10,11... | collective-permute-start | bytes 294920 | tf_op jit(solution)/shard_map/ppermute | solution.py:470
  112.1 6.8 %collective-permute-start.25 = (f32[200,128]{1,0:T(8,128)S(1)}, f32[200,128]{1,0:T(8,128)S(1)}, u32[]{:S(2)}, u32[]{:S(2)}) collective-permute-start(f32[200,128]{1,0:T(8,128)S(1)} %shard_map.108.mine_ref), channel_id=1, source_target_pairs={{0,4},{1,5},{2,6},{3,7},{4,0},{5,1},{6,2},{7,3},{8,12},{9,13},{10,... | collective-permute-start | bytes 307208 | tf_op jit(solution)/shard_map/ppermute | solution.py:518
  129.1 6.6 %collective-permute-start.26 = (f32[192,128]{1,0:T(8,128)S(1)}, f32[192,128]{1,0:T(8,128)S(1)}, u32[]{:S(2)}, u32[]{:S(2)}) collective-permute-start(f32[192,128]{1,0:T(8,128)S(1)} %get-tuple-element.93), channel_id=1, source_target_pairs={{0,3},{1,2},{2,1},{3,0},{4,7},{5,6},{6,5},{7,4},{8,11},{9,10},{10,... | collective-permute-start | bytes 294920 | tf_op jit(solution)/shard_map/ppermute | solution.py:470
  129.7 6.4 %collective-permute-start.27 = (f32[192,128]{1,0:T(8,128)S(1)}, f32[192,128]{1,0:T(8,128)S(1)}, u32[]{:S(2)}, u32[]{:S(2)}) collective-permute-start(f32[192,128]{1,0:T(8,128)S(1)} %get-tuple-element.94), channel_id=1, source_target_pairs={{0,1},{1,0},{2,3},{3,2},{4,5},{5,4},{6,7},{7,6},{8,9},{9,8},{10,11... | collective-permute-start | bytes 294920 | tf_op jit(solution)/shard_map/ppermute | solution.py:470
  136.1 7.2 %collective-permute-start.29 = (f32[192,128]{1,0:T(8,128)S(1)}, f32[192,128]{1,0:T(8,128)S(1)}, u32[]{:S(2)}, u32[]{:S(2)}) collective-permute-start(f32[192,128]{1,0:T(8,128)S(1)} %shard_map.111.refs_0_), channel_id=1, source_target_pairs={{0,4},{1,5},{2,6},{3,7},{4,0},{5,1},{6,2},{7,3},{8,12},{9,13},{10,... | collective-permute-start | bytes 294920 | tf_op jit(solution)/shard_map/ppermute | solution.py:481
  143.3 6.5 %collective-permute-start.30 = (f32[192,128]{1,0:T(8,128)S(1)}, f32[192,128]{1,0:T(8,128)S(1)}, u32[]{:S(2)}, u32[]{:S(2)}) collective-permute-start(f32[192,128]{1,0:T(8,128)S(1)} %shard_map.112.refs_0_), channel_id=1, source_target_pairs={{0,3},{1,2},{2,1},{3,0},{4,7},{5,6},{6,5},{7,4},{8,11},{9,10},{10,... | collective-permute-start | bytes 294920 | tf_op jit(solution)/shard_map/ppermute | solution.py:470
  143.6 6.3 %collective-permute-start.31 = (f32[192,128]{1,0:T(8,128)S(1)}, f32[192,128]{1,0:T(8,128)S(1)}, u32[]{:S(2)}, u32[]{:S(2)}) collective-permute-start(f32[192,128]{1,0:T(8,128)S(1)} %shard_map.112.refs_0_), channel_id=1, source_target_pairs={{0,1},{1,0},{2,3},{3,2},{4,5},{5,4},{6,7},{7,6},{8,9},{9,8},{10,11... | collective-permute-start | bytes 294920 | tf_op jit(solution)/shard_map/ppermute | solution.py:470
  145.0 6.0 %collective-permute-start.32 = (f32[192,128]{1,0:T(8,128)S(1)}, f32[192,128]{1,0:T(8,128)S(1)}, u32[]{:S(2)}, u32[]{:S(2)}) collective-permute-start(f32[192,128]{1,0:T(8,128)S(1)} %shard_map.112.refs_0_), channel_id=1, source_target_pairs={{0,2},{1,3},{2,0},{3,1},{4,6},{5,7},{6,4},{7,5},{8,10},{9,11},{10,... | collective-permute-start | bytes 294920 | tf_op jit(solution)/shard_map/ppermute | solution.py:470
  154.4 5.6 %collective-permute-start.34 = (f32[256,128]{1,0:T(8,128)S(1)}, f32[256,128]{1,0:T(8,128)S(1)}, u32[]{:S(2)}, u32[]{:S(2)}) collective-permute-start(f32[256,128]{1,0:T(8,128)S(1)} %add.44), channel_id=1, source_target_pairs={{0,16},{8,24},{16,0},{24,8},{1,17},{9,25},{17,1},{25,9},{2,18},{10... | collective-permute-start | bytes 393224 | tf_op jit(solution)/shard_map/ppermute | solution.py:504
  162.0 6.6 %collective-permute-start.35 = (f32[192,128]{1,0:T(8,128)S(1)}, f32[192,128]{1,0:T(8,128)S(1)}, u32[]{:S(2)}, u32[]{:S(2)}) collective-permute-start(f32[192,128]{1,0:T(8,128)S(1)} %get-tuple-element.99), channel_id=1, source_target_pairs={{0,3},{1,2},{2,1},{3,0},{4,7},{5,6},{6,5},{7,4},{8,11},{9,10},{10,... | collective-permute-start | bytes 294920 | tf_op jit(solution)/shard_map/ppermute | solution.py:470
  163.6 5.5 %collective-permute-start.36 = (f32[192,128]{1,0:T(8,128)S(1)}, f32[192,128]{1,0:T(8,128)S(1)}, u32[]{:S(2)}, u32[]{:S(2)}) collective-permute-start(f32[192,128]{1,0:T(8,128)S(1)} %get-tuple-element.100), channel_id=1, source_target_pairs={{0,1},{1,0},{2,3},{3,2},{4,5},{5,4},{6,7},{7,6},{8,9},{9,8},{10,11... | collective-permute-start | bytes 294920 | tf_op jit(solution)/shard_map/ppermute | solution.py:470
  169.2 6.7 %collective-permute-start.38 = (f32[200,128]{1,0:T(8,128)S(1)}, f32[200,128]{1,0:T(8,128)S(1)}, u32[]{:S(2)}, u32[]{:S(2)}) collective-permute-start(f32[200,128]{1,0:T(8,128)S(1)} %shard_map.115.mine_ref), channel_id=1, source_target_pairs={{0,4},{1,5},{2,6},{3,7},{4,0},{5,1},{6,2},{7,3},{8,12},{9,13},{10,... | collective-permute-start | bytes 307208 | tf_op jit(solution)/shard_map/ppermute | solution.py:518
  186.1 6.6 %collective-permute-start.39 = (f32[192,128]{1,0:T(8,128)S(1)}, f32[192,128]{1,0:T(8,128)S(1)}, u32[]{:S(2)}, u32[]{:S(2)}) collective-permute-start(f32[192,128]{1,0:T(8,128)S(1)} %get-tuple-element.104), channel_id=1, source_target_pairs={{0,3},{1,2},{2,1},{3,0},{4,7},{5,6},{6,5},{7,4},{8,11},{9,10},{10,... | collective-permute-start | bytes 294920 | tf_op jit(solution)/shard_map/ppermute | solution.py:470
  186.7 6.4 %collective-permute-start.40 = (f32[192,128]{1,0:T(8,128)S(1)}, f32[192,128]{1,0:T(8,128)S(1)}, u32[]{:S(2)}, u32[]{:S(2)}) collective-permute-start(f32[192,128]{1,0:T(8,128)S(1)} %get-tuple-element.105), channel_id=1, source_target_pairs={{0,1},{1,0},{2,3},{3,2},{4,5},{5,4},{6,7},{7,6},{8,9},{9,8},{10,11... | collective-permute-start | bytes 294920 | tf_op jit(solution)/shard_map/ppermute | solution.py:470
  193.1 7.2 %collective-permute-start.42 = (f32[192,128]{1,0:T(8,128)S(1)}, f32[192,128]{1,0:T(8,128)S(1)}, u32[]{:S(2)}, u32[]{:S(2)}) collective-permute-start(f32[192,128]{1,0:T(8,128)S(1)} %shard_map.118.refs_0_), channel_id=1, source_target_pairs={{0,4},{1,5},{2,6},{3,7},{4,0},{5,1},{6,2},{7,3},{8,12},{9,13},{10,... | collective-permute-start | bytes 294920 | tf_op jit(solution)/shard_map/ppermute | solution.py:481
  200.4 6.5 %collective-permute-start.43 = (f32[192,128]{1,0:T(8,128)S(1)}, f32[192,128]{1,0:T(8,128)S(1)}, u32[]{:S(2)}, u32[]{:S(2)}) collective-permute-start(f32[192,128]{1,0:T(8,128)S(1)} %shard_map.119.refs_0_), channel_id=1, source_target_pairs={{0,3},{1,2},{2,1},{3,0},{4,7},{5,6},{6,5},{7,4},{8,11},{9,10},{10,... | collective-permute-start | bytes 294920 | tf_op jit(solution)/shard_map/ppermute | solution.py:470
  200.5 6.5 %collective-permute-start.44 = (f32[192,128]{1,0:T(8,128)S(1)}, f32[192,128]{1,0:T(8,128)S(1)}, u32[]{:S(2)}, u32[]{:S(2)}) collective-permute-start(f32[192,128]{1,0:T(8,128)S(1)} %shard_map.119.refs_0_), channel_id=1, source_target_pairs={{0,1},{1,0},{2,3},{3,2},{4,5},{5,4},{6,7},{7,6},{8,9},{9,8},{10,11... | collective-permute-start | bytes 294920 | tf_op jit(solution)/shard_map/ppermute | solution.py:470
  202.1 6.0 %collective-permute-start.45 = (f32[192,128]{1,0:T(8,128)S(1)}, f32[192,128]{1,0:T(8,128)S(1)}, u32[]{:S(2)}, u32[]{:S(2)}) collective-permute-start(f32[192,128]{1,0:T(8,128)S(1)} %shard_map.119.refs_0_), channel_id=1, source_target_pairs={{0,2},{1,3},{2,0},{3,1},{4,6},{5,7},{6,4},{7,5},{8,10},{9,11},{10,... | collective-permute-start | bytes 294920 | tf_op jit(solution)/shard_map/ppermute | solution.py:470
  211.5 5.6 %collective-permute-start.47 = (f32[256,128]{1,0:T(8,128)S(1)}, f32[256,128]{1,0:T(8,128)S(1)}, u32[]{:S(2)}, u32[]{:S(2)}) collective-permute-start(f32[256,128]{1,0:T(8,128)S(1)} %add.46), channel_id=1, source_target_pairs={{0,16},{8,24},{16,0},{24,8},{1,17},{9,25},{17,1},{25,9},{2,18},{10... | collective-permute-start | bytes 393224 | tf_op jit(solution)/shard_map/ppermute | solution.py:504
  219.1 6.6 %collective-permute-start.48 = (f32[192,128]{1,0:T(8,128)S(1)}, f32[192,128]{1,0:T(8,128)S(1)}, u32[]{:S(2)}, u32[]{:S(2)}) collective-permute-start(f32[192,128]{1,0:T(8,128)S(1)} %get-tuple-element.110), channel_id=1, source_target_pairs={{0,3},{1,2},{2,1},{3,0},{4,7},{5,6},{6,5},{7,4},{8,11},{9,10},{10,... | collective-permute-start | bytes 294920 | tf_op jit(solution)/shard_map/ppermute | solution.py:470
  220.6 5.5 %collective-permute-start.49 = (f32[192,128]{1,0:T(8,128)S(1)}, f32[192,128]{1,0:T(8,128)S(1)}, u32[]{:S(2)}, u32[]{:S(2)}) collective-permute-start(f32[192,128]{1,0:T(8,128)S(1)} %get-tuple-element.111), channel_id=1, source_target_pairs={{0,1},{1,0},{2,3},{3,2},{4,5},{5,4},{6,7},{7,6},{8,9},{9,8},{10,11... | collective-permute-start | bytes 294920 | tf_op jit(solution)/shard_map/ppermute | solution.py:470
  226.2 6.7 %collective-permute-start.51 = (f32[200,128]{1,0:T(8,128)S(1)}, f32[200,128]{1,0:T(8,128)S(1)}, u32[]{:S(2)}, u32[]{:S(2)}) collective-permute-start(f32[200,128]{1,0:T(8,128)S(1)} %shard_map.122.mine_ref), channel_id=1, source_target_pairs={{0,4},{1,5},{2,6},{3,7},{4,0},{5,1},{6,2},{7,3},{8,12},{9,13},{10,... | collective-permute-start | bytes 307208 | tf_op jit(solution)/shard_map/ppermute | solution.py:518
  243.4 6.6 %collective-permute-start.52 = (f32[192,128]{1,0:T(8,128)S(1)}, f32[192,128]{1,0:T(8,128)S(1)}, u32[]{:S(2)}, u32[]{:S(2)}) collective-permute-start(f32[192,128]{1,0:T(8,128)S(1)} %get-tuple-element.115), channel_id=1, source_target_pairs={{0,3},{1,2},{2,1},{3,0},{4,7},{5,6},{6,5},{7,4},{8,11},{9,10},{10,... | collective-permute-start | bytes 294920 | tf_op jit(solution)/shard_map/ppermute | solution.py:470
  244.0 6.4 %collective-permute-start.53 = (f32[192,128]{1,0:T(8,128)S(1)}, f32[192,128]{1,0:T(8,128)S(1)}, u32[]{:S(2)}, u32[]{:S(2)}) collective-permute-start(f32[192,128]{1,0:T(8,128)S(1)} %get-tuple-element.116), channel_id=1, source_target_pairs={{0,1},{1,0},{2,3},{3,2},{4,5},{5,4},{6,7},{7,6},{8,9},{9,8},{10,11... | collective-permute-start | bytes 294920 | tf_op jit(solution)/shard_map/ppermute | solution.py:470
  250.4 7.2 %collective-permute-start.55 = (f32[192,128]{1,0:T(8,128)S(1)}, f32[192,128]{1,0:T(8,128)S(1)}, u32[]{:S(2)}, u32[]{:S(2)}) collective-permute-start(f32[192,128]{1,0:T(8,128)S(1)} %shard_map.125.refs_0_), channel_id=1, source_target_pairs={{0,4},{1,5},{2,6},{3,7},{4,0},{5,1},{6,2},{7,3},{8,12},{9,13},{10,... | collective-permute-start | bytes 294920 | tf_op jit(solution)/shard_map/ppermute | solution.py:481
  257.6 6.5 %collective-permute-start.56 = (f32[192,128]{1,0:T(8,128)S(1)}, f32[192,128]{1,0:T(8,128)S(1)}, u32[]{:S(2)}, u32[]{:S(2)}) collective-permute-start(f32[192,128]{1,0:T(8,128)S(1)} %shard_map.126.refs_0_), channel_id=1, source_target_pairs={{0,3},{1,2},{2,1},{3,0},{4,7},{5,6},{6,5},{7,4},{8,11},{9,10},{10,... | collective-permute-start | bytes 294920 | tf_op jit(solution)/shard_map/ppermute | solution.py:470
  257.7 6.4 %collective-permute-start.57 = (f32[192,128]{1,0:T(8,128)S(1)}, f32[192,128]{1,0:T(8,128)S(1)}, u32[]{:S(2)}, u32[]{:S(2)}) collective-permute-start(f32[192,128]{1,0:T(8,128)S(1)} %shard_map.126.refs_0_), channel_id=1, source_target_pairs={{0,1},{1,0},{2,3},{3,2},{4,5},{5,4},{6,7},{7,6},{8,9},{9,8},{10,11... | collective-permute-start | bytes 294920 | tf_op jit(solution)/shard_map/ppermute | solution.py:470
  259.4 6.0 %collective-permute-start.58 = (f32[192,128]{1,0:T(8,128)S(1)}, f32[192,128]{1,0:T(8,128)S(1)}, u32[]{:S(2)}, u32[]{:S(2)}) collective-permute-start(f32[192,128]{1,0:T(8,128)S(1)} %shard_map.126.refs_0_), channel_id=1, source_target_pairs={{0,2},{1,3},{2,0},{3,1},{4,6},{5,7},{6,4},{7,5},{8,10},{9,11},{10,... | collective-permute-start | bytes 294920 | tf_op jit(solution)/shard_map/ppermute | solution.py:470
  268.8 5.6 %collective-permute-start.60 = (f32[256,128]{1,0:T(8,128)S(1)}, f32[256,128]{1,0:T(8,128)S(1)}, u32[]{:S(2)}, u32[]{:S(2)}) collective-permute-start(f32[256,128]{1,0:T(8,128)S(1)} %add.48), channel_id=1, source_target_pairs={{0,16},{8,24},{16,0},{24,8},{1,17},{9,25},{17,1},{25,9},{2,18},{10... | collective-permute-start | bytes 393224 | tf_op jit(solution)/shard_map/ppermute | solution.py:504
  276.4 6.6 %collective-permute-start.61 = (f32[192,128]{1,0:T(8,128)S(1)}, f32[192,128]{1,0:T(8,128)S(1)}, u32[]{:S(2)}, u32[]{:S(2)}) collective-permute-start(f32[192,128]{1,0:T(8,128)S(1)} %get-tuple-element.121), channel_id=1, source_target_pairs={{0,3},{1,2},{2,1},{3,0},{4,7},{5,6},{6,5},{7,4},{8,11},{9,10},{10,... | collective-permute-start | bytes 294920 | tf_op jit(solution)/shard_map/ppermute | solution.py:470
  277.9 5.6 %collective-permute-start.62 = (f32[192,128]{1,0:T(8,128)S(1)}, f32[192,128]{1,0:T(8,128)S(1)}, u32[]{:S(2)}, u32[]{:S(2)}) collective-permute-start(f32[192,128]{1,0:T(8,128)S(1)} %get-tuple-element.122), channel_id=1, source_target_pairs={{0,1},{1,0},{2,3},{3,2},{4,5},{5,4},{6,7},{7,6},{8,9},{9,8},{10,11... | collective-permute-start | bytes 294920 | tf_op jit(solution)/shard_map/ppermute | solution.py:470
  283.5 6.7 %collective-permute-start.64 = (f32[200,128]{1,0:T(8,128)S(1)}, f32[200,128]{1,0:T(8,128)S(1)}, u32[]{:S(2)}, u32[]{:S(2)}) collective-permute-start(f32[200,128]{1,0:T(8,128)S(1)} %shard_map.129.mine_ref), channel_id=1, source_target_pairs={{0,4},{1,5},{2,6},{3,7},{4,0},{5,1},{6,2},{7,3},{8,12},{9,13},{10,... | collective-permute-start | bytes 307208 | tf_op jit(solution)/shard_map/ppermute | solution.py:518
  301.2 6.5 %collective-permute-start.65 = (f32[2,16,768]{2,1,0:T(8,128)S(1)}, f32[2,16,768]{2,1,0:T(8,128)S(1)}, u32[]{:S(2)}, u32[]{:S(2)}) collective-permute-start(f32[2,16,768]{2,1,0:T(8,128)S(1)} %get-tuple-element.127), channel_id=1, source_target_pairs={{0,3},{1,2},{2,1},{3,0},{4,7},{5,6},{6,5},{7,4},{8,11},{9,10},{10,... | collective-permute-start | bytes 294920 | tf_op jit(solution)/shard_map/ppermute | solution.py:470
  301.8 6.4 %collective-permute-start.66 = (f32[2,16,768]{2,1,0:T(8,128)S(1)}, f32[2,16,768]{2,1,0:T(8,128)S(1)}, u32[]{:S(2)}, u32[]{:S(2)}) collective-permute-start(f32[2,16,768]{2,1,0:T(8,128)S(1)} %get-tuple-element.128), channel_id=1, source_target_pairs={{0,1},{1,0},{2,3},{3,2},{4,5},{5,4},{6,7},{7,6},{8,9},{9,8},{10,11... | collective-permute-start | bytes 294920 | tf_op jit(solution)/shard_map/ppermute | solution.py:470
  (27 other events, 106.2 us)
